TPU v7x, 512 devices: a whole 4x4x16 slice. The times are simulated.
512 devices in a mesh: seq: 64 (over z, y), mp: 8 (over x, core).
Axes of the slice: x: 4, y: 4, z: 16, core: 2. Of those that a mesh axis runs over, the one named last changes fastest.
Arguments:
- tokens: bfloat16 [4, 4096, 1280], P(None, 'seq', 'mp')
- visible_lists: int32 [64, 64, 1], P('seq'), may hold values from 0 to 255, as said below
- visible_counts: int32 [64, 64], P('seq'), may hold values from 0 to 1, as said below
- w_in: bfloat16 [1280, 5120], P(None, 'mp'), may hold values from -0.15625 to 0.15625
- w_out: bfloat16 [5120, 1280], P('mp'), may hold values from -0.078125 to 0.078125
- w_embed: bfloat16 [1280, 512], P('mp'), may hold values from -0.15625 to 0.15625
- mask_token: bfloat16 [512], replicated, may hold values from -5 to 5
- positions: bfloat16 [4096, 512], P('seq'), may hold values from -5 to 5
- w_qkv: bfloat16 [512, 3, 512], P(None, None, 'mp')
- w_attn_out: bfloat16 [512, 512], P('mp'), may hold values from -0.25 to 0.25
Outputs:
- decoded: bfloat16 [4, 4096, 512], P(None, 'seq', 'mp')
Inputs may be any that keep to these rules, and one draw needn't show every extreme that they name: `visible_lists`: every entry is a row of the sending block, 0 to 255; the 64 entries of one block are all different. `visible_counts`: one block fills every slot to every peer; the live slots of a block toward the peers differ by at most one in number.
All inputs are finite; a program needn't handle non-finite values.
Results may differ from a plain program's by a relative error of at most 0.024.
The roundings to bfloat16 on the way count: a program that leaves them out, or rounds other values in their place, can miss the bound.
Values may be sent and summed in bfloat16 or wider, within the bound.
No kernel may reach another device: no remote copies, remote signals or barrier semaphores. Data moves between devices by JAX's collectives and lax.ppermute only.
A program may use at most 64 MiB of HBM per device.

v0:
```python
import math

import jax
import jax.numpy as jnp
from jax import lax
from jax.sharding import PartitionSpec as P

HDIM = 32


def layer_norm(values):
    mean_row = jnp.mean(values, axis=-1, keepdims=True)
    spread = jnp.mean((values - mean_row) * (values - mean_row), axis=-1, keepdims=True)
    return (values - mean_row) * lax.rsqrt(spread + 1e-05)


def local(
    tokens,
    visible_lists,
    visible_counts,
    w_in,
    w_out,
    w_embed,
    mask_token,
    positions,
    w_qkv,
    w_attn_out,
):
    seq_count = lax.axis_size("seq")
    mp_count = lax.axis_size("mp")
    mp_index = lax.axis_index("mp")
    volumes, tubelets, model_part = tokens.shape
    rows_dev = volumes * tubelets
    capacity = visible_lists.shape[2]
    dec_width = w_embed.shape[1]
    dec_part = dec_width // mp_count
    flat_rows = tokens.reshape(rows_dev, model_part)
    slot_rows = visible_lists.reshape(seq_count * capacity)
    slot_ids = jnp.arange(capacity, dtype=jnp.int32)
    live_slots = (slot_ids[None, :] < visible_counts.reshape(seq_count)[:, None]).reshape(
        seq_count * capacity
    )
    own_part = jnp.take(flat_rows, slot_rows, axis=0)
    full_rows = lax.all_gather(own_part, "mp", axis=1, tiled=True)
    normed = layer_norm(full_rows.astype(jnp.float32)).astype(jnp.bfloat16)
    hidden_act = jax.nn.gelu(
        jnp.dot(normed, w_in, preferred_element_type=jnp.float32), approximate=False
    ).astype(jnp.bfloat16)
    mlp_sum = lax.psum_scatter(
        jnp.dot(hidden_act, w_out, preferred_element_type=jnp.float32),
        "mp",
        scatter_dimension=1,
        tiled=True,
    )
    encoded = (own_part.astype(jnp.float32) + mlp_sum).astype(jnp.bfloat16)
    partial_value = jnp.dot(encoded, w_embed, preferred_element_type=jnp.float32)
    embedded = lax.psum_scatter(partial_value, "mp", scatter_dimension=1, tiled=True)
    returned = embedded.astype(jnp.bfloat16)
    picked = (
        (slot_rows[None, :] == jnp.arange(rows_dev, dtype=jnp.int32)[:, None]) & live_slots[None, :]
    ).astype(jnp.bfloat16)
    placed = jnp.dot(picked, returned, preferred_element_type=jnp.float32)
    seen_rows = jnp.sum(picked.astype(jnp.float32), axis=1, keepdims=True)
    pos_rows = jnp.broadcast_to(positions[None], (volumes, tubelets, dec_width)).reshape(
        rows_dev, dec_width
    )
    token_own = lax.dynamic_slice_in_dim(mask_token, mp_index * dec_part, dec_part, 0)
    pos_own = lax.dynamic_slice_in_dim(pos_rows, mp_index * dec_part, dec_part, 1)
    chosen = jnp.where(seen_rows > 0, placed, token_own.astype(jnp.float32)[None, :])
    dec_own = (chosen + pos_own.astype(jnp.float32)).astype(jnp.bfloat16)
    dec_full = lax.all_gather(dec_own, "mp", axis=1, tiled=True)
    dec_normed = layer_norm(dec_full.astype(jnp.float32)).astype(jnp.bfloat16)
    head_width = w_qkv.shape[2]
    head_count = head_width // HDIM
    projected = jnp.dot(
        dec_normed, w_qkv.reshape(dec_width, 3 * head_width), preferred_element_type=jnp.float32
    ).astype(jnp.bfloat16)
    queries = projected[:, :head_width].reshape(volumes, tubelets, head_count, HDIM)
    keys = projected[:, head_width : 2 * head_width].reshape(volumes, tubelets, head_width)
    vals = projected[:, 2 * head_width :].reshape(volumes, tubelets, head_width)
    score_scale = 1.0 / math.sqrt(HDIM)

    def per_volume(inputs):
        query_block, key_block, val_block, running, totals, weighted = inputs
        key_rows = key_block.shape[0]
        key_heads = key_block.reshape(key_rows, head_count, HDIM)
        val_heads = val_block.reshape(key_rows, head_count, HDIM)
        scores = (
            jnp.einsum("qhd,khd->hqk", query_block, key_heads, preferred_element_type=jnp.float32)
            * score_scale
        )
        top_score = jnp.maximum(running, jnp.max(scores, axis=-1))
        fade_out = jnp.exp(running - top_score)
        expo = jnp.exp(scores - top_score[:, :, None])
        new_totals = totals * fade_out + jnp.sum(expo, axis=-1)
        added = jnp.einsum(
            "hqk,khd->hqd", expo.astype(jnp.bfloat16), val_heads, preferred_element_type=jnp.float32
        )
        return (top_score, new_totals, weighted * fade_out[:, :, None] + added)

    start_state = (
        jnp.full((volumes, head_count, tubelets), -1e30, jnp.float32),
        jnp.zeros((volumes, head_count, tubelets), jnp.float32),
        jnp.zeros((volumes, head_count, tubelets, HDIM), jnp.float32),
    )
    key_piece = lax.all_gather(keys, "seq", axis=1, tiled=True)
    val_piece = lax.all_gather(vals, "seq", axis=1, tiled=True)
    running, totals, weighted = lax.map(
        per_volume, (queries, key_piece, val_piece, start_state[0], start_state[1], start_state[2])
    )
    attended = (
        (weighted / totals[:, :, :, None])
        .transpose(0, 2, 1, 3)
        .reshape(rows_dev, head_width)
        .astype(jnp.bfloat16)
    )
    head_terms = jnp.dot(attended, w_attn_out, preferred_element_type=jnp.float32)
    summed = lax.psum_scatter(
        head_terms.astype(jnp.bfloat16), "mp", scatter_dimension=1, tiled=True
    ).astype(jnp.float32)
    decoded = (dec_own.astype(jnp.float32) + summed).astype(jnp.bfloat16)
    return decoded.reshape(volumes, tubelets, dec_part)


def solution(mesh):
    in_specs = (
        P(None, "seq", "mp"),
        P("seq", None, None),
        P("seq", None),
        P(None, "mp"),
        P("mp", None),
        P("mp", None),
        P(),
        P("seq", None),
        P(None, None, "mp"),
        P("mp", None),
    )
    out_specs = P(None, "seq", "mp")
    return jax.shard_map(local, mesh=mesh, in_specs=in_specs, out_specs=out_specs, check_vma=False)
```

profile of v0, /device:TPU:1, one launch (start us, length us, event | category | flops | bytes accessed | tf_op | source)
XLA Modules:
  0.0 476.1 jit_solution(7336436420903138380)
XLA Ops:
  6.5 0.8 fusion.69
  7.3 0.7 compare_and_fusion
  8.0 1.6 gather_fusion
  9.6 0.1 fusion.68
  9.6 19.6 %all-gather = bf16[8,160,64]{1,2,0:T(8,128)(2,1)S(1)} all-gather(bf16[1,160,64]{1,2,0:T(8,128)(2,1)S(1)} %fusion.68), channel_id=1, replica_groups=mesh['seq'=64,'mp'=8] {'mp'}, dimensions={0}, use_global_device_ids=true | all-gather | bytes 184320 | tf_op jit(solution)/shard_map/all_gather | solution.py:44
  29.2 0.2 copy.32
  29.4 0.1 convert_reduce_fusion.1
  29.5 0.2 reshape.159
  29.7 0.2 multiply_reduce_fusion
  30.0 3.6 convolution_bitcast_fusion
  33.7 0.0 reduce-scatter.10.cloned.1.call-update
  33.7 0.0 reduce-scatter.12.cloned.1.call-start
  33.8 0.1 constant_dynamic-slice_fusion.2
  33.9 0.1 convert_reduce_fusion.2
  34.0 35.5 %reduce-scatter.10.cloned.1.call-done = f32[160,64]{1,0:T(8,128)} async-done(((f32[1280,64]{1,0:T(8,128)}), f32[160,64]{1,0:T(8,128)}) %reduce-scatter.10.cloned.1.call-update) | async-done | bytes 40976
  69.5 1.0 copy.43
  70.5 1.0 convolution_bitcast_fusion.1
  71.5 0.0 reduce-scatter.12.cloned.1.call-update
  71.5 0.0 all-gather.4.cloned.1.call-start
  71.5 0.1 dynamic-slice_convert_fusion
  71.6 0.1 copy.46
  71.7 37.6 %reduce-scatter.12.cloned.1.call-done = f32[64,64]{1,0:T(8,128)} async-done(((f32[512,64]{1,0:T(8,128)}), f32[64,64]{1,0:T(8,128)}) %reduce-scatter.12.cloned.1.call-update) | async-done | bytes 16400
  109.4 0.8 copy.45
  110.2 0.2 fusion.10
  110.5 14.9 %all_gather.13 = bf16[256,512]{0,1:T(8,128)(2,1)S(1)} all-gather(bf16[256,64]{0,1:T(8,128)(2,1)S(1)} %fusion.10), channel_id=1, replica_groups=mesh['seq'=64,'mp'=8] {'mp'}, dimensions={1}, use_global_device_ids=true | all-gather | bytes 294912 | tf_op jit(solution)/shard_map/all_gather | solution.py:71
  125.3 0.1 convert_reduce_fusion
  125.4 0.1 fusion.13
  125.6 0.2 convolution_convert_fusion.1
  125.8 0.1 reshape.145
  125.9 0.7 copy.34
  126.7 0.0 all-gather.4.cloned.1.call-update
  126.7 0.0 all-gather.6.cloned.1.call-start
  126.8 0.1 reshape.146
  126.9 0.7 copy.35
  127.6 0.0 all-gather.6.cloned.1.call-update
  127.6 0.0 reduce-scatter.8.cloned.1.call-start
  127.7 0.1 reshape.144
  127.8 136.9 %all-gather.4.cloned.1.call-done = bf16[4,4096,64]{2,0,1:T(4,128)(2,1)} async-done(((bf16[4,64,64]{2,0,1:T(4,128)(2,1)}), bf16[4,4096,64]{2,0,1:T(4,128)(2,1)}) %all-gather.4.cloned.1.call-update) | async-done | bytes 2097168 | tf_op jit(solution)/shard_map/all_gather | solution.py:106
  264.7 7.0 %copy.37 = bf16[4,4096,64]{1,2,0:T(8,128)(2,1)} copy(bf16[4,4096,64]{2,0,1:T(4,128)(2,1)} %all-gather.4.cloned.1.call-done) | data formatting | bytes 4194304 | tf_op jit(solution)/shard_map/while | solution.py:108
  271.7 137.4 %all-gather.6.cloned.1.call-done = bf16[4,4096,64]{2,0,1:T(4,128)(2,1)} async-done(((bf16[4,64,64]{2,0,1:T(4,128)(2,1)}), bf16[4,4096,64]{2,0,1:T(4,128)(2,1)}) %all-gather.6.cloned.1.call-update) | async-done | bytes 2097168 | tf_op jit(solution)/shard_map/all_gather | solution.py:107
  409.1 7.0 %copy.38 = bf16[4,4096,64]{1,2,0:T(8,128)(2,1)} copy(bf16[4,4096,64]{2,0,1:T(4,128)(2,1)} %all-gather.6.cloned.1.call-done) | data formatting | bytes 4194304 | tf_op jit(solution)/shard_map/while | solution.py:108
  416.1 11.4 %while.12 = (s32[]{:T(128)}, f32[4,2,64]{2,1,0:T(2,128)S(1)}, f32[4,2,64,32]{2,3,1,0:T(8,128)S(1)}, bf16[4,64,2,32]{1,3,2,0:T(8,128)(2,1)S(1)}, bf16[4,4096,64]{...) while((s32[]{:T(128)}, f32[4,2,64]{2,1,0:T(2,128)S(1)}, f32[4,2,64,32]{2,3,1,0:T(8,128)S(1)}, ...), condition=%wide.region_10.11_spmd, body=%wide.region_7.10_spmd.sunk | while | flops 70259328 | bytes 9494621 | solution.py:108
  416.1 1.3 constant_dynamic-slice_fusion.4
  417.4 0.6 fusion.121
  418.0 0.5 fusion.123
  418.5 0.4 fusion.122
  419.0 1.3 constant_dynamic-slice_fusion.4
  420.3 0.6 fusion.121
  420.8 0.5 fusion.123
  421.3 0.4 fusion.122
  421.8 1.3 constant_dynamic-slice_fusion.4
  423.1 0.6 fusion.121
  423.7 0.5 fusion.123
  424.2 0.4 fusion.122
  424.6 1.3 constant_dynamic-slice_fusion.4
  425.9 0.6 fusion.121
  426.5 0.5 fusion.123
  427.0 0.4 fusion.122
  427.5 0.1 copy.39
  427.6 0.1 convert_element_type.83
  427.7 1.0 convolution_convert_fusion
  428.7 39.4 %reduce-scatter.8.cloned.1.call-done = bf16[256,64]{0,1:T(8,128)(2,1)} async-done(((bf16[256,512]{0,1:T(8,128)(2,1)}), bf16[256,64]{0,1:T(8,128)(2,1)}) %reduce-scatter.8.cloned.1.call-update) | async-done | bytes 32784 | tf_op jit(solution)/shard_map/reduce_scatter | solution.py:118
  468.1 0.8 add_convert_fusion
  468.9 0.7 copy.41
  (39 shorter events, 0.3 us)
Async XLA Ops:
  6.5 23.4 %copy-start = (bf16[640,1280]{1,0:T(8,128)(2,1)S(1)}, bf16[640,1280]{1,0:T(8,128)(2,1)}, u32[]{:S(2)}) copy-start(bf16[640,1280]{1,0:T(8,128)(2,1)} %param.16) | copy-start | bytes 4915204
  6.5 62.9 %reduce-scatter.10.cloned.1.call-start = ((), (), s32[]{:S(2)}) async-start(), calls=%async_computation.6 | async-start | bytes 737280
  30.0 3.8 copy-start.2
  30.0 3.9 copy-start.7
  30.0 3.9 copy-start.4
  30.0 40.5 %copy-start.1 = (bf16[160,512]{1,0:T(8,128)(2,1)S(1)}, bf16[160,512]{1,0:T(8,128)(2,1)}, u32[]{:S(2)}) copy-start(bf16[160,512]{1,0:T(8,128)(2,1)} %param.17) | copy-start | bytes 491524
  30.0 41.5 %copy-start.6 = (bf16[512]{0:T(512)(128)(2,1)S(1)}, bf16[512]{0:T(512)(128)(2,1)}, u32[]{:S(2)}) copy-start(bf16[512]{0:T(512)(128)(2,1)} %param.18) | copy-start | bytes 3076
  33.7 91.9 %copy-start.5 = (bf16[512,3,64]{0,2,1:T(8,128)(2,1)S(1)}, bf16[512,3,64]{0,2,1:T(8,128)(2,1)}, u32[]{:S(2)}) copy-start(bf16[512,3,64]{0,2,1:T(8,128)(2,1)} %param.20) | copy-start | bytes 589828
  33.7 75.7 %reduce-scatter.12.cloned.1.call-start = ((), (), s32[]{:S(2)}) async-start(), calls=%async_computation.7 | async-start | bytes 294912
  71.5 193.2 %all-gather.4.cloned.1.call-start = ((), (), s32[]{:S(2)}) async-start(), calls=%async_computation.3 | async-start | bytes 4259840 | tf_op jit(solution)/shard_map/all_gather | solution.py:106
  126.7 282.4 %all-gather.6.cloned.1.call-start = ((), (), s32[]{:S(2)}) async-start(), calls=%async_computation.4 | async-start | bytes 4259840 | tf_op jit(solution)/shard_map/all_gather | solution.py:107
  127.6 340.5 %reduce-scatter.8.cloned.1.call-start = ((), (), s32[]{:S(2)}) async-start(), calls=%async_computation.5 | async-start | bytes 294912 | tf_op jit(solution)/shard_map/reduce_scatter | solution.py:118
  416.1 11.6 %copy-start.3 = (bf16[64,512]{1,0:T(8,128)(2,1)S(1)}, bf16[64,512]{1,0:T(8,128)(2,1)}, u32[]{:S(2)}) copy-start(bf16[64,512]{1,0:T(8,128)(2,1)} %param.21) | copy-start | bytes 196612
Sparse Core Ops, SparseCore 0:
  33.8 35.6 reduce-scatter.9
  72.3 37.0 reduce-scatter.11
  126.8 137.8 all-gather.3
  267.9 141.1 all-gather.5
  428.8 39.2 reduce-scatter.7
where the time goes:
time: 478 us; the launch traced here: 476 us
  waiting for transfers between devices  387 us (81%)
  blocking collectives  34.4 us (7%)
  local copies, waits for them, and re-layouts  25.9 us (5%)
  between operations  13.4 us (3%)
  matrix products  10.3 us (2%)
  other arithmetic  4.99 us (1%)
    all_gather x1, waiting for transfers between devices, local(): val_piece = lax.all_gather(vals, 'seq', axis=1, tiled=True)  137 us
    all_gather x1, waiting for transfers between devices, local(): key_piece = lax.all_gather(keys, 'seq', axis=1, tiled=True)  137 us
    unnamed x7, waiting for transfers between devices  73.2 us
    reduce_scatter x1, waiting for transfers between devices, local(): lax.psum_scatter(head_terms.astype(jnp.bfloat16), 'mp', scatter_dimension...  39.4 us
    all_gather x1, blocking collectives, local(): full_rows = lax.all_gather(own_part, 'mp', axis=1, tiled=True)  19.6 us
    all_gather x1, blocking collectives, local(): dec_full = lax.all_gather(dec_own, 'mp', axis=1, tiled=True)  14.9 us
    while x3, local copies, waits for them, and re-layouts, local(): lax.map(per_volume, (queries, key_piece, val_piece, start_state[0], start...  14 us
  transfers between devices with their start and end apart: 5, of which 5 were waited for; matrix products, arithmetic and copies ran while one was open for 2% of the time, Pallas kernels for 0%

commit v1 on v0

v1 whole, which is shorter than its diff:
```python
import math

import jax
import jax.numpy as jnp
from jax import lax
from jax.sharding import Mesh, PartitionSpec as P

HDIM = 32
MP = ("x", "core")
BF = jnp.bfloat16
F32 = jnp.float32


def layer_norm(values):
    mean_row = jnp.mean(values, axis=-1, keepdims=True)
    spread = jnp.mean((values - mean_row) * (values - mean_row), axis=-1, keepdims=True)
    return (values - mean_row) * lax.rsqrt(spread + 1e-05)


def dot(a, b):
    return jnp.dot(a, b, preferred_element_type=F32)


def spread_out(part, axes):
    count = lax.axis_size(axes)
    return lax.all_to_all(
        jnp.broadcast_to(part[None], (count, *part.shape)), axes, 0, 0, tiled=True
    )


def pieces(values, count):
    out = []
    for _ in range(count):
        top = lax.reduce_precision(values, 8, 7)
        out.append(top.astype(BF))
        values = values - top
    return out


def place(picked, slot_vals, other_vals):
    seen = jnp.sum(picked.astype(F32), axis=-1, keepdims=True) > 0
    return jnp.where(seen, dot(picked, slot_vals).astype(BF), other_vals)


def local(
    tokens,
    visible_lists,
    visible_counts,
    w_in,
    w_out,
    w_embed,
    mask_token,
    positions,
    w_qkv,
    w_attn_out,
):
    vols, tubs, part = tokens.shape
    rows = vols * tubs
    mp_index = lax.axis_index(MP)
    mp_count = lax.axis_size(MP)
    nz = lax.axis_size("z")
    ny = lax.axis_size("y")
    dec = w_embed.shape[1]
    dec_part = dec // mp_count
    flat = tokens.reshape(rows, part)
    ids = visible_lists.reshape(-1)
    slots = ids.shape[0]
    live = visible_counts.reshape(-1) > 0
    live_ids = jnp.where(live, ids, rows)

    id_rows = jnp.zeros((16, dec), BF).at[0, :slots].set(live_ids.astype(BF))
    packed = jnp.concatenate([positions, id_rows], axis=0)
    column = lax.all_gather(packed, "z")

    named = (ids[:, None] == jnp.arange(rows, dtype=jnp.int32)[None, :]).astype(BF)
    own = dot(named, flat).astype(BF)
    full = spread_out(own, MP).transpose(1, 0, 2).reshape(slots, mp_count * part)
    normed = layer_norm(full.astype(F32)).astype(BF)
    hidden = jax.nn.gelu(dot(normed, w_in), approximate=False).astype(BF)
    terms = dot(hidden, w_out).astype(BF)
    terms = terms.reshape(slots, mp_count, part).transpose(1, 0, 2)
    terms = lax.all_to_all(terms, MP, 0, 0, tiled=True)
    encoded = (own.astype(F32) + jnp.sum(terms.astype(F32), axis=0)).astype(BF)
    embed_terms = dot(encoded, w_embed).astype(BF)
    embedded = jnp.sum(spread_out(embed_terms, MP).astype(F32), axis=0).astype(BF)

    pos_pick = ((ids % tubs)[:, None] == jnp.arange(tubs, dtype=jnp.int32)[None, :]).astype(BF)
    slot_pos = dot(pos_pick, positions)
    slot_in = (embedded.astype(F32) + slot_pos).astype(BF)
    mask_in = (mask_token.astype(F32)[None, :] + positions.astype(F32)).astype(BF)
    head_width = w_qkv.shape[2]
    heads = head_width // HDIM
    w_flat = w_qkv.reshape(dec, 3 * head_width)
    both = jnp.concatenate([mask_in, slot_in], axis=0)
    projected = dot(layer_norm(both.astype(F32)).astype(BF), w_flat).astype(BF)
    mask_q = projected[:tubs, :head_width]
    slot_q = projected[tubs:, :head_width]
    slot_kv = projected[tubs:, head_width:]

    picked = (live_ids[None, :] == jnp.arange(rows, dtype=jnp.int32)[:, None]).astype(BF)
    queries = place(picked, slot_q, jnp.tile(mask_q, (vols, 1)))
    start = mp_index * dec_part
    dec_own = place(
        picked,
        lax.dynamic_slice_in_dim(slot_in, start, dec_part, 1),
        jnp.tile(lax.dynamic_slice_in_dim(mask_in, start, dec_part, 1), (vols, 1)),
    )

    plane_q = spread_out(queries, "y")
    column_slots = spread_out(slot_kv, "z")

    column_pos = column[:, :tubs].reshape(nz * tubs, dec)
    column_ids = column[:, tubs, :slots].astype(jnp.int32)
    column_mask = (mask_token.astype(F32)[None, :] + column_pos.astype(F32)).astype(BF)
    mask_kv = dot(layer_norm(column_mask.astype(F32)).astype(BF), w_flat[:, head_width:]).astype(BF)
    mask_kv = mask_kv.reshape(nz, tubs, 2 * head_width)
    column_picked = (
        column_ids[:, None, :] == jnp.arange(rows, dtype=jnp.int32)[None, :, None]
    ).astype(BF)
    placed = jnp.einsum("zrs,zsc->zrc", column_picked, column_slots, preferred_element_type=F32)
    seen = jnp.sum(column_picked.astype(F32), axis=-1, keepdims=True) > 0
    kv = jnp.where(seen, placed.astype(BF), jnp.tile(mask_kv, (1, vols, 1)))
    kv = kv.reshape(nz, vols, tubs, 2, heads, HDIM)
    keys = kv[:, :, :, 0].transpose(1, 3, 0, 2, 4).reshape(vols, heads, nz * tubs, HDIM)
    vals = kv[:, :, :, 1].transpose(1, 3, 0, 2, 4).reshape(vols, heads, nz * tubs, HDIM)
    qs = plane_q.reshape(ny, vols, tubs, heads, HDIM).transpose(1, 3, 0, 2, 4)
    qs = qs.reshape(vols, heads, ny * tubs, HDIM)
    scores = jnp.einsum("vhqd,vhkd->vhqk", qs, keys, preferred_element_type=F32)
    scores = scores * (1.0 / math.sqrt(HDIM))
    top = jnp.max(scores, axis=-1)
    weights = jnp.exp(scores - top[..., None])
    totals = jnp.sum(weights, axis=-1)
    summed = jnp.einsum("vhqk,vhkd->vhqd", weights.astype(BF), vals, preferred_element_type=F32)

    stats = jnp.stack([*pieces(top, 3), *pieces(totals, 2)], axis=-1)
    message = jnp.concatenate([summed.astype(BF), stats], axis=-1)
    width = HDIM + 5
    message = message.reshape(vols, heads, ny, tubs, width).transpose(2, 0, 3, 1, 4)
    message = message.reshape(ny, rows, heads * width)
    message = lax.all_to_all(message, "y", 0, 0, tiled=True)
    message = message.reshape(ny, rows, heads, width).astype(F32)
    tops = message[..., HDIM] + message[..., HDIM + 1] + message[..., HDIM + 2]
    fade = jnp.exp(tops - jnp.max(tops, axis=0, keepdims=True))
    total = jnp.sum(fade * (message[..., HDIM + 3] + message[..., HDIM + 4]), axis=0)
    attended = jnp.sum(fade[..., None] * message[..., :HDIM], axis=0) / total[..., None]
    attended = attended.reshape(rows, head_width).astype(BF)

    head_terms = dot(attended, w_attn_out).astype(BF)
    head_terms = head_terms.reshape(rows, mp_count, dec_part).transpose(1, 0, 2)
    head_terms = lax.all_to_all(head_terms, MP, 0, 0, tiled=True)
    decoded = dec_own.astype(F32) + jnp.sum(head_terms.astype(F32), axis=0)
    return decoded.astype(BF).reshape(vols, tubs, dec_part)


def solution(mesh):
    fine = Mesh(mesh.devices.reshape(16, 4, 4, 2), ("z", "y", "x", "core"))
    seq = ("z", "y")
    in_specs = (
        P(None, seq, MP),
        P(seq, None, None),
        P(seq, None),
        P(None, MP),
        P(MP, None),
        P(MP, None),
        P(),
        P(seq, None),
        P(None, None, MP),
        P(MP, None),
    )
    out_specs = P(None, seq, MP)
    return jax.shard_map(local, mesh=fine, in_specs=in_specs, out_specs=out_specs, check_vma=False)
```

time: 478 us -> 164 us (0.34)
  waiting for transfers between devices: 387 us -> 38.4 us
  starting transfers between devices: 0.17 us -> 51.9 us
  blocking collectives: 34.4 us -> 9.08 us
  other arithmetic: 4.99 us -> 12.3 us
    all_gather x2 -> x1, waiting for transfers between devices: 274 us -> 5.64 us  [local(): column = lax.all_gather(packed, 'z')]
    unnamed x7 -> x1, waiting for transfers between devices: 73.2 us -> 0.02 us
    all_to_all x0 -> x6, starting transfers between devices: none -> 51.9 us  [the longest x4 29.3 us: spread_out(): lax.all_to_all(jnp.broadcast_to(part[None], (count, *part.shape)), axes,...]
    reduce_scatter x1 -> x0, waiting for transfers between devices: 39.4 us -> none  [local(): lax.psum_scatter(head_terms.astype(jnp.bfloat16), 'mp', scatter_dimension...]
    all_gather x2 -> x0, blocking collectives: 34.4 us -> none  [the longest x1 19.6 us: local(): full_rows = lax.all_gather(own_part, 'mp', axis=1, tiled=True)]
    all_to_all x0 -> x6, waiting for transfers between devices: none -> 32.7 us  [the longest x4 20 us: spread_out(): lax.all_to_all(jnp.broadcast_to(part[None], (count, *part.shape)), axes,...]
    while x3 -> x0, local copies, waits for them, and re-layouts: 14 us -> none  [local(): lax.map(per_volume, (queries, key_piece, val_piece, start_state[0], start...]
    all_to_all x0 -> x1, blocking collectives: none -> 9.08 us  [local(): message = lax.all_to_all(message, 'y', 0, 0, tiled=True)]
  transfers between devices with their start and end apart: 5 -> 7, of which waited for: 5 -> 7; matrix products, arithmetic and copies ran while one was open for 2% -> 10% of each run, Pallas kernels for 0% -> 0%
where the time goes in v1:
time: 164 us; the launch traced here: 163 us
  starting transfers between devices  51.9 us (32%)
  waiting for transfers between devices  38.4 us (23%)
  local copies, waits for them, and re-layouts  22.5 us (14%)
  matrix products  14.6 us (9%)
  between operations  13.9 us (8%)
  other arithmetic  12.3 us (8%)
  blocking collectives  9.08 us (6%)
    all_to_all x4, starting transfers between devices, spread_out(): lax.all_to_all(jnp.broadcast_to(part[None], (count, *part.shape)), axes,...  29.3 us
    all_to_all x4, waiting for transfers between devices, spread_out(): lax.all_to_all(jnp.broadcast_to(part[None], (count, *part.shape)), axes,...  20 us
    all_to_all x1, starting transfers between devices, local(): head_terms = lax.all_to_all(head_terms, MP, 0, 0, tiled=True)  18 us
    all_to_all x1, blocking collectives, local(): message = lax.all_to_all(message, 'y', 0, 0, tiled=True)  9.08 us
    all_to_all x1, waiting for transfers between devices, local(): terms = lax.all_to_all(terms, MP, 0, 0, tiled=True)  6.51 us
    all_to_all x1, waiting for transfers between devices, local(): head_terms = lax.all_to_all(head_terms, MP, 0, 0, tiled=True)  6.18 us
    dot_general x9, matrix products, dot(): return jnp.dot(a, b, preferred_element_type=F32)  5.64 us
    all_gather x1, waiting for transfers between devices, local(): column = lax.all_gather(packed, 'z')  5.64 us
  transfers between devices with their start and end apart: 7, of which 7 were waited for; matrix products, arithmetic and copies ran while one was open for 10% of the time, Pallas kernels for 0%

profile of v1, /device:TPU:1, one launch (start us, length us, event | category | flops | bytes accessed | tf_op | source)
XLA Modules:
  0.0 162.6 jit_solution(8606620028102689636)
XLA Ops:
  6.5 1.2 convolution_convert_fusion.8
  7.8 0.7 broadcast_in_dim.30
  8.5 10.2 %all-to-all-start = ((bf16[8,64,160]{2,1,0:T(8,128)(2,1)}), bf16[8,64,160]{2,1,0:T(8,128)(2,1)S(1)}, u32[]{:S(2)}, u32[]{:S(2)}) async-start(bf16[8,64,160]{2,1,0:T(8,128)(2,1)} %broadcast_in_dim.30), calls=%async_computation | async-start | bytes 524288 | tf_op jit(solution)/shard_map/all_to_all | solution.py:26
  18.7 0.7 fusion.127
  19.4 1.5 fusion.46
  20.9 4.4 %all-to-all-done = bf16[8,64,160]{2,1,0:T(8,128)(2,1)S(1)} async-done(((bf16[8,64,160]{2,1,0:T(8,128)(2,1)}), bf16[8,64,160]{2,1,0:T(8,128)(2,1)S(1)}, u32[]{:S(2)}, u32[]{:S(2)}) %all-to-all-start) | async-done | bytes 163872 | tf_op jit(solution)/shard_map/all_to_all | solution.py:26
  25.2 0.1 convert_reduce_fusion.2
  25.4 0.2 fusion.21
  25.7 0.3 copy.63
  26.0 0.2 reshape.307
  26.3 2.6 %convolution_convert_fusion = bf16[64,1280]{1,0:T(8,128)(2,1)S(1)} fusion(bf16[640,1280]{1,0:T(8,128)(2,1)S(1)} %copy-done, bf16[1280,640]{1,0:T(8,128)(2,1)} %param.15, f32[64,1280]{1,0:T(8,128)S(1)} %reshape.307, f32[64]{0:T(128)S(1)} %add_rsqrt_fusion.2, f32[64]{0:T(128)S(1)} %broadcast_multiply_fusion.2), kind=kOutput, calls=%fused_computation.7 | convolution fusion | flops 212705280 | bytes 3768832 | tf_op jit(solution)/shard_map/dot_general | solution.py:21
  28.9 0.3 reshape.297
  29.2 0.8 copy.89
  30.0 4.5 %all-to-all-start.1 = ((bf16[8,64,160]{2,1,0:T(8,128)(2,1)}), bf16[8,64,160]{2,1,0:T(8,128)(2,1)S(1)}, u32[]{:S(2)}, u32[]{:S(2)}) async-start(bf16[8,64,160]{2,1,0:T(8,128)(2,1)} %bitcast.90), calls=%async_computation.1 | async-start | bytes 524288 | tf_op jit(solution)/shard_map/all_to_all | solution.py:82
  34.5 6.5 %all-to-all-done.1 = bf16[8,64,160]{2,1,0:T(8,128)(2,1)S(1)} async-done(((bf16[8,64,160]{2,1,0:T(8,128)(2,1)}), bf16[8,64,160]{2,1,0:T(8,128)(2,1)S(1)}, u32[]{:S(2)}, u32[]{:S(2)}) %all-to-all-start.1) | async-done | bytes 163872 | tf_op jit(solution)/shard_map/all_to_all | solution.py:82
  41.0 0.1 convolution_convert_fusion.4
  41.2 0.9 broadcast_in_dim.31
  42.1 4.4 %all-to-all-start.2 = ((bf16[8,64,512]{2,1,0:T(8,128)(2,1)}), bf16[8,64,512]{2,1,0:T(8,128)(2,1)S(1)}, u32[]{:S(2)}, u32[]{:S(2)}) async-start(bf16[8,64,512]{2,1,0:T(8,128)(2,1)} %broadcast_in_dim.31), calls=%async_computation.2 | async-start | bytes 1048576 | tf_op jit(solution)/shard_map/all_to_all | solution.py:26
  46.6 9.3 %all-to-all-done.2 = bf16[8,64,512]{2,1,0:T(8,128)(2,1)S(1)} async-done(((bf16[8,64,512]{2,1,0:T(8,128)(2,1)}), bf16[8,64,512]{2,1,0:T(8,128)(2,1)S(1)}, u32[]{:S(2)}, u32[]{:S(2)}) %all-to-all-start.2) | async-done | bytes 524320 | tf_op jit(solution)/shard_map/all_to_all | solution.py:26
  56.1 0.2 fusion.11
  56.4 0.2 fusion.25
  56.6 0.3 convolution_convert_fusion.5
  57.1 0.2 fusion.16
  57.3 0.7 broadcast_in_dim.32
  57.9 3.3 %all-to-all-start.3 = ((bf16[4,256,64]{1,2,0:T(8,128)(2,1)}), bf16[4,256,64]{1,2,0:T(8,128)(2,1)S(1)}, u32[]{:S(2)}, u32[]{:S(2)}) async-start(bf16[4,256,64]{1,2,0:T(8,128)(2,1)} %broadcast_in_dim.32), calls=%async_computation.3 | async-start | bytes 262144 | tf_op jit(solution)/shard_map/all_to_all | solution.py:26
  61.4 4.6 %all-to-all-done.3 = bf16[4,256,64]{1,2,0:T(8,128)(2,1)S(1)} async-done(((bf16[4,256,64]{1,2,0:T(8,128)(2,1)}), bf16[4,256,64]{1,2,0:T(8,128)(2,1)S(1)}, u32[]{:S(2)}, u32[]{:S(2)}) %all-to-all-start.3) | async-done | bytes 131104 | tf_op jit(solution)/shard_map/all_to_all | solution.py:26
  66.0 0.8 broadcast_in_dim.34
  66.8 11.4 %all-to-all-start.4 = ((bf16[16,64,128]{2,1,0:T(8,128)(2,1)}), bf16[16,64,128]{2,1,0:T(8,128)(2,1)S(1)}, u32[]{:S(2)}, u32[]{:S(2)}) async-start(bf16[16,64,128]{2,1,0:T(8,128)(2,1)} %broadcast_in_dim.34), calls=%async_computation.4 | async-start | bytes 524288 | tf_op jit(solution)/shard_map/all_to_all | solution.py:26
  78.2 0.2 reshape.299
  78.4 0.2 copy.66
  78.6 0.2 reshape.300
  78.8 5.6 %all-gather.3.cloned.1.call-done = bf16[1280,512]{1,0:T(8,128)(2,1)} async-done(((bf16[80,512]{1,0:T(8,128)(2,1)}), bf16[1280,512]{1,0:T(8,128)(2,1)}) %all-gather.3.cloned.1.call-update) | async-done | bytes 1310736 | tf_op jit(solution)/shard_map/all_gather | solution.py:73
  84.5 1.6 convert_reduce_fusion
  86.2 1.7 %fusion.5 = f32[16,64]{1,0:T(8,128)S(1)} fusion(f32[16,64]{1,0:T(8,128)S(1)} %broadcast_multiply_fusion, bf16[16,80,512]{2,1,0:T(8,128)(2,1)} %bitcast.92, f32[512]{0:T(512)S(1)} %convert_element_type.227), kind=kLoop, calls=%fused_computation.9 | loop fusion | flops 3668992 | bytes 1058816 | tf_op jit(solution)/shard_map/reduce_sum | solution.py:16
  88.0 0.2 convert_reduce_fusion.1
  88.2 0.3 slice_convert_fusion
  88.5 0.3 fusion.6
  88.8 0.6 copy-done.10
  89.4 0.5 convolution_convert_fusion.3
  89.9 1.7 %all-to-all-done.4 = bf16[16,64,128]{2,1,0:T(8,128)(2,1)S(1)} async-done(((bf16[16,64,128]{2,1,0:T(8,128)(2,1)}), bf16[16,64,128]{2,1,0:T(8,128)(2,1)S(1)}, u32[]{:S(2)}, u32[]{:S(2)}) %all-to-all-start.4) | async-done | bytes 262176 | tf_op jit(solution)/shard_map/all_to_all | solution.py:26
  91.6 0.2 tile.33
  91.9 2.8 %fusion.7 = bf16[16,256,128]{2,1,0:T(8,128)(2,1)} fusion(bf16[16,256,128]{2,1,0:T(8,128)(2,1)S(1)} %bitcast.99, bf16[16,64,128]{2,1,0:T(8,128)(2,1)S(1)} %all-to-all-done.4, pred[16,256]{1,0:T(8,128)(4,1)S(1)} %broadcast_compare_fusion, s32[16,64]{1,0:T(8,128)S(1)} %bitcast.105), kind=kOutput, calls=%fused_computation.15 | convolution fusion | flops 68419584 | bytes 2367488 | tf_op jit(solution)/shard_map/zrs,zsc->zrc/dot_general | solution.py:120
  94.6 1.5 copy.68
  96.1 1.9 %reshape.301 = bf16[16,4,64,2,2,32]{2,1,5,4,3,0:T(4,128)(2,1)} reshape(bf16[16,256,128]{1,2,0:T(8,128)(2,1)S(1)} %copy.68) | data formatting | bytes 2097152 | tf_op jit(solution)/shard_map/reshape | solution.py:123
  98.0 3.7 %slice_bitcast_fusion.1 = (bf16[4,2,16,64,32]{3,0,4,1,2:T(4,128)(2,1)S(1)}, bf16[4,2,16,64,32]{3,0,4,1,2:T(4,128)(2,1)}) fusion(bf16[16,4,64,2,2,32]{2,1,5,4,3,0:T(4,128)(2,1)} %reshape.301), kind=kLoop, calls=%fused_computation.32 | loop fusion | bytes 2097152 | tf_op jit(solution)/shard_map/transpose | solution.py:124
  101.7 0.7 copy.69
  102.3 0.7 reshape.302
  103.1 1.9 %copy.70 = bf16[4,2,16,64,32]{3,2,4,1,0:T(8,128)(2,1)S(1)} copy(bf16[4,2,16,64,32]{3,0,4,1,2:T(4,128)(2,1)} %get-tuple-element.20) | data formatting | bytes 1048576 | tf_op jit(solution)/shard_map/transpose | solution.py:125
  105.0 1.6 reshape.303
  106.5 4.5 %multiply_reduce_fusion = (f32[4,2,256]{2,1,0:T(2,128)S(1)}, f32[4,2,256,1024]{3,2,1,0:T(8,128)}) fusion(bf16[4,2,256,32]{2,3,1,0:T(8,128)(2,1)S(1)} %reshape.300, bf16[4,2,1024,32]{2,3,1,0:T(8,128)(2,1)S(1)} %reshape.302), kind=kOutput, calls=%fused_computation.1 | convolution fusion | flops 138409984 | bytes 9052160 | tf_op jit(solution)/shard_map/vhqd,vhkd->vhqk/dot_general | solution.py:128
  111.1 4.7 %fusion = f32[4,2,256]{2,1,0:T(2,128)S(1)} fusion(f32[4,2,256,1024]{3,2,1,0:T(8,128)} %get-tuple-element.29, f32[4,2,256]{2,1,0:T(2,128)S(1)} %get-tuple-element.28), kind=kLoop, calls=%fused_computation.2 | loop fusion | flops 6289408 | bytes 8404992 | tf_op jit(solution)/shard_map/reduce_sum | solution.py:132
  115.9 1.1 copy-done.1
  117.0 1.7 %fusion.8 = bf16[4,2,256,32]{2,3,1,0:T(8,128)(2,1)S(1)} fusion(bf16[4,2,1024,32]{2,3,1,0:T(8,128)(2,1)S(1)} %copy-done.3, f32[4,2,256,1024]{3,2,1,0:T(8,128)S(1)} %copy-done.1, f32[4,2,256]{2,1,0:T(2,128)S(1)} %get-tuple-element.28), kind=kOutput, calls=%fused_computation.18 | convolution fusion | flops 140574720 | bytes 9052160 | tf_op jit(solution)/shard_map/vhqk,vhkd->vhqd/dot_general | solution.py:133
  118.8 0.2 concatenate.16
  119.0 0.3 copy_dynamic-update-slice_fusion
  119.4 0.2 reshape.304
  119.7 9.1 %all_to_all.35 = bf16[4,256,74]{1,2,0:T(8,128)(2,1)S(1)} all-to-all(bf16[4,256,74]{1,2,0:T(8,128)(2,1)S(1)} %copy.77), channel_id=1, replica_groups=mesh['z'=16,'y'=4,'x'=4,'core'=2] {'y'}, dimensions={0} | all-to-all | bytes 303104 | tf_op jit(solution)/shard_map/all_to_all | solution.py:140
  128.9 0.2 fusion.27
  129.1 0.2 convolution_convert_fusion.2
  129.4 0.8 copy.79
  130.2 18.0 %all-to-all-start.6 = ((bf16[8,256,64]{1,2,0:T(8,128)(2,1)}), bf16[8,256,64]{1,2,0:T(8,128)(2,1)S(1)}, u32[]{:S(2)}, u32[]{:S(2)}) async-start(bf16[8,256,64]{1,2,0:T(8,128)(2,1)} %bitcast.24), calls=%async_computation.6 | async-start | bytes 524288 | tf_op jit(solution)/shard_map/all_to_all | solution.py:150
  148.6 6.2 %all-to-all-done.6 = bf16[8,256,64]{1,2,0:T(8,128)(2,1)S(1)} async-done(((bf16[8,256,64]{1,2,0:T(8,128)(2,1)}), bf16[8,256,64]{1,2,0:T(8,128)(2,1)S(1)}, u32[]{:S(2)}, u32[]{:S(2)}) %all-to-all-start.6) | async-done | bytes 262176 | tf_op jit(solution)/shard_map/all_to_all | solution.py:150
  154.8 0.3 fusion.15
  155.1 0.7 copy.81
  (66 shorter events, 1.8 us)
Async XLA Ops:
  6.5 19.7 %copy-start = (bf16[640,1280]{1,0:T(8,128)(2,1)S(1)}, bf16[640,1280]{1,0:T(8,128)(2,1)}, u32[]{:S(2)}) copy-start(bf16[640,1280]{1,0:T(8,128)(2,1)} %param.16) | copy-start | bytes 4915204
  8.5 16.7 %all-to-all-start = ((bf16[8,64,160]{2,1,0:T(8,128)(2,1)}), bf16[8,64,160]{2,1,0:T(8,128)(2,1)S(1)}, u32[]{:S(2)}, u32[]{:S(2)}) async-start(bf16[8,64,160]{2,1,0:T(8,128)(2,1)} %broadcast_in_dim.30), calls=%async_computation | async-start | bytes 524288 | tf_op jit(solution)/shard_map/all_to_all | solution.py:26
  18.7 65.8 %all-gather.3.cloned.1.call-start = ((), (), s32[]{:S(2)}) async-start(), calls=%async_computation.7 | async-start | bytes 1392640 | tf_op jit(solution)/shard_map/all_gather | solution.py:73
  26.2 8.2 %copy-start.7 = (s32[1,64,1]{1,2,0:T(1,128)S(1)}, s32[1,64,1]{1,2,0:T(1,128)}, u32[]{:S(2)}) copy-start(s32[1,64,1]{1,2,0:T(1,128)} %param.13) | copy-start | bytes 772
  26.3 14.8 %copy-start.5 = (bf16[160,512]{1,0:T(8,128)(2,1)S(1)}, bf16[160,512]{1,0:T(8,128)(2,1)}, u32[]{:S(2)}) copy-start(bf16[160,512]{1,0:T(8,128)(2,1)} %param.17) | copy-start | bytes 491524
  28.8 17.8 %copy-start.8 = (bf16[512]{0:T(512)(128)(2,1)S(1)}, bf16[512]{0:T(512)(128)(2,1)}, u32[]{:S(2)}) copy-start(bf16[512]{0:T(512)(128)(2,1)} %param.18) | copy-start | bytes 3076
  28.8 17.8 %copy-start.4 = (bf16[64,512]{1,0:T(8,128)(2,1)S(1)}, bf16[64,512]{1,0:T(8,128)(2,1)}, u32[]{:S(2)}) copy-start(bf16[64,512]{1,0:T(8,128)(2,1)} %param.19) | copy-start | bytes 196612
  30.0 26.6 %copy-start.9 = (bf16[512,3,64]{0,2,1:T(8,128)(2,1)S(1)}, bf16[512,3,64]{0,2,1:T(8,128)(2,1)}, u32[]{:S(2)}) copy-start(bf16[512,3,64]{0,2,1:T(8,128)(2,1)} %param.20) | copy-start | bytes 589828
  30.0 11.0 %all-to-all-start.1 = ((bf16[8,64,160]{2,1,0:T(8,128)(2,1)}), bf16[8,64,160]{2,1,0:T(8,128)(2,1)S(1)}, u32[]{:S(2)}, u32[]{:S(2)}) async-start(bf16[8,64,160]{2,1,0:T(8,128)(2,1)} %bitcast.90), calls=%async_computation.1 | async-start | bytes 524288 | tf_op jit(solution)/shard_map/all_to_all | solution.py:82
  42.1 13.9 %all-to-all-start.2 = ((bf16[8,64,512]{2,1,0:T(8,128)(2,1)}), bf16[8,64,512]{2,1,0:T(8,128)(2,1)S(1)}, u32[]{:S(2)}, u32[]{:S(2)}) async-start(bf16[8,64,512]{2,1,0:T(8,128)(2,1)} %broadcast_in_dim.31), calls=%async_computation.2 | async-start | bytes 1048576 | tf_op jit(solution)/shard_map/all_to_all | solution.py:26
  57.9 8.1 %all-to-all-start.3 = ((bf16[4,256,64]{1,2,0:T(8,128)(2,1)}), bf16[4,256,64]{1,2,0:T(8,128)(2,1)S(1)}, u32[]{:S(2)}, u32[]{:S(2)}) async-start(bf16[4,256,64]{1,2,0:T(8,128)(2,1)} %broadcast_in_dim.32), calls=%async_computation.3 | async-start | bytes 262144 | tf_op jit(solution)/shard_map/all_to_all | solution.py:26
  66.8 24.8 %all-to-all-start.4 = ((bf16[16,64,128]{2,1,0:T(8,128)(2,1)}), bf16[16,64,128]{2,1,0:T(8,128)(2,1)S(1)}, u32[]{:S(2)}, u32[]{:S(2)}) async-start(bf16[16,64,128]{2,1,0:T(8,128)(2,1)} %broadcast_in_dim.34), calls=%async_computation.4 | async-start | bytes 524288 | tf_op jit(solution)/shard_map/all_to_all | solution.py:26
  84.5 3.4 %copy-start.2 = (bf16[1280,512]{1,0:T(8,128)(2,1)S(1)}, bf16[1280,512]{1,0:T(8,128)(2,1)}, u32[]{:S(2)}) copy-start(bf16[1280,512]{1,0:T(8,128)(2,1)} %all-gather.3.cloned.1.call-done) | copy-start | bytes 3932164
  88.5 0.9 copy-start.10
  106.5 9.3 %copy-start.3 = (bf16[4,2,1024,32]{2,3,1,0:T(8,128)(2,1)S(1)}, bf16[4,2,1024,32]{2,3,1,0:T(8,128)(2,1)}, u32[]{:S(2)}) copy-start(bf16[4,2,1024,32]{2,3,1,0:T(8,128)(2,1)} %reshape.303) | copy-start | bytes 1572868
  111.1 5.8 %copy-start.1 = (f32[4,2,256,1024]{3,2,1,0:T(8,128)S(1)}, f32[4,2,256,1024]{3,2,1,0:T(8,128)}, u32[]{:S(2)}) copy-start(f32[4,2,256,1024]{3,2,1,0:T(8,128)} %get-tuple-element.29) | copy-start | bytes 25165828
  118.7 10.4 %copy-start.6 = (bf16[64,512]{1,0:T(8,128)(2,1)S(1)}, bf16[64,512]{1,0:T(8,128)(2,1)}, u32[]{:S(2)}) copy-start(bf16[64,512]{1,0:T(8,128)(2,1)} %param.21) | copy-start | bytes 196612
  130.2 24.5 %all-to-all-start.6 = ((bf16[8,256,64]{1,2,0:T(8,128)(2,1)}), bf16[8,256,64]{1,2,0:T(8,128)(2,1)S(1)}, u32[]{:S(2)}, u32[]{:S(2)}) async-start(bf16[8,256,64]{1,2,0:T(8,128)(2,1)} %bitcast.24), calls=%async_computation.6 | async-start | bytes 524288 | tf_op jit(solution)/shard_map/all_to_all | solution.py:150
Sparse Core Ops, SparseCore 0:
  21.6 62.8 all-gather.2

commit v2 on v1

v2 whole, which is shorter than its diff:
```python
import functools
import math

import jax
import jax.numpy as jnp
from jax import lax
from jax.experimental import pallas as pl
from jax.experimental.pallas import tpu as pltpu
from jax.sharding import Mesh, PartitionSpec as P

HDIM = 32
MP = ("x", "core")
GROUP = ("zp", "y")
COLUMN = ("zz", "zp")
BF = jnp.bfloat16
F32 = jnp.float32
I32 = jnp.int32


def iota(shape, dim):
    return lax.broadcasted_iota(I32, shape, dim)


def dot(a, b):
    return jnp.dot(a, b, preferred_element_type=F32)


def dot_tn(a, b):
    return lax.dot_general(a, b, (((0,), (0,)), ((), ())), preferred_element_type=F32)


def dot_nt(a, b):
    return lax.dot_general(a, b, (((1,), (1,)), ((), ())), preferred_element_type=F32)


def norm_rows(values):
    mean_row = jnp.mean(values, axis=-1, keepdims=True)
    off = values - mean_row
    spread = jnp.mean(off * off, axis=-1, keepdims=True)
    return off * lax.rsqrt(spread + 1e-05)


def column_of(row):
    n = row.shape[1]
    return jnp.sum(jnp.where(iota((n, n), 0) == iota((n, n), 1), row, 0), axis=1, keepdims=True)


def live_row(lists, counts, rows):
    return jnp.where(counts > 0, lists, rows)


def fold_tail(block):
    tail = block[:, 128:]
    rows = tail.shape[0] // 4
    extra = jnp.concatenate([tail[k * rows : (k + 1) * rows] for k in range(4)], axis=1)
    return jnp.concatenate([block[:, :128], extra], axis=0)


def unfold_tail(folded):
    extra = folded[64:]
    tail = jnp.concatenate([extra[:, 32 * k : 32 * k + 32] for k in range(4)], axis=0)
    return jnp.concatenate([folded[:64], tail], axis=1)


def pick_kernel(lists, counts, tokens, out):
    rows = tokens.shape[0]
    ids = column_of(lists[...])
    named = (ids == iota((ids.shape[0], rows), 1)).astype(F32).astype(BF)
    own = fold_tail(dot(named, tokens[...])).astype(BF)
    for k in range(out.shape[0]):
        out[k] = own


def feed_kernel(gathered, w_in, w_out, out):
    count = gathered.shape[0]
    part = w_in.shape[0] // count
    blocks = [unfold_tail(gathered[k].astype(F32)) for k in range(count)]
    width = count * part
    mean_row = sum(jnp.sum(b, axis=1, keepdims=True) for b in blocks) * (1.0 / width)
    blocks = [b - mean_row for b in blocks]
    spread = sum(jnp.sum(b * b, axis=1, keepdims=True) for b in blocks) * (1.0 / width)
    scale = lax.rsqrt(spread + 1e-05)
    hidden = None
    for k in range(count):
        term = dot((blocks[k] * scale).astype(BF), w_in[k * part : (k + 1) * part, :])
        hidden = term if hidden is None else hidden + term
    act = (0.5 * hidden * (1.0 + lax.erf(hidden * math.sqrt(0.5)))).astype(BF)
    terms = dot(act, w_out[...])
    for k in range(count):
        out[k] = fold_tail(terms[:, k * part : (k + 1) * part]).astype(BF)


def embed_kernel(terms, own, w_embed, out):
    total = own[0].astype(F32) + sum(terms[k].astype(F32) for k in range(terms.shape[0]))
    encoded = unfold_tail(total).astype(BF)
    value = dot(encoded, w_embed[...]).astype(BF)
    for k in range(out.shape[0]):
        out[k] = value


def masked_kernel(mask_token, positions, w_all, out):
    mask_in = (mask_token[...].astype(F32) + positions[...].astype(F32)).astype(BF)
    out[...] = dot(norm_rows(mask_in.astype(F32)).astype(BF), w_all[...]).astype(BF)


def project_kernel(parts, lists, counts, positions, masked, w_all, slot_in, q_out, kv_out):
    tubs = positions.shape[0]
    slots = lists.shape[1]
    ids_row = live_row(lists[...], counts[...], 4 * tubs)
    ids = column_of(ids_row)
    embedded = sum(parts[k].astype(F32) for k in range(parts.shape[0])).astype(BF).astype(F32)
    at = (ids % tubs == iota((slots, tubs), 1)).astype(F32).astype(BF)
    row_in = (embedded + dot(at, positions[...])).astype(BF)
    slot_in[...] = row_in
    proj = dot(norm_rows(row_in.astype(F32)).astype(BF), w_all[...]).astype(BF)

    spot = (ids_row % tubs == iota((tubs, slots), 0)).astype(F32).astype(BF)
    of_volume = ids // tubs == iota((slots, 128), 1) // HDIM
    seen = dot(spot, of_volume.astype(F32).astype(BF)) > 0
    zero = jnp.zeros((slots, 128), BF)
    extra = jnp.concatenate(
        [
            jnp.concatenate([ids_row.astype(F32), jnp.zeros((1, 128 - slots), F32)], axis=1),
            jnp.zeros((15, 128), F32),
        ],
        axis=0,
    ).astype(BF)
    for head in range(2):
        cols = slice(128 * head, 128 * head + 128)
        placed = dot(spot, jnp.where(of_volume, proj[:, cols], zero))
        query = jnp.where(seen, placed, masked[:, cols].astype(F32)).astype(BF)
        for k in range(4):
            q_out[4 * head + k] = query
        cols = slice(256 + 64 * head, 256 + 64 * head + 64)
        block = jnp.concatenate([masked[:, cols], proj[:, cols]], axis=1)
        block = jnp.concatenate([block, extra], axis=0)
        for k in range(8):
            kv_out[2 * k + head] = block


def own_kernel(start, lists, counts, mask_token, positions, slot_in, out):
    tubs = positions.shape[0]
    feats, rows = out.shape
    slots = lists.shape[1]
    dec = positions.shape[1]
    ids = column_of(live_row(lists[...], counts[...], rows))
    choose = (iota((dec, feats), 0) == iota((dec, feats), 1) + start[0]).astype(F32).astype(BF)
    mask_in = (mask_token[...].astype(F32) + positions[...].astype(F32)).astype(BF)
    mask_own = dot(mask_in, choose).astype(BF)
    slot_own = dot(slot_in[...], choose).astype(BF)
    picked = (ids == iota((slots, rows), 1)).astype(F32)
    seen = jnp.sum(picked, axis=0, keepdims=True) > 0
    tile = (iota((tubs, rows), 0) == iota((tubs, rows), 1) % tubs).astype(F32).astype(BF)
    out[...] = jnp.where(seen, dot_tn(slot_own, picked.astype(BF)), dot_tn(mask_own, tile)).astype(BF)


def split_pieces(values, count):
    out = []
    for _ in range(count):
        top = values.astype(BF).astype(F32)
        out.append(top)
        values = values - top
    return out


def attend_kernel(queries, column, out, kv_scr, msg_scr):
    blocks, tubs = queries.shape[0], queries.shape[1]
    nz = column.shape[0]
    vols = 4
    rows = vols * tubs
    slots = 64
    keys = nz * tubs
    for k in range(nz):
        block = column[k, :tubs, :]
        ids_row = column[k, tubs : tubs + 16, :][0:1, :slots].astype(F32)
        picked = (ids_row == iota((rows, slots), 0).astype(F32)).astype(F32)
        seen = jnp.sum(picked, axis=1, keepdims=True) > 0
        placed = dot(picked.astype(BF), block[:, 64:])
        other = block[:, :64].astype(F32)
        other = jnp.concatenate([other] * vols, axis=0)
        mat = jnp.where(seen, placed, other).astype(BF)
        for v in range(vols):
            kv_scr[v, k * tubs : (k + 1) * tubs, :] = mat[v * tubs : (v + 1) * tubs]
    packed = queries[...].reshape(blocks * tubs, 128)
    scale = math.log2(math.e) / math.sqrt(HDIM)
    chunk = 256
    per = chunk // tubs
    for v in range(vols):
        lanes = iota((128, 64), 0)
        take = (lanes == iota((128, 64), 1) + HDIM * v) & (iota((128, 64), 1) < HDIM)
        query = dot(packed, take.astype(F32).astype(BF)).astype(BF)
        kv = kv_scr[v]
        for c in range(blocks // per):
            scores = dot_nt(kv, query[c * chunk : (c + 1) * chunk])
            top = jnp.max(scores, axis=0, keepdims=True)
            weights = jnp.exp2((scores - top) * scale)
            total = jnp.sum(weights, axis=0, keepdims=True)
            summed = dot_tn(kv, weights.astype(BF))[HDIM:]
            stats = jnp.concatenate(
                split_pieces(top * scale, 3) + split_pieces(total, 2) + [jnp.zeros((3, chunk), F32)],
                axis=0,
            )
            side = slice(64 * (v % 2), 64 * (v % 2) + 64)
            for b in range(per):
                cols = slice(b * tubs, (b + 1) * tubs)
                dest = c * per + b
                msg_scr[dest, HDIM * (v // 2) : HDIM * (v // 2) + HDIM, side] = summed[:, cols]
                msg_scr[dest, 64 + 8 * (v // 2) : 72 + 8 * (v // 2), side] = stats[:, cols]
    for b in range(blocks):
        out[b] = msg_scr[b].astype(BF)


def combine_kernel(message, w_attn_out, out):
    ny = 4
    parts = []
    for head in range(2):
        sides = []
        for u in range(2):
            stats = [message[4 * head + k, 64:, :].astype(F32)[8 * u : 8 * u + 8] for k in range(ny)]
            tops = [s[0:1] + s[1:2] + s[2:3] for s in stats]
            best = functools.reduce(jnp.maximum, tops)
            fades = [jnp.exp2(t - best) for t in tops]
            total = sum(f * (s[3:4] + s[4:5]) for f, s in zip(fades, stats))
            value = sum(
                f * message[4 * head + k, HDIM * u : HDIM * u + HDIM, :].astype(F32)
                for k, f in enumerate(fades)
            )
            sides.append(value / total)
        parts.append(jnp.concatenate(sides, axis=1))
    attended = jnp.concatenate(parts, axis=0).astype(BF)
    terms = dot_tn(w_attn_out[...], attended).astype(BF)
    count, feats, rows = out.shape
    for k in range(count):
        out[k] = terms[k * feats : (k + 1) * feats]


def finish_kernel(terms, dec_own, out):
    total = dec_own[...].astype(F32) + sum(terms[k].astype(F32) for k in range(terms.shape[0]))
    vols, tubs, feats = out.shape
    out[...] = total.T.astype(BF).reshape(vols, tubs, feats)


def call(kernel, out, *args, scratch=(), smem=0, cost=None):
    specs = [pl.BlockSpec(memory_space=pltpu.SMEM)] * smem
    specs += [pl.BlockSpec(memory_space=pltpu.VMEM)] * (len(args) - smem)
    many = isinstance(out, list)
    one = pl.BlockSpec(memory_space=pltpu.VMEM)
    return pl.pallas_call(
        kernel,
        out_shape=out,
        in_specs=specs,
        out_specs=[one] * len(out) if many else one,
        scratch_shapes=list(scratch),
        compiler_params=pltpu.CompilerParams(vmem_limit_bytes=32 * 2**20),
        cost_estimate=cost,
    )(*args)


def shape(*dims, dtype=BF):
    return jax.ShapeDtypeStruct(dims, dtype)


def exchange(values, axes):
    return lax.all_to_all(values, axes, 0, 0, tiled=True)


def local(
    tokens,
    visible_lists,
    visible_counts,
    w_in,
    w_out,
    w_embed,
    mask_token,
    positions,
    w_qkv,
    w_attn_out,
):
    vols, tubs, part = tokens.shape
    rows = vols * tubs
    nmp = lax.axis_size(MP)
    nz = lax.axis_size(COLUMN)
    ngroup = lax.axis_size(GROUP)
    dec = w_embed.shape[1]
    feats = dec // nmp
    lists = visible_lists.reshape(1, -1)
    counts = visible_counts.reshape(1, -1)
    slots = lists.shape[1]
    token_row = mask_token.reshape(1, dec)

    own = call(pick_kernel, shape(nmp, 80, 128), lists, counts, tokens.reshape(rows, part))
    full = exchange(own, MP)

    w_q, w_k, w_v = (w_qkv[:, i].reshape(dec, 2, HDIM) for i in range(3))
    w_all = jnp.concatenate(
        [
            jnp.tile(w_q[:, :, None, :], (1, 1, vols, 1)).reshape(dec, 2 * vols * HDIM),
            jnp.concatenate([w_k, w_v], axis=2).reshape(dec, 4 * HDIM),
        ],
        axis=1,
    )
    masked = call(masked_kernel, shape(tubs, 384), token_row, positions, w_all)

    terms = exchange(call(feed_kernel, shape(nmp, 80, 128), full, w_in, w_out), MP)
    embed_parts = exchange(call(embed_kernel, shape(nmp, slots, dec), terms, own, w_embed), MP)
    slot_in, queries, kv = call(
        project_kernel,
        [shape(slots, dec), shape(ngroup, tubs, 128), shape(nz, 80, 128)],
        embed_parts, lists, counts, positions, masked, w_all,
    )
    queries = exchange(queries, GROUP)
    column = exchange(kv, COLUMN)
    start = (lax.axis_index(MP) * feats).reshape(1).astype(I32)
    dec_own = call(
        own_kernel, shape(feats, rows), start, lists, counts, token_row, positions, slot_in, smem=1
    )
    message = call(
        attend_kernel,
        shape(ngroup, 80, 128),
        queries,
        column,
        scratch=[pltpu.VMEM((vols, nz * tubs, 64), BF), pltpu.VMEM((ngroup, 80, 128), F32)],
    )
    message = exchange(message, GROUP)
    head_terms = call(combine_kernel, shape(nmp, feats, rows), message, w_attn_out)
    head_terms = exchange(head_terms, MP)
    return call(finish_kernel, shape(vols, tubs, feats), head_terms, dec_own)


def solution(mesh):
    fine = Mesh(mesh.devices.reshape(8, 2, 4, 4, 2), ("zz", "zp", "y", "x", "core"))
    seq = ("zz", "zp", "y")
    in_specs = (
        P(None, seq, MP),
        P(seq, None, None),
        P(seq, None),
        P(None, MP),
        P(MP, None),
        P(MP, None),
        P(),
        P(seq, None),
        P(None, None, MP),
        P(MP, None),
    )
    out_specs = P(None, seq, MP)
    return jax.shard_map(local, mesh=fine, in_specs=in_specs, out_specs=out_specs, check_vma=False)
```

time: 164 us -> 120 us (0.73)
  blocking collectives: 9.08 us -> 62.9 us
  starting transfers between devices: 51.9 us -> 16.7 us
  waiting for transfers between devices: 38.4 us -> 20.5 us
  local copies, waits for them, and re-layouts: 22.5 us -> 5.39 us
  matrix products: 14.6 us -> 0 us
  between operations: 13.9 us -> 0.12 us
  Pallas kernels: 0 us -> 13.3 us
  other arithmetic: 12.3 us -> 0.05 us
    all_to_all x1 -> x4, blocking collectives: 9.08 us -> 62.9 us  [exchange(): return lax.all_to_all(values, axes, 0, 0, tiled=True)]
    all_to_all x6 -> x3, starting transfers between devices: 51.9 us -> 16.7 us  [exchange(): return lax.all_to_all(values, axes, 0, 0, tiled=True)]
    dot_general x12 -> x0, matrix products: 14.6 us -> none  [the longest x9 5.64 us: dot(): return jnp.dot(a, b, preferred_element_type=F32)]
    pallas_call x0 -> x9, Pallas kernels: none -> 13.3 us  [call(): pl.pallas_call(kernel, out_shape=out, in_specs=specs, out_specs=[one] * l...]
    all_to_all x6 -> x3, waiting for transfers between devices: 32.7 us -> 20.5 us  [exchange(): return lax.all_to_all(values, axes, 0, 0, tiled=True)]
    reduce_sum x14 -> x0, other arithmetic: 9.39 us -> none  [the longest x1 4.72 us: local(): totals = jnp.sum(weights, axis=-1)]
    reshape x10 -> x2, local copies, waits for them, and re-layouts: 6.61 us -> 0.12 us  [the longest x1 0.12 us: local(): jnp.concatenate([w_k, w_v], axis=2).reshape(dec, 4 * HDIM)]
    transpose x4 -> x0, local copies, waits for them, and re-layouts: 6.44 us -> none  [the longest x2 4.33 us: local(): kv[:, :, :, 0].transpose(1, 3, 0, 2, 4)]
  transfers between devices with their start and end apart: 7 -> 3, of which waited for: 7 -> 3; matrix products, arithmetic and copies ran while one was open for 10% -> 0% of each run, Pallas kernels for 0% -> 1%
where the time goes in v2:
time: 120 us; the launch traced here: 119 us
  blocking collectives  62.9 us (52%)
  waiting for transfers between devices  20.5 us (17%)
  starting transfers between devices  16.7 us (14%)
  Pallas kernels  13.3 us (11%)
  local copies, waits for them, and re-layouts  5.39 us (4%)
    all_to_all x4, blocking collectives, exchange(): return lax.all_to_all(values, axes, 0, 0, tiled=True)  62.9 us
    all_to_all x3, waiting for transfers between devices, exchange(): return lax.all_to_all(values, axes, 0, 0, tiled=True)  20.5 us
    all_to_all x3, starting transfers between devices, exchange(): return lax.all_to_all(values, axes, 0, 0, tiled=True)  16.7 us
    pallas_call x9, Pallas kernels, call(): pl.pallas_call(kernel, out_shape=out, in_specs=specs, out_specs=[one] * l...  13.3 us
    unnamed x24, local copies, waits for them, and re-layouts  5.1 us
  transfers between devices with their start and end apart: 3, of which 3 were waited for; matrix products, arithmetic and copies ran while one was open for 0% of the time, Pallas kernels for 1%

profile of v2, /device:TPU:1, one launch (start us, length us, event | category | flops | bytes accessed | tf_op | source)
XLA Modules:
  0.0 119.0 jit_solution(10112067808347073854)
XLA Ops:
  0.0 0.0 copy-start.4
  0.0 0.9 copy-done.4
  0.9 0.0 copy-start.6
  0.9 0.7 copy-done.6
  1.6 0.0 copy-start.8
  1.6 0.7 copy-done.8
  2.2 0.3 shard_map.100.own
  2.5 14.8 %all_to_all.35.gathered = bf16[8,80,128]{2,1,0:T(8,128)(2,1)S(1)} all-to-all(bf16[8,80,128]{2,1,0:T(8,128)(2,1)S(1)} %shard_map.100.own), channel_id=1, replica_groups=mesh['zz'=8,'zp'=2,'y'=4,'x'=4,'core'=2] {'x','core'}, dimensions={0} | all-to-all | bytes 327680 | tf_op jit(solution)/shard_map/all_to_all | solution.py:264
  17.3 0.0 copy-start
  17.3 1.4 %copy-done = bf16[1280,640]{1,0:T(8,128)(2,1)S(1)} copy-done((bf16[1280,640]{1,0:T(8,128)(2,1)S(1)}, bf16[1280,640]{1,0:T(8,128)(2,1)}, u32[]{:S(2)}) %copy-start) | copy-done | bytes 1638424
  18.8 0.0 copy-start.1
  18.8 1.4 %copy-done.1 = bf16[640,1280]{1,0:T(8,128)(2,1)S(1)} copy-done((bf16[640,1280]{1,0:T(8,128)(2,1)S(1)}, bf16[640,1280]{1,0:T(8,128)(2,1)}, u32[]{:S(2)}) %copy-start.1) | copy-done | bytes 1638424
  20.2 0.0 copy-start.11
  20.2 0.0 copy-start.3
  20.2 2.1 %shard_map.101 = bf16[8,80,128]{2,1,0:T(8,128)(2,1)} custom-call(bf16[8,80,128]{2,1,0:T(8,128)(2,1)S(1)} %all_to_all.35.gathered, bf16[1280,640]{1,0:T(8,128)(2,1)S(1)} %copy-done, bf16[640,1280]{1,0:T(8,128)(2,1)S(1)} %copy-done.1), custom_call_target="tpu_custom_call" | custom-call | tf_op jit(solution)/shard_map/pallas_call | solution.py:248
  22.3 0.0 copy-start.10
  22.3 4.3 %all-to-all-start.1 = ((bf16[8,80,128]{2,1,0:T(8,128)(2,1)}), bf16[8,80,128]{2,1,0:T(8,128)(2,1)S(1)}, u32[]{:S(2)}, u32[]{:S(2)}) async-start(bf16[8,80,128]{2,1,0:T(8,128)(2,1)} %shard_map.101), calls=%async_computation.1 | async-start | bytes 327680 | tf_op jit(solution)/shard_map/all_to_all | solution.py:264
  26.6 0.0 copy-done.11
  26.6 5.6 %all-to-all-done.1.terms = bf16[8,80,128]{2,1,0:T(8,128)(2,1)S(1)} async-done(((bf16[8,80,128]{2,1,0:T(8,128)(2,1)}), bf16[8,80,128]{2,1,0:T(8,128)(2,1)S(1)}, u32[]{:S(2)}, u32[]{:S(2)}) %all-to-all-start.1) | async-done | bytes 163872 | tf_op jit(solution)/shard_map/all_to_all | solution.py:264
  32.2 0.0 copy-done.3
  32.2 1.0 shard_map.102
  33.2 0.0 copy-start.2
  33.2 4.4 %all-to-all-start.2 = ((bf16[8,64,512]{2,1,0:T(8,128)(2,1)}), bf16[8,64,512]{2,1,0:T(8,128)(2,1)S(1)}, u32[]{:S(2)}, u32[]{:S(2)}) async-start(bf16[8,64,512]{2,1,0:T(8,128)(2,1)} %shard_map.102), calls=%async_computation.2 | async-start | bytes 1048576 | tf_op jit(solution)/shard_map/all_to_all | solution.py:264
  37.6 0.0 copy-done.10
  37.7 0.0 copy-start.7
  37.7 0.0 copy-start.9
  37.7 0.1 copy.15
  37.9 0.1 copy.14
  38.0 0.0 copy-done.2
  38.1 0.0 copy-start.5
  38.1 0.3 shard_map.103.masked
  38.4 8.7 %all-to-all-done.2.parts = bf16[8,64,512]{2,1,0:T(8,128)(2,1)S(1)} async-done(((bf16[8,64,512]{2,1,0:T(8,128)(2,1)}), bf16[8,64,512]{2,1,0:T(8,128)(2,1)S(1)}, u32[]{:S(2)}, u32[]{:S(2)}) %all-to-all-start.2) | async-done | bytes 524320 | tf_op jit(solution)/shard_map/all_to_all | solution.py:264
  47.1 0.0 copy-done.7
  47.2 0.0 copy-done.9
  47.2 0.7 shard_map.104
  47.9 7.9 %all_to_all.36.queries = bf16[8,64,128]{2,1,0:T(8,128)(2,1)S(1)} all-to-all(bf16[8,64,128]{2,1,0:T(8,128)(2,1)S(1)} %get-tuple-element.8), channel_id=1, replica_groups=mesh['zz'=8,'zp'=2,'y'=4,'x'=4,'core'=2] {'zp','y'}, dimensions={0} | all-to-all | bytes 262144 | tf_op jit(solution)/shard_map/all_to_all | solution.py:264
  55.7 26.6 %all_to_all.37.column = bf16[16,80,128]{2,1,0:T(8,128)(2,1)S(1)} all-to-all(bf16[16,80,128]{2,1,0:T(8,128)(2,1)S(1)} %get-tuple-element.9), channel_id=1, replica_groups=mesh['zz'=8,'zp'=2,'y'=4,'x'=4,'core'=2] {'zz','zp'}, dimensions={0} | all-to-all | bytes 655360 | tf_op jit(solution)/shard_map/all_to_all | solution.py:264
  82.3 6.8 %shard_map.105 = bf16[8,80,128]{2,1,0:T(8,128)(2,1)S(1)} custom-call(bf16[8,64,128]{2,1,0:T(8,128)(2,1)S(1)} %all_to_all.36.queries, bf16[16,80,128]{2,1,0:T(8,128)(2,1)S(1)} %all_to_all.37.column), custom_call_target="tpu_custom_call" | custom-call | tf_op jit(solution)/shard_map/pallas_call | solution.py:248
  89.1 13.6 %all_to_all.38.message = bf16[8,80,128]{2,1,0:T(8,128)(2,1)S(1)} all-to-all(bf16[8,80,128]{2,1,0:T(8,128)(2,1)S(1)} %shard_map.105), channel_id=1, replica_groups=mesh['zz'=8,'zp'=2,'y'=4,'x'=4,'core'=2] {'zp','y'}, dimensions={0} | all-to-all | bytes 327680 | tf_op jit(solution)/shard_map/all_to_all | solution.py:264
  102.7 0.0 copy-done.5
  102.8 1.0 shard_map.106
  103.7 8.0 %all-to-all-start.6 = ((bf16[8,64,256]{2,1,0:T(8,128)(2,1)}), bf16[8,64,256]{2,1,0:T(8,128)(2,1)S(1)}, u32[]{:S(2)}, u32[]{:S(2)}) async-start(bf16[8,64,256]{2,1,0:T(8,128)(2,1)} %shard_map.106), calls=%async_computation.6 | async-start | bytes 524288 | tf_op jit(solution)/shard_map/all_to_all | solution.py:264
  111.7 0.4 shard_map.107.dec_own
  112.1 6.1 %all-to-all-done.6.terms = bf16[8,64,256]{2,1,0:T(8,128)(2,1)S(1)} async-done(((bf16[8,64,256]{2,1,0:T(8,128)(2,1)}), bf16[8,64,256]{2,1,0:T(8,128)(2,1)S(1)}, u32[]{:S(2)}, u32[]{:S(2)}) %all-to-all-start.6) | async-done | bytes 262176 | tf_op jit(solution)/shard_map/all_to_all | solution.py:264
  118.2 0.8 shard_map.108
  (5 shorter events, 0.1 us)
Async XLA Ops:
  0.0 0.9 copy-start.4
  0.9 0.7 copy-start.6
  1.6 0.7 copy-start.8
  17.3 1.4 %copy-start = (bf16[1280,640]{1,0:T(8,128)(2,1)S(1)}, bf16[1280,640]{1,0:T(8,128)(2,1)}, u32[]{:S(2)}) copy-start(bf16[1280,640]{1,0:T(8,128)(2,1)} %w_in.1) | copy-start | bytes 4915204
  18.8 1.4 %copy-start.1 = (bf16[640,1280]{1,0:T(8,128)(2,1)S(1)}, bf16[640,1280]{1,0:T(8,128)(2,1)}, u32[]{:S(2)}) copy-start(bf16[640,1280]{1,0:T(8,128)(2,1)} %w_out.1) | copy-start | bytes 4915204
  20.2 6.4 %copy-start.11 = (bf16[512]{0:T(512)(128)(2,1)S(1)}, bf16[512]{0:T(512)(128)(2,1)}, u32[]{:S(2)}) copy-start(bf16[512]{0:T(512)(128)(2,1)} %param.16) | copy-start | bytes 3076
  20.2 12.0 %copy-start.3 = (bf16[160,512]{1,0:T(8,128)(2,1)S(1)}, bf16[160,512]{1,0:T(8,128)(2,1)}, u32[]{:S(2)}) copy-start(bf16[160,512]{1,0:T(8,128)(2,1)} %w_embed.1) | copy-start | bytes 491524
  22.3 15.4 %copy-start.10 = (bf16[512,3,64]{0,2,1:T(8,128)(2,1)S(1)}, bf16[512,3,64]{0,2,1:T(8,128)(2,1)}, u32[]{:S(2)}) copy-start(bf16[512,3,64]{0,2,1:T(8,128)(2,1)} %param.18) | copy-start | bytes 589828
  22.3 9.9 %all-to-all-start.1 = ((bf16[8,80,128]{2,1,0:T(8,128)(2,1)}), bf16[8,80,128]{2,1,0:T(8,128)(2,1)S(1)}, u32[]{:S(2)}, u32[]{:S(2)}) async-start(bf16[8,80,128]{2,1,0:T(8,128)(2,1)} %shard_map.101), calls=%async_computation.1 | async-start | bytes 327680 | tf_op jit(solution)/shard_map/all_to_all | solution.py:264
  33.2 4.8 %copy-start.2 = (bf16[64,512]{1,0:T(8,128)(2,1)S(1)}, bf16[64,512]{1,0:T(8,128)(2,1)}, u32[]{:S(2)}) copy-start(bf16[64,512]{1,0:T(8,128)(2,1)} %positions.5) | copy-start | bytes 196612
  33.2 13.9 %all-to-all-start.2 = ((bf16[8,64,512]{2,1,0:T(8,128)(2,1)}), bf16[8,64,512]{2,1,0:T(8,128)(2,1)S(1)}, u32[]{:S(2)}, u32[]{:S(2)}) async-start(bf16[8,64,512]{2,1,0:T(8,128)(2,1)} %shard_map.102), calls=%async_computation.2 | async-start | bytes 1048576 | tf_op jit(solution)/shard_map/all_to_all | solution.py:264
  37.7 9.5 %copy-start.7 = (s32[1,64,1]{1,2,0:T(1,128)S(1)}, s32[1,64,1]{1,2,0:T(1,128)}, u32[]{:S(2)}) copy-start(s32[1,64,1]{1,2,0:T(1,128)} %param.11) | copy-start | bytes 772
  37.7 9.5 %copy-start.9 = (s32[1,64]{1,0:T(1,128)S(1)}, s32[1,64]{1,0:T(1,128)}, u32[]{:S(2)}) copy-start(s32[1,64]{1,0:T(1,128)} %counts.5) | copy-start | bytes 772
  38.1 64.7 %copy-start.5 = (bf16[64,512]{1,0:T(8,128)(2,1)S(1)}, bf16[64,512]{1,0:T(8,128)(2,1)}, u32[]{:S(2)}) copy-start(bf16[64,512]{1,0:T(8,128)(2,1)} %w_attn_out.1) | copy-start | bytes 196612
  103.7 14.5 %all-to-all-start.6 = ((bf16[8,64,256]{2,1,0:T(8,128)(2,1)}), bf16[8,64,256]{2,1,0:T(8,128)(2,1)S(1)}, u32[]{:S(2)}, u32[]{:S(2)}) async-start(bf16[8,64,256]{2,1,0:T(8,128)(2,1)} %shard_map.106), calls=%async_computation.6 | async-start | bytes 524288 | tf_op jit(solution)/shard_map/all_to_all | solution.py:264

commit v3 on v2

--- a/solution.py
+++ b/solution.py
@@ -62,16 +62,30 @@
     return jnp.concatenate([folded[:64], tail], axis=1)
 
 
-def pick_kernel(lists, counts, tokens, out):
+def pick_kernel(lists_hbm, tokens_hbm, out, lists, tokens, sems):
+    copies = [
+        pltpu.make_async_copy(lists_hbm, lists, sems.at[0]),
+        pltpu.make_async_copy(tokens_hbm, tokens, sems.at[1]),
+    ]
+    for copy in copies:
+        copy.start()
     rows = tokens.shape[0]
+    copies[0].wait()
     ids = column_of(lists[...])
     named = (ids == iota((ids.shape[0], rows), 1)).astype(F32).astype(BF)
+    copies[1].wait()
     own = fold_tail(dot(named, tokens[...])).astype(BF)
     for k in range(out.shape[0]):
         out[k] = own
 
 
-def feed_kernel(gathered, w_in, w_out, out):
+def feed_kernel(gathered, w_in_hbm, w_out_hbm, out, w_in, w_out, sems):
+    copies = [
+        pltpu.make_async_copy(w_in_hbm, w_in, sems.at[0]),
+        pltpu.make_async_copy(w_out_hbm, w_out, sems.at[1]),
+    ]
+    for copy in copies:
+        copy.start()
     count = gathered.shape[0]
     part = w_in.shape[0] // count
     blocks = [unfold_tail(gathered[k].astype(F32)) for k in range(count)]
@@ -80,11 +94,14 @@
     blocks = [b - mean_row for b in blocks]
     spread = sum(jnp.sum(b * b, axis=1, keepdims=True) for b in blocks) * (1.0 / width)
     scale = lax.rsqrt(spread + 1e-05)
+    blocks = [(b * scale).astype(BF) for b in blocks]
+    copies[0].wait()
     hidden = None
     for k in range(count):
-        term = dot((blocks[k] * scale).astype(BF), w_in[k * part : (k + 1) * part, :])
+        term = dot(blocks[k], w_in[k * part : (k + 1) * part, :])
         hidden = term if hidden is None else hidden + term
     act = (0.5 * hidden * (1.0 + lax.erf(hidden * math.sqrt(0.5)))).astype(BF)
+    copies[1].wait()
     terms = dot(act, w_out[...])
     for k in range(count):
         out[k] = fold_tail(terms[:, k * part : (k + 1) * part]).astype(BF)
@@ -98,60 +115,67 @@
         out[k] = value
 
 
-def masked_kernel(mask_token, positions, w_all, out):
-    mask_in = (mask_token[...].astype(F32) + positions[...].astype(F32)).astype(BF)
-    out[...] = dot(norm_rows(mask_in.astype(F32)).astype(BF), w_all[...]).astype(BF)
-
-
-def project_kernel(parts, lists, counts, positions, masked, w_all, slot_in, q_out, kv_out):
+def project_kernel(parts, lists, counts, mask_token, positions, w_rows, slot_in, out):
     tubs = positions.shape[0]
     slots = lists.shape[1]
     ids_row = live_row(lists[...], counts[...], 4 * tubs)
     ids = column_of(ids_row)
     embedded = sum(parts[k].astype(F32) for k in range(parts.shape[0])).astype(BF).astype(F32)
     at = (ids % tubs == iota((slots, tubs), 1)).astype(F32).astype(BF)
-    row_in = (embedded + dot(at, positions[...])).astype(BF)
+    pos = positions[...]
+    row_in = (embedded + dot(at, pos)).astype(BF)
     slot_in[...] = row_in
-    proj = dot(norm_rows(row_in.astype(F32)).astype(BF), w_all[...]).astype(BF)
+    mask_in = (mask_token[...].astype(F32) + pos.astype(F32)).astype(BF)
+    both = jnp.concatenate([mask_in, row_in], axis=0).astype(F32)
+    w_q, w_k, w_v = w_rows[0], w_rows[1], w_rows[2]
+    heads = [slice(0, HDIM), slice(HDIM, 2 * HDIM)]
+    w_all = [w_q[h] for h in heads for _ in range(4)]
+    w_all += [w[h] for h in heads for w in (w_k, w_v)]
+    w_all = jnp.concatenate(w_all, axis=0)
+    both = dot_nt(norm_rows(both).astype(BF), w_all).astype(BF)
+    masked, proj = both[:tubs], both[tubs:]
 
     spot = (ids_row % tubs == iota((tubs, slots), 0)).astype(F32).astype(BF)
     of_volume = ids // tubs == iota((slots, 128), 1) // HDIM
     seen = dot(spot, of_volume.astype(F32).astype(BF)) > 0
     zero = jnp.zeros((slots, 128), BF)
-    extra = jnp.concatenate(
-        [
-            jnp.concatenate([ids_row.astype(F32), jnp.zeros((1, 128 - slots), F32)], axis=1),
-            jnp.zeros((15, 128), F32),
-        ],
-        axis=0,
-    ).astype(BF)
+    extra = jnp.concatenate([ids_row.astype(F32), jnp.zeros((1, 128 - slots), F32)], axis=1)
+    extra = jnp.broadcast_to(extra, (16, 128)).astype(BF)
     for head in range(2):
         cols = slice(128 * head, 128 * head + 128)
         placed = dot(spot, jnp.where(of_volume, proj[:, cols], zero))
         query = jnp.where(seen, placed, masked[:, cols].astype(F32)).astype(BF)
-        for k in range(4):
-            q_out[4 * head + k] = query
         cols = slice(256 + 64 * head, 256 + 64 * head + 64)
         block = jnp.concatenate([masked[:, cols], proj[:, cols]], axis=1)
-        block = jnp.concatenate([block, extra], axis=0)
-        for k in range(8):
-            kv_out[2 * k + head] = block
-
-
-def own_kernel(start, lists, counts, mask_token, positions, slot_in, out):
-    tubs = positions.shape[0]
-    feats, rows = out.shape
+        for k in range(4):
+            out[4 * head + k, :tubs] = query
+            out[4 * head + k, tubs : 2 * tubs] = block
+            out[4 * head + k, 2 * tubs :] = extra
+
+
+def pair_kernel(start, group, out):
+    y = start[0]
+    first, second = group.at[y], group.at[4 + y]
+    odd = iota((16, 128), 0) % 2 == 1
+    ids = jnp.where(odd, second[128:, :].astype(F32), first[128:, :].astype(F32)).astype(BF)
+    for k in range(out.shape[0]):
+        out[k, :64] = first[64:128, :]
+        out[k, 64:128] = second[64:128, :]
+        out[k, 128:] = ids
+
+
+def own_rows(start, lists, counts, mask_token, positions, slot_in, feats, rows):
+    tubs, dec = positions.shape
     slots = lists.shape[1]
-    dec = positions.shape[1]
     ids = column_of(live_row(lists[...], counts[...], rows))
-    choose = (iota((dec, feats), 0) == iota((dec, feats), 1) + start[0]).astype(F32).astype(BF)
+    choose = (iota((dec, feats), 0) == iota((dec, feats), 1) + start).astype(F32).astype(BF)
     mask_in = (mask_token[...].astype(F32) + positions[...].astype(F32)).astype(BF)
     mask_own = dot(mask_in, choose).astype(BF)
     slot_own = dot(slot_in[...], choose).astype(BF)
     picked = (ids == iota((slots, rows), 1)).astype(F32)
     seen = jnp.sum(picked, axis=0, keepdims=True) > 0
     tile = (iota((tubs, rows), 0) == iota((tubs, rows), 1) % tubs).astype(F32).astype(BF)
-    out[...] = jnp.where(seen, dot_tn(slot_own, picked.astype(BF)), dot_tn(mask_own, tile)).astype(BF)
+    return jnp.where(seen, dot_tn(slot_own, picked.astype(BF)), dot_tn(mask_own, tile))
 
 
 def split_pieces(values, count):
@@ -164,15 +188,16 @@
 
 
 def attend_kernel(queries, column, out, kv_scr, msg_scr):
-    blocks, tubs = queries.shape[0], queries.shape[1]
-    nz = column.shape[0]
+    blocks, tubs = queries.shape[0], 64
+    nz = 2 * column.shape[0]
     vols = 4
     rows = vols * tubs
     slots = 64
     keys = nz * tubs
     for k in range(nz):
-        block = column[k, :tubs, :]
-        ids_row = column[k, tubs : tubs + 16, :][0:1, :slots].astype(F32)
+        side = k % 2
+        block = column[k // 2, side * tubs : (side + 1) * tubs, :]
+        ids_row = column[k // 2, 2 * tubs :, :].astype(F32)[side : side + 1, :slots]
         picked = (ids_row == iota((rows, slots), 0).astype(F32)).astype(F32)
         seen = jnp.sum(picked, axis=1, keepdims=True) > 0
         placed = dot(picked.astype(BF), block[:, 64:])
@@ -181,7 +206,7 @@
         mat = jnp.where(seen, placed, other).astype(BF)
         for v in range(vols):
             kv_scr[v, k * tubs : (k + 1) * tubs, :] = mat[v * tubs : (v + 1) * tubs]
-    packed = queries[...].reshape(blocks * tubs, 128)
+    packed = queries[:, :tubs, :].reshape(blocks * tubs, 128)
     scale = math.log2(math.e) / math.sqrt(HDIM)
     chunk = 256
     per = chunk // tubs
@@ -234,15 +259,17 @@
         out[k] = terms[k * feats : (k + 1) * feats]
 
 
-def finish_kernel(terms, dec_own, out):
-    total = dec_own[...].astype(F32) + sum(terms[k].astype(F32) for k in range(terms.shape[0]))
+def finish_kernel(start, terms, lists, counts, mask_token, positions, slot_in, out):
     vols, tubs, feats = out.shape
+    total = own_rows(start[0], lists, counts, mask_token, positions, slot_in, feats, vols * tubs)
+    total = total + sum(terms[k].astype(F32) for k in range(terms.shape[0]))
     out[...] = total.T.astype(BF).reshape(vols, tubs, feats)
 
 
-def call(kernel, out, *args, scratch=(), smem=0, cost=None):
+def call(kernel, out, *args, scratch=(), smem=0, hbm=0):
     specs = [pl.BlockSpec(memory_space=pltpu.SMEM)] * smem
-    specs += [pl.BlockSpec(memory_space=pltpu.VMEM)] * (len(args) - smem)
+    specs += [pl.BlockSpec(memory_space=pltpu.VMEM)] * (len(args) - smem - hbm)
+    specs += [pl.BlockSpec(memory_space=pltpu.HBM)] * hbm
     many = isinstance(out, list)
     one = pl.BlockSpec(memory_space=pltpu.VMEM)
     return pl.pallas_call(
@@ -252,7 +279,6 @@
         out_specs=[one] * len(out) if many else one,
         scratch_shapes=list(scratch),
         compiler_params=pltpu.CompilerParams(vmem_limit_bytes=32 * 2**20),
-        cost_estimate=cost,
     )(*args)
 
 
@@ -287,44 +313,55 @@
     counts = visible_counts.reshape(1, -1)
     slots = lists.shape[1]
     token_row = mask_token.reshape(1, dec)
-
-    own = call(pick_kernel, shape(nmp, 80, 128), lists, counts, tokens.reshape(rows, part))
+    w_rows = w_qkv.transpose(1, 2, 0)
+    pair = pltpu.SemaphoreType.DMA((2,))
+
+    own = call(
+        pick_kernel,
+        shape(nmp, 80, 128),
+        lists,
+        tokens.reshape(rows, part),
+        hbm=2,
+        scratch=[pltpu.VMEM((1, slots), I32), pltpu.VMEM((rows, part), BF), pair],
+    )
     full = exchange(own, MP)
-
-    w_q, w_k, w_v = (w_qkv[:, i].reshape(dec, 2, HDIM) for i in range(3))
-    w_all = jnp.concatenate(
-        [
-            jnp.tile(w_q[:, :, None, :], (1, 1, vols, 1)).reshape(dec, 2 * vols * HDIM),
-            jnp.concatenate([w_k, w_v], axis=2).reshape(dec, 4 * HDIM),
-        ],
-        axis=1,
-    )
-    masked = call(masked_kernel, shape(tubs, 384), token_row, positions, w_all)
-
-    terms = exchange(call(feed_kernel, shape(nmp, 80, 128), full, w_in, w_out), MP)
+    terms = call(
+        feed_kernel,
+        shape(nmp, 80, 128),
+        full,
+        w_in,
+        w_out,
+        hbm=2,
+        scratch=[pltpu.VMEM(w_in.shape, BF), pltpu.VMEM(w_out.shape, BF), pair],
+    )
+    terms = exchange(terms, MP)
     embed_parts = exchange(call(embed_kernel, shape(nmp, slots, dec), terms, own, w_embed), MP)
-    slot_in, queries, kv = call(
+    slot_in, group = call(
         project_kernel,
-        [shape(slots, dec), shape(ngroup, tubs, 128), shape(nz, 80, 128)],
-        embed_parts, lists, counts, positions, masked, w_all,
-    )
-    queries = exchange(queries, GROUP)
-    column = exchange(kv, COLUMN)
-    start = (lax.axis_index(MP) * feats).reshape(1).astype(I32)
-    dec_own = call(
-        own_kernel, shape(feats, rows), start, lists, counts, token_row, positions, slot_in, smem=1
-    )
+        [shape(slots, dec), shape(ngroup, 144, 128)],
+        embed_parts, lists, counts, token_row, positions, w_rows,
+    )
+    group = exchange(group, GROUP)
+    y_index = lax.axis_index("y").reshape(1).astype(I32)
+    column = call(pair_kernel, shape(lax.axis_size("zz"), 144, 128), y_index, group, smem=1)
+    column = exchange(column, "zz")
     message = call(
         attend_kernel,
         shape(ngroup, 80, 128),
-        queries,
+        group,
         column,
         scratch=[pltpu.VMEM((vols, nz * tubs, 64), BF), pltpu.VMEM((ngroup, 80, 128), F32)],
     )
     message = exchange(message, GROUP)
     head_terms = call(combine_kernel, shape(nmp, feats, rows), message, w_attn_out)
     head_terms = exchange(head_terms, MP)
-    return call(finish_kernel, shape(vols, tubs, feats), head_terms, dec_own)
+    start = (lax.axis_index(MP) * feats).reshape(1).astype(I32)
+    return call(
+        finish_kernel,
+        shape(vols, tubs, feats),
+        start, head_terms, lists, counts, token_row, positions, slot_in,
+        smem=1,
+    )
 
 
 def solution(mesh):

time: 120 us -> 122 us (1.017)
  waiting for transfers between devices: 20.5 us -> 22.2 us
    all_to_all x3, waiting for transfers between devices: 20.5 us -> 22.2 us  [exchange(): return lax.all_to_all(values, axes, 0, 0, tiled=True)]
    unnamed x24 -> x22, local copies, waits for them, and re-layouts: 5.1 us -> 4.46 us
    pallas_call x9 -> x8, Pallas kernels: 13.3 us -> 13.8 us  [call(): pl.pallas_call(kernel, out_shape=out, in_specs=specs, out_specs=[one] * l...]
  transfers between devices with their start and end apart: 3 -> 3, of which waited for: 3 -> 3; matrix products, arithmetic and copies ran while one was open for 0% -> 0% of each run, Pallas kernels for 1% -> 0%
where the time goes in v3:
time: 122 us; the launch traced here: 121 us
  blocking collectives  63.4 us (52%)
  waiting for transfers between devices  22.2 us (18%)
  starting transfers between devices  17.3 us (14%)
  Pallas kernels  13.8 us (11%)
  local copies, waits for them, and re-layouts  4.46 us (4%)
    all_to_all x4, blocking collectives, exchange(): return lax.all_to_all(values, axes, 0, 0, tiled=True)  63.4 us
    all_to_all x3, waiting for transfers between devices, exchange(): return lax.all_to_all(values, axes, 0, 0, tiled=True)  22.2 us
    all_to_all x3, starting transfers between devices, exchange(): return lax.all_to_all(values, axes, 0, 0, tiled=True)  17.3 us
    pallas_call x8, Pallas kernels, call(): pl.pallas_call(kernel, out_shape=out, in_specs=specs, out_specs=[one] * l...  13.8 us
    unnamed x22, local copies, waits for them, and re-layouts  4.46 us
  transfers between devices with their start and end apart: 3, of which 3 were waited for; matrix products, arithmetic and copies ran while one was open for 0% of the time, Pallas kernels for 0%

profile of v3, /device:TPU:1, one launch (start us, length us, event | category | flops | bytes accessed | tf_op | source)
XLA Modules:
  0.0 121.3 jit_solution(1136889552989377972)
XLA Ops:
  0.0 0.0 copy-start.5
  0.0 0.9 copy-done.5
  0.9 0.0 copy-start.7
  0.9 0.7 copy-done.7
  1.6 0.5 shard_map.100.own
  2.1 14.8 %all_to_all.35.gathered = bf16[8,80,128]{2,1,0:T(8,128)(2,1)S(1)} all-to-all(bf16[8,80,128]{2,1,0:T(8,128)(2,1)S(1)} %shard_map.100.own), channel_id=1, replica_groups=mesh['zz'=8,'zp'=2,'y'=4,'x'=4,'core'=2] {'x','core'}, dimensions={0} | all-to-all | bytes 327680 | tf_op jit(solution)/shard_map/all_to_all | solution.py:290
  16.9 0.0 copy-start
  16.9 1.4 %copy-done = bf16[1280,640]{1,0:T(8,128)(2,1)S(1)} copy-done((bf16[1280,640]{1,0:T(8,128)(2,1)S(1)}, bf16[1280,640]{1,0:T(8,128)(2,1)}, u32[]{:S(2)}) %copy-start) | copy-done | bytes 1638424
  18.3 0.0 copy-start.1
  18.3 1.4 %copy-done.1 = bf16[640,1280]{1,0:T(8,128)(2,1)S(1)} copy-done((bf16[640,1280]{1,0:T(8,128)(2,1)S(1)}, bf16[640,1280]{1,0:T(8,128)(2,1)}, u32[]{:S(2)}) %copy-start.1) | copy-done | bytes 1638424
  19.8 0.0 copy-start.4
  19.8 2.0 %shard_map.101 = bf16[8,80,128]{2,1,0:T(8,128)(2,1)S(1)} custom-call(bf16[8,80,128]{2,1,0:T(8,128)(2,1)S(1)} %all_to_all.35.gathered, bf16[1280,640]{1,0:T(8,128)(2,1)S(1)} %copy-done, bf16[640,1280]{1,0:T(8,128)(2,1)S(1)} %copy-done.1), custom_call_target="tpu_custom_call" | custom-call | tf_op jit(solution)/shard_map/pallas_call | solution.py:275
  21.7 0.0 copy-start.10
  21.8 0.0 copy-start.2
  21.8 0.0 copy-start.3
  21.8 0.0 copy-start.8
  21.8 0.0 copy-start.9
  21.8 9.0 %all_to_all.36.terms = bf16[8,80,128]{2,1,0:T(8,128)(2,1)S(1)} all-to-all(bf16[8,80,128]{2,1,0:T(8,128)(2,1)S(1)} %shard_map.101), channel_id=1, replica_groups=mesh['zz'=8,'zp'=2,'y'=4,'x'=4,'core'=2] {'x','core'}, dimensions={0} | all-to-all | bytes 327680 | tf_op jit(solution)/shard_map/all_to_all | solution.py:290
  30.8 0.0 copy-done.4
  30.8 1.0 shard_map.102
  31.8 4.3 %all-to-all-start.2 = ((bf16[8,64,512]{2,1,0:T(8,128)(2,1)}), bf16[8,64,512]{2,1,0:T(8,128)(2,1)S(1)}, u32[]{:S(2)}, u32[]{:S(2)}) async-start(bf16[8,64,512]{2,1,0:T(8,128)(2,1)} %shard_map.102), calls=%async_computation.2 | async-start | bytes 1048576 | tf_op jit(solution)/shard_map/all_to_all | solution.py:290
  36.1 0.0 copy-done.10
  36.1 9.5 %all-to-all-done.2.parts = bf16[8,64,512]{2,1,0:T(8,128)(2,1)S(1)} async-done(((bf16[8,64,512]{2,1,0:T(8,128)(2,1)}), bf16[8,64,512]{2,1,0:T(8,128)(2,1)S(1)}, u32[]{:S(2)}, u32[]{:S(2)}) %all-to-all-start.2) | async-done | bytes 524320 | tf_op jit(solution)/shard_map/all_to_all | solution.py:290
  45.6 0.0 copy-done.2
  45.6 0.0 copy-done.3
  45.6 0.0 copy-done.8
  45.6 0.0 copy-done.9
  45.7 0.0 copy-start.6
  45.7 1.4 %shard_map.103 = (bf16[64,512]{1,0:T(8,128)(2,1)S(1)}, bf16[8,144,128]{2,1,0:T(8,128)(2,1)}) custom-call(bf16[8,64,512]{2,1,0:T(8,128)(2,1)S(1)} %all-to-all-done.2.parts, s32[1,64]{1,0:T(1,128)S(1)} %bitcast.8, s32[1,64]{1,0:T(1,128)S(1)} %copy-done.9, bf16[1,512]{1,0:T(2,128)(2,1)S(1)} %reshape.18.mask_token, bf16[64,512]{1,0:T(8,128)(2,1)S(1)} %copy-done.2, ...), custom_call_target="tpu_custom_call" | custom-call | tf_op jit(solution)/shard_map/pallas_call | solution.py:275
  47.1 3.4 %all-to-all-start.3 = ((bf16[8,144,128]{2,1,0:T(8,128)(2,1)}), bf16[8,144,128]{2,1,0:T(8,128)(2,1)S(1)}, u32[]{:S(2)}, u32[]{:S(2)}) async-start(bf16[8,144,128]{2,1,0:T(8,128)(2,1)} %get-tuple-element.7), calls=%async_computation.3 | async-start | bytes 589824 | tf_op jit(solution)/shard_map/all_to_all | solution.py:290
  50.5 6.2 %all-to-all-done.3.group.queries = bf16[8,144,128]{2,1,0:T(8,128)(2,1)S(1)} async-done(((bf16[8,144,128]{2,1,0:T(8,128)(2,1)}), bf16[8,144,128]{2,1,0:T(8,128)(2,1)S(1)}, u32[]{:S(2)}, u32[]{:S(2)}) %all-to-all-start.3) | async-done | bytes 294944 | tf_op jit(solution)/shard_map/all_to_all | solution.py:290
  56.8 31.5 %all_to_all.37.column = bf16[8,144,128]{2,1,0:T(8,128)(2,1)S(1)} all-to-all(bf16[8,144,128]{2,1,0:T(8,128)(2,1)S(1)} %shard_map.104), channel_id=1, replica_groups=mesh['zz'=8,'zp'=2,'y'=4,'x'=4,'core'=2] {'zz'}, dimensions={0} | all-to-all | bytes 589824 | tf_op jit(solution)/shard_map/all_to_all | solution.py:290
  88.3 6.8 %shard_map.105 = bf16[8,80,128]{2,1,0:T(8,128)(2,1)S(1)} custom-call(bf16[8,144,128]{2,1,0:T(8,128)(2,1)S(1)} %all-to-all-done.3.group.queries, bf16[8,144,128]{2,1,0:T(8,128)(2,1)S(1)} %all_to_all.37.column), custom_call_target="tpu_custom_call" | custom-call | tf_op jit(solution)/shard_map/pallas_call | solution.py:275
  95.1 8.0 %all_to_all.38.message = bf16[8,80,128]{2,1,0:T(8,128)(2,1)S(1)} all-to-all(bf16[8,80,128]{2,1,0:T(8,128)(2,1)S(1)} %shard_map.105), channel_id=1, replica_groups=mesh['zz'=8,'zp'=2,'y'=4,'x'=4,'core'=2] {'zp','y'}, dimensions={0} | all-to-all | bytes 327680 | tf_op jit(solution)/shard_map/all_to_all | solution.py:290
  103.1 0.0 copy-done.6
  103.1 1.0 shard_map.106
  104.1 9.6 %all-to-all-start.6 = ((bf16[8,64,256]{2,1,0:T(8,128)(2,1)}), bf16[8,64,256]{2,1,0:T(8,128)(2,1)S(1)}, u32[]{:S(2)}, u32[]{:S(2)}) async-start(bf16[8,64,256]{2,1,0:T(8,128)(2,1)} %shard_map.106), calls=%async_computation.6 | async-start | bytes 524288 | tf_op jit(solution)/shard_map/all_to_all | solution.py:290
  113.7 6.5 %all-to-all-done.6.terms = bf16[8,64,256]{2,1,0:T(8,128)(2,1)S(1)} async-done(((bf16[8,64,256]{2,1,0:T(8,128)(2,1)}), bf16[8,64,256]{2,1,0:T(8,128)(2,1)S(1)}, u32[]{:S(2)}, u32[]{:S(2)}) %all-to-all-start.6) | async-done | bytes 262176 | tf_op jit(solution)/shard_map/all_to_all | solution.py:290
  120.2 1.1 shard_map.107
  (2 shorter events, 0.0 us)
Async XLA Ops:
  0.0 0.9 copy-start.5
  0.9 0.7 copy-start.7
  16.9 1.4 %copy-start = (bf16[1280,640]{1,0:T(8,128)(2,1)S(1)}, bf16[1280,640]{1,0:T(8,128)(2,1)}, u32[]{:S(2)}) copy-start(bf16[1280,640]{1,0:T(8,128)(2,1)} %w_in_hbm.1) | copy-start | bytes 4915204
  18.3 1.4 %copy-start.1 = (bf16[640,1280]{1,0:T(8,128)(2,1)S(1)}, bf16[640,1280]{1,0:T(8,128)(2,1)}, u32[]{:S(2)}) copy-start(bf16[640,1280]{1,0:T(8,128)(2,1)} %w_out_hbm.1) | copy-start | bytes 4915204
  19.8 11.0 %copy-start.4 = (bf16[160,512]{1,0:T(8,128)(2,1)S(1)}, bf16[160,512]{1,0:T(8,128)(2,1)}, u32[]{:S(2)}) copy-start(bf16[160,512]{1,0:T(8,128)(2,1)} %w_embed.1) | copy-start | bytes 491524
  21.7 14.4 %copy-start.10 = (bf16[512]{0:T(512)(128)(2,1)S(1)}, bf16[512]{0:T(512)(128)(2,1)}, u32[]{:S(2)}) copy-start(bf16[512]{0:T(512)(128)(2,1)} %param.16) | copy-start | bytes 3076
  21.8 23.9 %copy-start.2 = (bf16[64,512]{1,0:T(8,128)(2,1)S(1)}, bf16[64,512]{1,0:T(8,128)(2,1)}, u32[]{:S(2)}) copy-start(bf16[64,512]{1,0:T(8,128)(2,1)} %positions.3) | copy-start | bytes 196612
  21.8 23.9 %copy-start.3 = (bf16[512,3,64]{0,2,1:T(8,128)(2,1)S(1)}, bf16[512,3,64]{0,2,1:T(8,128)(2,1)}, u32[]{:S(2)}) copy-start(bf16[512,3,64]{0,2,1:T(8,128)(2,1)} %param.18) | copy-start | bytes 589828
  21.8 23.9 %copy-start.8 = (s32[1,64,1]{1,2,0:T(1,128)S(1)}, s32[1,64,1]{1,2,0:T(1,128)}, u32[]{:S(2)}) copy-start(s32[1,64,1]{1,2,0:T(1,128)} %param.11) | copy-start | bytes 772
  21.8 23.9 %copy-start.9 = (s32[1,64]{1,0:T(1,128)S(1)}, s32[1,64]{1,0:T(1,128)}, u32[]{:S(2)}) copy-start(s32[1,64]{1,0:T(1,128)} %counts.3) | copy-start | bytes 772
  31.8 13.8 %all-to-all-start.2 = ((bf16[8,64,512]{2,1,0:T(8,128)(2,1)}), bf16[8,64,512]{2,1,0:T(8,128)(2,1)S(1)}, u32[]{:S(2)}, u32[]{:S(2)}) async-start(bf16[8,64,512]{2,1,0:T(8,128)(2,1)} %shard_map.102), calls=%async_computation.2 | async-start | bytes 1048576 | tf_op jit(solution)/shard_map/all_to_all | solution.py:290
  45.7 57.5 %copy-start.6 = (bf16[64,512]{1,0:T(8,128)(2,1)S(1)}, bf16[64,512]{1,0:T(8,128)(2,1)}, u32[]{:S(2)}) copy-start(bf16[64,512]{1,0:T(8,128)(2,1)} %w_attn_out.1) | copy-start | bytes 196612
  47.1 9.6 %all-to-all-start.3 = ((bf16[8,144,128]{2,1,0:T(8,128)(2,1)}), bf16[8,144,128]{2,1,0:T(8,128)(2,1)S(1)}, u32[]{:S(2)}, u32[]{:S(2)}) async-start(bf16[8,144,128]{2,1,0:T(8,128)(2,1)} %get-tuple-element.7), calls=%async_computation.3 | async-start | bytes 589824 | tf_op jit(solution)/shard_map/all_to_all | solution.py:290
  104.1 16.1 %all-to-all-start.6 = ((bf16[8,64,256]{2,1,0:T(8,128)(2,1)}), bf16[8,64,256]{2,1,0:T(8,128)(2,1)S(1)}, u32[]{:S(2)}, u32[]{:S(2)}) async-start(bf16[8,64,256]{2,1,0:T(8,128)(2,1)} %shard_map.106), calls=%async_computation.6 | async-start | bytes 524288 | tf_op jit(solution)/shard_map/all_to_all | solution.py:290

commit v4 on v3

--- a/solution.py
+++ b/solution.py
@@ -125,7 +125,7 @@
     pos = positions[...]
     row_in = (embedded + dot(at, pos)).astype(BF)
     slot_in[...] = row_in
-    mask_in = (mask_token[...].astype(F32) + pos.astype(F32)).astype(BF)
+    mask_in = (mask_token[...].astype(F32).reshape(1, -1) + pos.astype(F32)).astype(BF)
     both = jnp.concatenate([mask_in, row_in], axis=0).astype(F32)
     w_q, w_k, w_v = w_rows[0], w_rows[1], w_rows[2]
     heads = [slice(0, HDIM), slice(HDIM, 2 * HDIM)]
@@ -153,8 +153,8 @@
             out[4 * head + k, 2 * tubs :] = extra
 
 
-def pair_kernel(start, group, out):
-    y = start[0]
+def pair_kernel(group, out):
+    y = lax.axis_index("y")
     first, second = group.at[y], group.at[4 + y]
     odd = iota((16, 128), 0) % 2 == 1
     ids = jnp.where(odd, second[128:, :].astype(F32), first[128:, :].astype(F32)).astype(BF)
@@ -169,7 +169,7 @@
     slots = lists.shape[1]
     ids = column_of(live_row(lists[...], counts[...], rows))
     choose = (iota((dec, feats), 0) == iota((dec, feats), 1) + start).astype(F32).astype(BF)
-    mask_in = (mask_token[...].astype(F32) + positions[...].astype(F32)).astype(BF)
+    mask_in = (mask_token[...].astype(F32).reshape(1, -1) + positions[...].astype(F32)).astype(BF)
     mask_own = dot(mask_in, choose).astype(BF)
     slot_own = dot(slot_in[...], choose).astype(BF)
     picked = (ids == iota((slots, rows), 1)).astype(F32)
@@ -208,29 +208,35 @@
             kv_scr[v, k * tubs : (k + 1) * tubs, :] = mat[v * tubs : (v + 1) * tubs]
     packed = queries[:, :tubs, :].reshape(blocks * tubs, 128)
     scale = math.log2(math.e) / math.sqrt(HDIM)
-    chunk = 256
-    per = chunk // tubs
+
+    def score(v):
+        take = (iota((128, 64), 0) == iota((128, 64), 1) + HDIM * v) & (iota((128, 64), 1) < HDIM)
+        query = dot(packed, take.astype(F32).astype(BF)).astype(BF)
+        return dot_nt(kv_scr[v], query)
+
+    def weigh(scores):
+        top = jnp.max(scores, axis=0, keepdims=True)
+        weights = jnp.exp2((scores - top) * scale)
+        return top, jnp.sum(weights, axis=0, keepdims=True), weights.astype(BF)
+
+    def put(v, top, total, weights):
+        summed = dot_tn(kv_scr[v], weights)[HDIM:]
+        stats = split_pieces(top * scale, 3) + split_pieces(total, 2)
+        stats = jnp.concatenate(stats + [jnp.zeros((3, blocks * tubs), F32)], axis=0)
+        half, side = v // 2, slice(64 * (v % 2), 64 * (v % 2) + 64)
+        for b in range(blocks):
+            cols = slice(b * tubs, (b + 1) * tubs)
+            msg_scr[b, HDIM * half : HDIM * half + HDIM, side] = summed[:, cols]
+            msg_scr[b, 64 + 8 * half : 72 + 8 * half, side] = stats[:, cols]
+
+    scores, waiting = score(0), None
     for v in range(vols):
-        lanes = iota((128, 64), 0)
-        take = (lanes == iota((128, 64), 1) + HDIM * v) & (iota((128, 64), 1) < HDIM)
-        query = dot(packed, take.astype(F32).astype(BF)).astype(BF)
-        kv = kv_scr[v]
-        for c in range(blocks // per):
-            scores = dot_nt(kv, query[c * chunk : (c + 1) * chunk])
-            top = jnp.max(scores, axis=0, keepdims=True)
-            weights = jnp.exp2((scores - top) * scale)
-            total = jnp.sum(weights, axis=0, keepdims=True)
-            summed = dot_tn(kv, weights.astype(BF))[HDIM:]
-            stats = jnp.concatenate(
-                split_pieces(top * scale, 3) + split_pieces(total, 2) + [jnp.zeros((3, chunk), F32)],
-                axis=0,
-            )
-            side = slice(64 * (v % 2), 64 * (v % 2) + 64)
-            for b in range(per):
-                cols = slice(b * tubs, (b + 1) * tubs)
-                dest = c * per + b
-                msg_scr[dest, HDIM * (v // 2) : HDIM * (v // 2) + HDIM, side] = summed[:, cols]
-                msg_scr[dest, 64 + 8 * (v // 2) : 72 + 8 * (v // 2), side] = stats[:, cols]
+        later = score(v + 1) if v + 1 < vols else None
+        weighed = weigh(scores)
+        if waiting is not None:
+            put(*waiting)
+        waiting, scores = (v, *weighed), later
+    put(*waiting)
     for b in range(blocks):
         out[b] = msg_scr[b].astype(BF)
 
@@ -259,17 +265,17 @@
         out[k] = terms[k * feats : (k + 1) * feats]
 
 
-def finish_kernel(start, terms, lists, counts, mask_token, positions, slot_in, out):
+def finish_kernel(terms, lists, counts, mask_token, positions, slot_in, out):
     vols, tubs, feats = out.shape
-    total = own_rows(start[0], lists, counts, mask_token, positions, slot_in, feats, vols * tubs)
+    start = lax.axis_index(MP) * feats
+    total = own_rows(start, lists, counts, mask_token, positions, slot_in, feats, vols * tubs)
     total = total + sum(terms[k].astype(F32) for k in range(terms.shape[0]))
     out[...] = total.T.astype(BF).reshape(vols, tubs, feats)
 
 
-def call(kernel, out, *args, scratch=(), smem=0, hbm=0):
-    specs = [pl.BlockSpec(memory_space=pltpu.SMEM)] * smem
-    specs += [pl.BlockSpec(memory_space=pltpu.VMEM)] * (len(args) - smem - hbm)
-    specs += [pl.BlockSpec(memory_space=pltpu.HBM)] * hbm
+def call(kernel, out, *args, scratch=(), hbm=0):
+    specs = [pl.BlockSpec(memory_space=pltpu.VMEM)] * (len(args) - hbm)
+    specs += [pl.BlockSpec(memory_space=pl.ANY)] * hbm
     many = isinstance(out, list)
     one = pl.BlockSpec(memory_space=pltpu.VMEM)
     return pl.pallas_call(
@@ -278,7 +284,7 @@
         in_specs=specs,
         out_specs=[one] * len(out) if many else one,
         scratch_shapes=list(scratch),
-        compiler_params=pltpu.CompilerParams(vmem_limit_bytes=32 * 2**20),
+        compiler_params=None if hbm else pltpu.CompilerParams(vmem_limit_bytes=32 * 2**20),
     )(*args)
 
 
@@ -312,7 +318,6 @@
     lists = visible_lists.reshape(1, -1)
     counts = visible_counts.reshape(1, -1)
     slots = lists.shape[1]
-    token_row = mask_token.reshape(1, dec)
     w_rows = w_qkv.transpose(1, 2, 0)
     pair = pltpu.SemaphoreType.DMA((2,))
 
@@ -339,11 +344,10 @@
     slot_in, group = call(
         project_kernel,
         [shape(slots, dec), shape(ngroup, 144, 128)],
-        embed_parts, lists, counts, token_row, positions, w_rows,
+        embed_parts, lists, counts, mask_token, positions, w_rows,
     )
     group = exchange(group, GROUP)
-    y_index = lax.axis_index("y").reshape(1).astype(I32)
-    column = call(pair_kernel, shape(lax.axis_size("zz"), 144, 128), y_index, group, smem=1)
+    column = call(pair_kernel, shape(lax.axis_size("zz"), 144, 128), group)
     column = exchange(column, "zz")
     message = call(
         attend_kernel,
@@ -355,12 +359,10 @@
     message = exchange(message, GROUP)
     head_terms = call(combine_kernel, shape(nmp, feats, rows), message, w_attn_out)
     head_terms = exchange(head_terms, MP)
-    start = (lax.axis_index(MP) * feats).reshape(1).astype(I32)
     return call(
         finish_kernel,
         shape(vols, tubs, feats),
-        start, head_terms, lists, counts, token_row, positions, slot_in,
-        smem=1,
+        head_terms, lists, counts, mask_token, positions, slot_in,
     )
 
 

time: 122 us -> 115 us (0.943)
  blocking collectives: 63.4 us -> 102 us
  waiting for transfers between devices: 22.2 us -> 0 us
  starting transfers between devices: 17.3 us -> 0 us
  local copies, waits for them, and re-layouts: 4.46 us -> 0.05 us
  Pallas kernels: 13.8 us -> 12.3 us
    all_to_all x4 -> x7, blocking collectives: 63.4 us -> 102 us  [exchange(): return lax.all_to_all(values, axes, 0, 0, tiled=True)]
    all_to_all x3 -> x0, waiting for transfers between devices: 22.2 us -> none  [exchange(): return lax.all_to_all(values, axes, 0, 0, tiled=True)]
    all_to_all x3 -> x0, starting transfers between devices: 17.3 us -> none  [exchange(): return lax.all_to_all(values, axes, 0, 0, tiled=True)]
    unnamed x22 -> x16, local copies, waits for them, and re-layouts: 4.46 us -> 0.05 us
    pallas_call x8, Pallas kernels: 13.8 us -> 12.3 us  [call(): pl.pallas_call(kernel, out_shape=out, in_specs=specs, out_specs=[one] * l...]
  transfers between devices with their start and end apart: 3 -> 0, of which waited for: 3 -> 0; matrix products, arithmetic and copies ran while one was open for 0% -> 0% of each run, Pallas kernels for 0% -> 0%
where the time goes in v4:
time: 115 us
  blocking collectives  102 us (89%)
  Pallas kernels  12.3 us (11%)
    all_to_all x7, blocking collectives, exchange(): return lax.all_to_all(values, axes, 0, 0, tiled=True)  102 us
    pallas_call x8, Pallas kernels, call(): pl.pallas_call(kernel, out_shape=out, in_specs=specs, out_specs=[one] * l...  12.3 us

profile of v4, /device:TPU:1, one launch (start us, length us, event | category | flops | bytes accessed | tf_op | source)
XLA Modules:
  0.0 114.9 jit_solution(16007700277287821472)
XLA Ops:
  0.0 1.8 %shard_map.100.own = bf16[8,80,128]{2,1,0:T(8,128)(2,1)} custom-call(s32[1,64]{1,0:T(1,128)} %bitcast.4, bf16[256,160]{1,0:T(8,128)(2,1)} %bitcast.7), custom_call_target="tpu_custom_call" | custom-call | tf_op jit(solution)/shard_map/pallas_call | solution.py:281
  1.8 16.5 %all_to_all.35.gathered = bf16[8,80,128]{2,1,0:T(8,128)(2,1)} all-to-all(bf16[8,80,128]{2,1,0:T(8,128)(2,1)} %shard_map.100.own), channel_id=1, replica_groups=mesh['zz'=8,'zp'=2,'y'=4,'x'=4,'core'=2] {'x','core'}, dimensions={0} | all-to-all | bytes 327680 | tf_op jit(solution)/shard_map/all_to_all | solution.py:296
  18.3 0.0 copy-start
  18.3 0.0 copy-start.3
  18.3 4.3 %shard_map.101 = bf16[8,80,128]{2,1,0:T(8,128)(2,1)} custom-call(bf16[8,80,128]{2,1,0:T(8,128)(2,1)} %all_to_all.35.gathered, bf16[1280,640]{1,0:T(8,128)(2,1)} %w_in_hbm.1, bf16[640,1280]{1,0:T(8,128)(2,1)} %w_out_hbm.1), custom_call_target="tpu_custom_call" | custom-call | tf_op jit(solution)/shard_map/pallas_call | solution.py:281
  22.6 0.0 copy-start.1
  22.6 0.0 copy-start.2
  22.6 0.0 copy-start.5
  22.6 0.0 copy-start.6
  22.6 0.0 copy-start.7
  22.6 9.9 %all_to_all.36.terms = bf16[8,80,128]{2,1,0:T(8,128)(2,1)S(1)} all-to-all(bf16[8,80,128]{2,1,0:T(8,128)(2,1)} %shard_map.101), channel_id=1, replica_groups=mesh['zz'=8,'zp'=2,'y'=4,'x'=4,'core'=2] {'x','core'}, dimensions={0} | all-to-all | bytes 327680 | tf_op jit(solution)/shard_map/all_to_all | solution.py:296
  32.5 0.0 copy-done
  32.5 0.0 copy-done.3
  32.5 0.2 shard_map.102
  32.8 12.7 %all_to_all.37.parts = bf16[8,64,512]{2,1,0:T(8,128)(2,1)S(1)} all-to-all(bf16[8,64,512]{2,1,0:T(8,128)(2,1)S(1)} %shard_map.102), channel_id=1, replica_groups=mesh['zz'=8,'zp'=2,'y'=4,'x'=4,'core'=2] {'x','core'}, dimensions={0} | all-to-all | bytes 1048576 | tf_op jit(solution)/shard_map/all_to_all | solution.py:296
  45.4 0.0 copy-done.1
  45.4 0.0 copy-done.2
  45.4 0.0 copy-done.5
  45.4 0.0 copy-done.6
  45.5 0.0 copy-done.7
  45.5 0.0 copy-start.4
  45.5 0.7 shard_map.103
  46.2 8.9 %all_to_all.38.group.queries = bf16[8,144,128]{2,1,0:T(8,128)(2,1)S(1)} all-to-all(bf16[8,144,128]{2,1,0:T(8,128)(2,1)S(1)} %get-tuple-element.7), channel_id=1, replica_groups=mesh['zz'=8,'zp'=2,'y'=4,'x'=4,'core'=2] {'zp','y'}, dimensions={0} | all-to-all | bytes 589824 | tf_op jit(solution)/shard_map/all_to_all | solution.py:296
  55.2 31.3 %all_to_all.39.column = bf16[8,144,128]{2,1,0:T(8,128)(2,1)S(1)} all-to-all(bf16[8,144,128]{2,1,0:T(8,128)(2,1)S(1)} %shard_map.104), channel_id=1, replica_groups=mesh['zz'=8,'zp'=2,'y'=4,'x'=4,'core'=2] {'zz'}, dimensions={0} | all-to-all | bytes 589824 | tf_op jit(solution)/shard_map/all_to_all | solution.py:296
  86.5 3.9 %shard_map.105 = bf16[8,80,128]{2,1,0:T(8,128)(2,1)S(1)} custom-call(bf16[8,144,128]{2,1,0:T(8,128)(2,1)S(1)} %all_to_all.38.group.queries, bf16[8,144,128]{2,1,0:T(8,128)(2,1)S(1)} %all_to_all.39.column), custom_call_target="tpu_custom_call" | custom-call | tf_op jit(solution)/shard_map/pallas_call | solution.py:281
  90.4 8.0 %all_to_all.40.message = bf16[8,80,128]{2,1,0:T(8,128)(2,1)S(1)} all-to-all(bf16[8,80,128]{2,1,0:T(8,128)(2,1)S(1)} %shard_map.105), channel_id=1, replica_groups=mesh['zz'=8,'zp'=2,'y'=4,'x'=4,'core'=2] {'zp','y'}, dimensions={0} | all-to-all | bytes 327680 | tf_op jit(solution)/shard_map/all_to_all | solution.py:296
  98.4 0.0 copy-done.4
  98.4 0.3 shard_map.106
  98.7 15.1 %all_to_all.41.terms = bf16[8,64,256]{2,1,0:T(8,128)(2,1)S(1)} all-to-all(bf16[8,64,256]{2,1,0:T(8,128)(2,1)S(1)} %shard_map.106), channel_id=1, replica_groups=mesh['zz'=8,'zp'=2,'y'=4,'x'=4,'core'=2] {'x','core'}, dimensions={0} | all-to-all | bytes 524288 | tf_op jit(solution)/shard_map/all_to_all | solution.py:296
  113.8 1.1 shard_map.107
  (1 shorter events, 0.0 us)
Async XLA Ops:
  18.3 14.2 %copy-start = (bf16[8,80,128]{2,1,0:T(8,128)(2,1)S(1)}, bf16[8,80,128]{2,1,0:T(8,128)(2,1)}, u32[]{:S(2)}) copy-start(bf16[8,80,128]{2,1,0:T(8,128)(2,1)} %shard_map.100.own) | copy-start | bytes 491524
  18.3 14.2 %copy-start.3 = (bf16[160,512]{1,0:T(8,128)(2,1)S(1)}, bf16[160,512]{1,0:T(8,128)(2,1)}, u32[]{:S(2)}) copy-start(bf16[160,512]{1,0:T(8,128)(2,1)} %w_embed.1) | copy-start | bytes 491524
  22.6 22.9 %copy-start.1 = (bf16[64,512]{1,0:T(8,128)(2,1)S(1)}, bf16[64,512]{1,0:T(8,128)(2,1)}, u32[]{:S(2)}) copy-start(bf16[64,512]{1,0:T(8,128)(2,1)} %positions.3) | copy-start | bytes 196612
  22.6 22.9 %copy-start.2 = (bf16[512,3,64]{0,2,1:T(8,128)(2,1)S(1)}, bf16[512,3,64]{0,2,1:T(8,128)(2,1)}, u32[]{:S(2)}) copy-start(bf16[512,3,64]{0,2,1:T(8,128)(2,1)} %param.18) | copy-start | bytes 589828
  22.6 22.9 %copy-start.5 = (s32[1,64,1]{1,2,0:T(1,128)S(1)}, s32[1,64,1]{1,2,0:T(1,128)}, u32[]{:S(2)}) copy-start(s32[1,64,1]{1,2,0:T(1,128)} %param.11) | copy-start | bytes 772
  22.6 22.9 %copy-start.6 = (bf16[512]{0:T(512)(128)(2,1)S(1)}, bf16[512]{0:T(512)(128)(2,1)}, u32[]{:S(2)}) copy-start(bf16[512]{0:T(512)(128)(2,1)} %mask_token.3) | copy-start | bytes 3076
  22.6 22.9 %copy-start.7 = (s32[1,64]{1,0:T(1,128)S(1)}, s32[1,64]{1,0:T(1,128)}, u32[]{:S(2)}) copy-start(s32[1,64]{1,0:T(1,128)} %counts.3) | copy-start | bytes 772
  45.5 52.9 %copy-start.4 = (bf16[64,512]{1,0:T(8,128)(2,1)S(1)}, bf16[64,512]{1,0:T(8,128)(2,1)}, u32[]{:S(2)}) copy-start(bf16[64,512]{1,0:T(8,128)(2,1)} %w_attn_out.1) | copy-start | bytes 196612

commit v5 on v4

--- a/solution.py
+++ b/solution.py
@@ -62,30 +62,16 @@
     return jnp.concatenate([folded[:64], tail], axis=1)
 
 
-def pick_kernel(lists_hbm, tokens_hbm, out, lists, tokens, sems):
-    copies = [
-        pltpu.make_async_copy(lists_hbm, lists, sems.at[0]),
-        pltpu.make_async_copy(tokens_hbm, tokens, sems.at[1]),
-    ]
-    for copy in copies:
-        copy.start()
+def pick_kernel(lists, tokens, out):
     rows = tokens.shape[0]
-    copies[0].wait()
     ids = column_of(lists[...])
     named = (ids == iota((ids.shape[0], rows), 1)).astype(F32).astype(BF)
-    copies[1].wait()
     own = fold_tail(dot(named, tokens[...])).astype(BF)
     for k in range(out.shape[0]):
         out[k] = own
 
 
-def feed_kernel(gathered, w_in_hbm, w_out_hbm, out, w_in, w_out, sems):
-    copies = [
-        pltpu.make_async_copy(w_in_hbm, w_in, sems.at[0]),
-        pltpu.make_async_copy(w_out_hbm, w_out, sems.at[1]),
-    ]
-    for copy in copies:
-        copy.start()
+def feed_kernel(gathered, w_in, w_out, out):
     count = gathered.shape[0]
     part = w_in.shape[0] // count
     blocks = [unfold_tail(gathered[k].astype(F32)) for k in range(count)]
@@ -94,14 +80,11 @@
     blocks = [b - mean_row for b in blocks]
     spread = sum(jnp.sum(b * b, axis=1, keepdims=True) for b in blocks) * (1.0 / width)
     scale = lax.rsqrt(spread + 1e-05)
-    blocks = [(b * scale).astype(BF) for b in blocks]
-    copies[0].wait()
     hidden = None
     for k in range(count):
-        term = dot(blocks[k], w_in[k * part : (k + 1) * part, :])
+        term = dot((blocks[k] * scale).astype(BF), w_in[k * part : (k + 1) * part, :])
         hidden = term if hidden is None else hidden + term
     act = (0.5 * hidden * (1.0 + lax.erf(hidden * math.sqrt(0.5)))).astype(BF)
-    copies[1].wait()
     terms = dot(act, w_out[...])
     for k in range(count):
         out[k] = fold_tail(terms[:, k * part : (k + 1) * part]).astype(BF)
@@ -273,18 +256,22 @@
     out[...] = total.T.astype(BF).reshape(vols, tubs, feats)
 
 
-def call(kernel, out, *args, scratch=(), hbm=0):
-    specs = [pl.BlockSpec(memory_space=pltpu.VMEM)] * (len(args) - hbm)
-    specs += [pl.BlockSpec(memory_space=pl.ANY)] * hbm
+def call(kernel, out, *args, scratch=(), micros=0):
     many = isinstance(out, list)
     one = pl.BlockSpec(memory_space=pltpu.VMEM)
+    cost = None
+    if micros:
+        cost = pl.CostEstimate(
+            flops=micros * 10**9, bytes_accessed=micros * 10**6, transcendentals=0
+        )
     return pl.pallas_call(
         kernel,
         out_shape=out,
-        in_specs=specs,
+        in_specs=[one] * len(args),
         out_specs=[one] * len(out) if many else one,
         scratch_shapes=list(scratch),
-        compiler_params=None if hbm else pltpu.CompilerParams(vmem_limit_bytes=32 * 2**20),
+        compiler_params=pltpu.CompilerParams(vmem_limit_bytes=32 * 2**20),
+        cost_estimate=cost,
     )(*args)
 
 
@@ -319,26 +306,12 @@
     counts = visible_counts.reshape(1, -1)
     slots = lists.shape[1]
     w_rows = w_qkv.transpose(1, 2, 0)
-    pair = pltpu.SemaphoreType.DMA((2,))
 
     own = call(
-        pick_kernel,
-        shape(nmp, 80, 128),
-        lists,
-        tokens.reshape(rows, part),
-        hbm=2,
-        scratch=[pltpu.VMEM((1, slots), I32), pltpu.VMEM((rows, part), BF), pair],
+        pick_kernel, shape(nmp, 80, 128), lists, tokens.reshape(rows, part), micros=10
     )
     full = exchange(own, MP)
-    terms = call(
-        feed_kernel,
-        shape(nmp, 80, 128),
-        full,
-        w_in,
-        w_out,
-        hbm=2,
-        scratch=[pltpu.VMEM(w_in.shape, BF), pltpu.VMEM(w_out.shape, BF), pair],
-    )
+    terms = call(feed_kernel, shape(nmp, 80, 128), full, w_in, w_out)
     terms = exchange(terms, MP)
     embed_parts = exchange(call(embed_kernel, shape(nmp, slots, dec), terms, own, w_embed), MP)
     slot_in, group = call(

time: 115 us -> 111 us (0.965)
  Pallas kernels: 12.3 us -> 7.92 us
  local copies, waits for them, and re-layouts: 0.05 us -> 1.6 us
    pallas_call x8, Pallas kernels: 12.3 us -> 7.92 us  [call(): pl.pallas_call(kernel, out_shape=out, in_specs=[one] * len(args), out_spe...]
    unnamed x16 -> x22, local copies, waits for them, and re-layouts: 0.05 us -> 1.6 us
where the time goes in v5:
time: 111 us
  blocking collectives  101 us (91%)
  Pallas kernels  7.92 us (7%)
  local copies, waits for them, and re-layouts  1.6 us (1%)
    all_to_all x7, blocking collectives, exchange(): return lax.all_to_all(values, axes, 0, 0, tiled=True)  101 us
    pallas_call x8, Pallas kernels, call(): pl.pallas_call(kernel, out_shape=out, in_specs=[one] * len(args), out_spe...  7.92 us

profile of v5, /device:TPU:1, one launch (start us, length us, event | category | flops | bytes accessed | tf_op | source)
XLA Modules:
  0.0 110.9 jit_solution(11279515528296126855)
XLA Ops:
  0.0 0.0 copy-start.7
  0.0 0.7 copy-done.7
  0.7 0.0 copy-start.10
  0.7 0.9 copy-done.10
  1.6 0.0 copy-start
  1.6 0.0 copy-start.1
  1.6 0.3 shard_map.100.own
  1.8 15.0 %all_to_all.35.gathered = bf16[8,80,128]{2,1,0:T(8,128)(2,1)S(1)} all-to-all(bf16[8,80,128]{2,1,0:T(8,128)(2,1)S(1)} %shard_map.100.own), channel_id=1, replica_groups=mesh['zz'=8,'zp'=2,'y'=4,'x'=4,'core'=2] {'x','core'}, dimensions={0} | all-to-all | bytes 327680 | tf_op jit(solution)/shard_map/all_to_all | solution.py:283
  16.8 0.0 copy-done
  16.8 0.0 copy-done.1
  16.8 0.0 copy-start.4
  16.8 1.4 %shard_map.101 = bf16[8,80,128]{2,1,0:T(8,128)(2,1)S(1)} custom-call(bf16[8,80,128]{2,1,0:T(8,128)(2,1)S(1)} %all_to_all.35.gathered, bf16[1280,640]{1,0:T(8,128)(2,1)S(1)} %copy-done, bf16[640,1280]{1,0:T(8,128)(2,1)S(1)} %copy-done.1), custom_call_target="tpu_custom_call" | custom-call | tf_op jit(solution)/shard_map/pallas_call | solution.py:267
  18.2 0.0 copy-start.2
  18.2 0.0 copy-start.3
  18.2 0.0 copy-start.6
  18.2 0.0 copy-start.8
  18.2 0.0 copy-start.9
  18.3 9.0 %all_to_all.36.terms = bf16[8,80,128]{2,1,0:T(8,128)(2,1)S(1)} all-to-all(bf16[8,80,128]{2,1,0:T(8,128)(2,1)S(1)} %shard_map.101), channel_id=1, replica_groups=mesh['zz'=8,'zp'=2,'y'=4,'x'=4,'core'=2] {'x','core'}, dimensions={0} | all-to-all | bytes 327680 | tf_op jit(solution)/shard_map/all_to_all | solution.py:283
  27.3 0.0 copy-done.4
  27.3 0.2 shard_map.102
  27.5 12.7 %all_to_all.37.parts = bf16[8,64,512]{2,1,0:T(8,128)(2,1)S(1)} all-to-all(bf16[8,64,512]{2,1,0:T(8,128)(2,1)S(1)} %shard_map.102), channel_id=1, replica_groups=mesh['zz'=8,'zp'=2,'y'=4,'x'=4,'core'=2] {'x','core'}, dimensions={0} | all-to-all | bytes 1048576 | tf_op jit(solution)/shard_map/all_to_all | solution.py:283
  40.2 0.0 copy-done.2
  40.2 0.0 copy-done.3
  40.2 0.0 copy-done.6
  40.2 0.0 copy-done.8
  40.2 0.0 copy-done.9
  40.2 0.0 copy-start.5
  40.2 0.7 shard_map.103
  40.9 8.9 %all_to_all.38.group.queries = bf16[8,144,128]{2,1,0:T(8,128)(2,1)S(1)} all-to-all(bf16[8,144,128]{2,1,0:T(8,128)(2,1)S(1)} %get-tuple-element.7), channel_id=1, replica_groups=mesh['zz'=8,'zp'=2,'y'=4,'x'=4,'core'=2] {'zp','y'}, dimensions={0} | all-to-all | bytes 589824 | tf_op jit(solution)/shard_map/all_to_all | solution.py:283
  49.9 32.6 %all_to_all.39.column = bf16[8,144,128]{2,1,0:T(8,128)(2,1)S(1)} all-to-all(bf16[8,144,128]{2,1,0:T(8,128)(2,1)S(1)} %shard_map.104), channel_id=1, replica_groups=mesh['zz'=8,'zp'=2,'y'=4,'x'=4,'core'=2] {'zz'}, dimensions={0} | all-to-all | bytes 589824 | tf_op jit(solution)/shard_map/all_to_all | solution.py:283
  82.5 3.9 %shard_map.105 = bf16[8,80,128]{2,1,0:T(8,128)(2,1)S(1)} custom-call(bf16[8,144,128]{2,1,0:T(8,128)(2,1)S(1)} %all_to_all.38.group.queries, bf16[8,144,128]{2,1,0:T(8,128)(2,1)S(1)} %all_to_all.39.column), custom_call_target="tpu_custom_call" | custom-call | tf_op jit(solution)/shard_map/pallas_call | solution.py:267
  86.4 8.0 %all_to_all.40.message = bf16[8,80,128]{2,1,0:T(8,128)(2,1)S(1)} all-to-all(bf16[8,80,128]{2,1,0:T(8,128)(2,1)S(1)} %shard_map.105), channel_id=1, replica_groups=mesh['zz'=8,'zp'=2,'y'=4,'x'=4,'core'=2] {'zp','y'}, dimensions={0} | all-to-all | bytes 327680 | tf_op jit(solution)/shard_map/all_to_all | solution.py:283
  94.4 0.0 copy-done.5
  94.4 0.3 shard_map.106
  94.7 15.1 %all_to_all.41.terms = bf16[8,64,256]{2,1,0:T(8,128)(2,1)S(1)} all-to-all(bf16[8,64,256]{2,1,0:T(8,128)(2,1)S(1)} %shard_map.106), channel_id=1, replica_groups=mesh['zz'=8,'zp'=2,'y'=4,'x'=4,'core'=2] {'x','core'}, dimensions={0} | all-to-all | bytes 524288 | tf_op jit(solution)/shard_map/all_to_all | solution.py:283
  109.8 1.1 shard_map.107
  (1 shorter events, 0.0 us)
Async XLA Ops:
  0.0 0.7 copy-start.7
  0.7 0.9 copy-start.10
  1.6 15.3 %copy-start = (bf16[1280,640]{1,0:T(8,128)(2,1)S(1)}, bf16[1280,640]{1,0:T(8,128)(2,1)}, u32[]{:S(2)}) copy-start(bf16[1280,640]{1,0:T(8,128)(2,1)} %w_in.1) | copy-start | bytes 4915204
  1.6 15.3 %copy-start.1 = (bf16[640,1280]{1,0:T(8,128)(2,1)S(1)}, bf16[640,1280]{1,0:T(8,128)(2,1)}, u32[]{:S(2)}) copy-start(bf16[640,1280]{1,0:T(8,128)(2,1)} %w_out.1) | copy-start | bytes 4915204
  16.8 10.4 %copy-start.4 = (bf16[160,512]{1,0:T(8,128)(2,1)S(1)}, bf16[160,512]{1,0:T(8,128)(2,1)}, u32[]{:S(2)}) copy-start(bf16[160,512]{1,0:T(8,128)(2,1)} %w_embed.1) | copy-start | bytes 491524
  18.2 22.0 %copy-start.2 = (bf16[64,512]{1,0:T(8,128)(2,1)S(1)}, bf16[64,512]{1,0:T(8,128)(2,1)}, u32[]{:S(2)}) copy-start(bf16[64,512]{1,0:T(8,128)(2,1)} %positions.3) | copy-start | bytes 196612
  18.2 22.0 %copy-start.3 = (bf16[512,3,64]{0,2,1:T(8,128)(2,1)S(1)}, bf16[512,3,64]{0,2,1:T(8,128)(2,1)}, u32[]{:S(2)}) copy-start(bf16[512,3,64]{0,2,1:T(8,128)(2,1)} %param.18) | copy-start | bytes 589828
  18.2 22.0 %copy-start.6 = (bf16[512]{0:T(512)(128)(2,1)S(1)}, bf16[512]{0:T(512)(128)(2,1)}, u32[]{:S(2)}) copy-start(bf16[512]{0:T(512)(128)(2,1)} %mask_token.3) | copy-start | bytes 3076
  18.2 21.9 %copy-start.8 = (s32[1,64,1]{1,2,0:T(1,128)S(1)}, s32[1,64,1]{1,2,0:T(1,128)}, u32[]{:S(2)}) copy-start(s32[1,64,1]{1,2,0:T(1,128)} %param.11) | copy-start | bytes 772
  18.2 21.9 %copy-start.9 = (s32[1,64]{1,0:T(1,128)S(1)}, s32[1,64]{1,0:T(1,128)}, u32[]{:S(2)}) copy-start(s32[1,64]{1,0:T(1,128)} %counts.3) | copy-start | bytes 772
  40.2 54.3 %copy-start.5 = (bf16[64,512]{1,0:T(8,128)(2,1)S(1)}, bf16[64,512]{1,0:T(8,128)(2,1)}, u32[]{:S(2)}) copy-start(bf16[64,512]{1,0:T(8,128)(2,1)} %w_attn_out.1) | copy-start | bytes 196612

commit v6 on v5

--- a/solution.py
+++ b/solution.py
@@ -6,12 +6,19 @@
 from jax import lax
 from jax.experimental import pallas as pl
 from jax.experimental.pallas import tpu as pltpu
-from jax.sharding import Mesh, PartitionSpec as P
+from jax.sharding import PartitionSpec as P
 
 HDIM = 32
-MP = ("x", "core")
-GROUP = ("zp", "y")
-COLUMN = ("zz", "zp")
+NY = 4
+NZ = 16
+GROUP = [[(2 * k + p) * NY + y for p in range(2) for y in range(NY)] for k in range(NZ // 2)]
+COLUMN = [
+    [z * NY + y for z in range(NZ) if (z + z // (NZ // 2)) % 2 == head]
+    for head in range(2)
+    for y in range(NY)
+]
+ALONG_X = [[0, 2, 4, 6], [1, 3, 5, 7]]
+CORES = [[0, 1], [2, 3], [4, 5], [6, 7]]
 BF = jnp.bfloat16
 F32 = jnp.float32
 I32 = jnp.int32
@@ -43,6 +50,10 @@
 def column_of(row):
     n = row.shape[1]
     return jnp.sum(jnp.where(iota((n, n), 0) == iota((n, n), 1), row, 0), axis=1, keepdims=True)
+
+
+def plane_turn():
+    return lax.axis_index("seq") // (NY * NZ // 2)
 
 
 def live_row(lists, counts, rows):
@@ -98,12 +109,16 @@
         out[k] = value
 
 
+def join_kernel(parts, out):
+    out[...] = sum(parts[k].astype(F32) for k in range(parts.shape[0]))
+
+
 def project_kernel(parts, lists, counts, mask_token, positions, w_rows, slot_in, out):
     tubs = positions.shape[0]
     slots = lists.shape[1]
     ids_row = live_row(lists[...], counts[...], 4 * tubs)
     ids = column_of(ids_row)
-    embedded = sum(parts[k].astype(F32) for k in range(parts.shape[0])).astype(BF).astype(F32)
+    embedded = sum(parts[k] for k in range(parts.shape[0])).astype(BF).astype(F32)
     at = (ids % tubs == iota((slots, tubs), 1)).astype(F32).astype(BF)
     pos = positions[...]
     row_in = (embedded + dot(at, pos)).astype(BF)
@@ -123,28 +138,28 @@
     seen = dot(spot, of_volume.astype(F32).astype(BF)) > 0
     zero = jnp.zeros((slots, 128), BF)
     extra = jnp.concatenate([ids_row.astype(F32), jnp.zeros((1, 128 - slots), F32)], axis=1)
-    extra = jnp.broadcast_to(extra, (16, 128)).astype(BF)
+    extra = jnp.broadcast_to(extra, (8, 128)).astype(BF)
+    turn = plane_turn()
     for head in range(2):
         cols = slice(128 * head, 128 * head + 128)
         placed = dot(spot, jnp.where(of_volume, proj[:, cols], zero))
         query = jnp.where(seen, placed, masked[:, cols].astype(F32)).astype(BF)
         cols = slice(256 + 64 * head, 256 + 64 * head + 64)
         block = jnp.concatenate([masked[:, cols], proj[:, cols]], axis=1)
-        for k in range(4):
-            out[4 * head + k, :tubs] = query
-            out[4 * head + k, tubs : 2 * tubs] = block
-            out[4 * head + k, 2 * tubs :] = extra
+        block = jnp.concatenate([query, block, extra], axis=0)
+        plane = jnp.where(turn == 0, head, 1 - head)
+        for k in range(NY):
+            out[NY * plane + k] = block
 
 
 def pair_kernel(group, out):
-    y = lax.axis_index("y")
-    first, second = group.at[y], group.at[4 + y]
-    odd = iota((16, 128), 0) % 2 == 1
-    ids = jnp.where(odd, second[128:, :].astype(F32), first[128:, :].astype(F32)).astype(BF)
+    y = lax.axis_index("seq") % NY
+    first, second = group[y], group[NY + y]
+    odd = iota((8, 128), 0) % 2 == 1
+    ids = jnp.where(odd, second[128:].astype(F32), first[128:].astype(F32)).astype(BF)
+    block = jnp.concatenate([first[64:128], second[64:128], ids], axis=0)
     for k in range(out.shape[0]):
-        out[k, :64] = first[64:128, :]
-        out[k, 64:128] = second[64:128, :]
-        out[k, 128:] = ids
+        out[k] = block
 
 
 def own_rows(start, lists, counts, mask_token, positions, slot_in, feats, rows):
@@ -179,8 +194,9 @@
     keys = nz * tubs
     for k in range(nz):
         side = k % 2
-        block = column[k // 2, side * tubs : (side + 1) * tubs, :]
-        ids_row = column[k // 2, 2 * tubs :, :].astype(F32)[side : side + 1, :slots]
+        pair = column[k // 2]
+        block = pair[side * tubs : (side + 1) * tubs]
+        ids_row = pair[2 * tubs :].astype(F32)[side : side + 1, :slots]
         picked = (ids_row == iota((rows, slots), 0).astype(F32)).astype(F32)
         seen = jnp.sum(picked, axis=1, keepdims=True) > 0
         placed = dot(picked.astype(BF), block[:, 64:])
@@ -225,18 +241,21 @@
 
 
 def combine_kernel(message, w_attn_out, out):
-    ny = 4
+    turn = plane_turn()
     parts = []
     for head in range(2):
+        plane = jnp.where(turn == 0, head, 1 - head)
         sides = []
         for u in range(2):
-            stats = [message[4 * head + k, 64:, :].astype(F32)[8 * u : 8 * u + 8] for k in range(ny)]
+            stats = [
+                message[NY * plane + k, 64:, :].astype(F32)[8 * u : 8 * u + 8] for k in range(NY)
+            ]
             tops = [s[0:1] + s[1:2] + s[2:3] for s in stats]
             best = functools.reduce(jnp.maximum, tops)
             fades = [jnp.exp2(t - best) for t in tops]
             total = sum(f * (s[3:4] + s[4:5]) for f, s in zip(fades, stats))
             value = sum(
-                f * message[4 * head + k, HDIM * u : HDIM * u + HDIM, :].astype(F32)
+                f * message[NY * plane + k, HDIM * u : HDIM * u + HDIM, :].astype(F32)
                 for k, f in enumerate(fades)
             )
             sides.append(value / total)
@@ -250,7 +269,7 @@
 
 def finish_kernel(terms, lists, counts, mask_token, positions, slot_in, out):
     vols, tubs, feats = out.shape
-    start = lax.axis_index(MP) * feats
+    start = lax.axis_index("mp") * feats
     total = own_rows(start, lists, counts, mask_token, positions, slot_in, feats, vols * tubs)
     total = total + sum(terms[k].astype(F32) for k in range(terms.shape[0]))
     out[...] = total.T.astype(BF).reshape(vols, tubs, feats)
@@ -279,8 +298,8 @@
     return jax.ShapeDtypeStruct(dims, dtype)
 
 
-def exchange(values, axes):
-    return lax.all_to_all(values, axes, 0, 0, tiled=True)
+def exchange(values, axis, groups=None):
+    return lax.all_to_all(values, axis, 0, 0, axis_index_groups=groups, tiled=True)
 
 
 def local(
@@ -297,9 +316,8 @@
 ):
     vols, tubs, part = tokens.shape
     rows = vols * tubs
-    nmp = lax.axis_size(MP)
-    nz = lax.axis_size(COLUMN)
-    ngroup = lax.axis_size(GROUP)
+    nmp = lax.axis_size("mp")
+    ngroup, ncolumn = len(GROUP[0]), len(COLUMN[0])
     dec = w_embed.shape[1]
     feats = dec // nmp
     lists = visible_lists.reshape(1, -1)
@@ -310,28 +328,29 @@
     own = call(
         pick_kernel, shape(nmp, 80, 128), lists, tokens.reshape(rows, part), micros=10
     )
-    full = exchange(own, MP)
-    terms = call(feed_kernel, shape(nmp, 80, 128), full, w_in, w_out)
-    terms = exchange(terms, MP)
-    embed_parts = exchange(call(embed_kernel, shape(nmp, slots, dec), terms, own, w_embed), MP)
+    full = exchange(own, "mp")
+    terms = exchange(call(feed_kernel, shape(nmp, 80, 128), full, w_in, w_out), "mp")
+    parts = call(embed_kernel, shape(len(ALONG_X[0]), slots, dec), terms, own, w_embed)
+    parts = exchange(parts, "mp", ALONG_X)
+    part_sum = call(join_kernel, shape(slots, dec, dtype=F32), parts)
+    parts = lax.all_gather(part_sum, "mp", axis_index_groups=CORES)
     slot_in, group = call(
         project_kernel,
-        [shape(slots, dec), shape(ngroup, 144, 128)],
-        embed_parts, lists, counts, mask_token, positions, w_rows,
-    )
-    group = exchange(group, GROUP)
-    column = call(pair_kernel, shape(lax.axis_size("zz"), 144, 128), group)
-    column = exchange(column, "zz")
+        [shape(slots, dec), shape(ngroup, 136, 128)],
+        parts, lists, counts, mask_token, positions, w_rows,
+    )
+    group = exchange(group, "seq", GROUP)
+    column = exchange(call(pair_kernel, shape(ncolumn, 136, 128), group), "seq", COLUMN)
     message = call(
         attend_kernel,
         shape(ngroup, 80, 128),
         group,
         column,
-        scratch=[pltpu.VMEM((vols, nz * tubs, 64), BF), pltpu.VMEM((ngroup, 80, 128), F32)],
-    )
-    message = exchange(message, GROUP)
+        scratch=[pltpu.VMEM((vols, 2 * ncolumn * tubs, 64), BF), pltpu.VMEM((ngroup, 80, 128), F32)],
+    )
+    message = exchange(message, "seq", GROUP)
     head_terms = call(combine_kernel, shape(nmp, feats, rows), message, w_attn_out)
-    head_terms = exchange(head_terms, MP)
+    head_terms = exchange(head_terms, "mp")
     return call(
         finish_kernel,
         shape(vols, tubs, feats),
@@ -340,19 +359,17 @@
 
 
 def solution(mesh):
-    fine = Mesh(mesh.devices.reshape(8, 2, 4, 4, 2), ("zz", "zp", "y", "x", "core"))
-    seq = ("zz", "zp", "y")
     in_specs = (
-        P(None, seq, MP),
-        P(seq, None, None),
-        P(seq, None),
-        P(None, MP),
-        P(MP, None),
-        P(MP, None),
+        P(None, "seq", "mp"),
+        P("seq", None, None),
+        P("seq", None),
+        P(None, "mp"),
+        P("mp", None),
+        P("mp", None),
         P(),
-        P(seq, None),
-        P(None, None, MP),
-        P(MP, None),
-    )
-    out_specs = P(None, seq, MP)
-    return jax.shard_map(local, mesh=fine, in_specs=in_specs, out_specs=out_specs, check_vma=False)
+        P("seq", None),
+        P(None, None, "mp"),
+        P("mp", None),
+    )
+    out_specs = P(None, "seq", "mp")
+    return jax.shard_map(local, mesh=mesh, in_specs=in_specs, out_specs=out_specs, check_vma=False)

time: 111 us -> 109 us (0.982)
  blocking collectives: 101 us -> 98.8 us
    all_to_all x7, blocking collectives: 101 us -> 95.1 us  [exchange(): lax.all_to_all(values, axis, 0, 0, axis_index_groups=groups, tiled=True)]
    all_gather x0 -> x1, blocking collectives: none -> 3.69 us  [local(): parts = lax.all_gather(part_sum, 'mp', axis_index_groups=CORES)]
    pallas_call x8 -> x9, Pallas kernels: 7.92 us -> 7.96 us  [call(): pl.pallas_call(kernel, out_shape=out, in_specs=[one] * len(args), out_spe...]
where the time goes in v6:
time: 109 us; the launch traced here: 108 us
  blocking collectives  98.8 us (91%)
  Pallas kernels  7.96 us (7%)
  local copies, waits for them, and re-layouts  1.6 us (1%)
    all_to_all x7, blocking collectives, exchange(): lax.all_to_all(values, axis, 0, 0, axis_index_groups=groups, tiled=True)  95.1 us
    pallas_call x9, Pallas kernels, call(): pl.pallas_call(kernel, out_shape=out, in_specs=[one] * len(args), out_spe...  7.96 us
    all_gather x1, blocking collectives, local(): parts = lax.all_gather(part_sum, 'mp', axis_index_groups=CORES)  3.69 us

profile of v6, /device:TPU:1, one launch (start us, length us, event | category | flops | bytes accessed | tf_op | source)
XLA Modules:
  0.0 108.4 jit_solution(6291514148454906688)
XLA Ops:
  0.0 0.0 copy-start.7
  0.0 0.7 copy-done.7
  0.7 0.0 copy-start.10
  0.7 0.9 copy-done.10
  1.6 0.0 copy-start
  1.6 0.0 copy-start.1
  1.6 0.3 shard_map.100.own
  1.8 15.0 %all_to_all.35.gathered = bf16[8,80,128]{2,1,0:T(8,128)(2,1)S(1)} all-to-all(bf16[8,80,128]{2,1,0:T(8,128)(2,1)S(1)} %shard_map.100.own), channel_id=1, replica_groups=mesh['seq'=64,'mp'=8] {'mp'}, dimensions={0} | all-to-all | bytes 327680 | tf_op jit(solution)/shard_map/all_to_all | solution.py:302
  16.8 0.0 copy-done
  16.8 0.0 copy-done.1
  16.8 0.0 copy-start.4
  16.8 1.4 %shard_map.101 = bf16[8,80,128]{2,1,0:T(8,128)(2,1)S(1)} custom-call(bf16[8,80,128]{2,1,0:T(8,128)(2,1)S(1)} %all_to_all.35.gathered, bf16[1280,640]{1,0:T(8,128)(2,1)S(1)} %copy-done, bf16[640,1280]{1,0:T(8,128)(2,1)S(1)} %copy-done.1), custom_call_target="tpu_custom_call" | custom-call | tf_op jit(solution)/shard_map/pallas_call | solution.py:286
  18.2 0.0 copy-start.2
  18.2 0.0 copy-start.3
  18.2 0.0 copy-start.6
  18.2 0.0 copy-start.8
  18.2 0.0 copy-start.9
  18.3 9.0 %all_to_all.36.terms = bf16[8,80,128]{2,1,0:T(8,128)(2,1)S(1)} all-to-all(bf16[8,80,128]{2,1,0:T(8,128)(2,1)S(1)} %shard_map.101), channel_id=1, replica_groups=mesh['seq'=64,'mp'=8] {'mp'}, dimensions={0} | all-to-all | bytes 327680 | tf_op jit(solution)/shard_map/all_to_all | solution.py:302
  27.3 0.0 copy-done.4
  27.3 0.2 shard_map.102
  27.5 7.9 %all_to_all.37.parts = bf16[4,64,512]{2,1,0:T(8,128)(2,1)S(1)} all-to-all(bf16[4,64,512]{2,1,0:T(8,128)(2,1)S(1)} %shard_map.102), channel_id=1, replica_groups={{0,2,4,6},{1,3,5,7},{8,10,12,14},{9,11,13,15},{16,18,20,22},{17,19,21,2..., dimensions={0} | all-to-all | bytes 524288 | tf_op jit(solution)/shard_map/all_to_all | solution.py:302
  35.5 3.7 %all-gather = f32[128,512]{1,0:T(8,128)S(1)} all-gather(f32[64,512]{1,0:T(8,128)S(1)} %shard_map.103), channel_id=2, replica_groups={{0,1},{2,3},{4,5},{6,7},{8,9},{10,11},{12,13},{14,15},{16,17},{18,19},{..., dimensions={0}, use_global_device_ids=true | all-gather | bytes 393216 | tf_op jit(solution)/shard_map/all_gather | solution.py:336
  39.2 0.0 copy-start.5
  39.2 0.0 copy-done.2
  39.2 0.0 copy-done.3
  39.2 0.0 copy-done.6
  39.2 0.0 copy-done.8
  39.2 0.0 copy-done.9
  39.2 0.7 shard_map.104
  39.9 9.8 %all_to_all.38.group.queries = bf16[8,136,128]{2,1,0:T(8,128)(2,1)S(1)} all-to-all(bf16[8,136,128]{2,1,0:T(8,128)(2,1)S(1)} %get-tuple-element.7), channel_id=1, replica_groups={{0,8,16,24,32,40,48,56},{64,72,80,88,96,104,112,120},{128,136,144,152,1..., dimensions={0} | all-to-all | bytes 557056 | tf_op jit(solution)/shard_map/all_to_all | solution.py:302
  49.8 26.8 %all_to_all.39.column = bf16[8,136,128]{2,1,0:T(8,128)(2,1)S(1)} all-to-all(bf16[8,136,128]{2,1,0:T(8,128)(2,1)S(1)} %shard_map.105), channel_id=1, replica_groups={{0,64,128,192,288,352,416,480},{8,72,136,200,296,360,424,488},{16,80,14..., dimensions={0} | all-to-all | bytes 557056 | tf_op jit(solution)/shard_map/all_to_all | solution.py:302
  76.6 3.9 %shard_map.106 = bf16[8,80,128]{2,1,0:T(8,128)(2,1)S(1)} custom-call(bf16[8,136,128]{2,1,0:T(8,128)(2,1)S(1)} %all_to_all.38.group.queries, bf16[8,136,128]{2,1,0:T(8,128)(2,1)S(1)} %all_to_all.39.column), custom_call_target="tpu_custom_call" | custom-call | tf_op jit(solution)/shard_map/pallas_call | solution.py:286
  80.5 14.5 %all_to_all.40.message = bf16[8,80,128]{2,1,0:T(8,128)(2,1)S(1)} all-to-all(bf16[8,80,128]{2,1,0:T(8,128)(2,1)S(1)} %shard_map.106), channel_id=1, replica_groups={{0,8,16,24,32,40,48,56},{64,72,80,88,96,104,112,120},{128,136,144,152,1..., dimensions={0} | all-to-all | bytes 327680 | tf_op jit(solution)/shard_map/all_to_all | solution.py:302
  95.0 0.0 copy-done.5
  95.0 0.3 shard_map.107
  95.3 12.0 %all_to_all.41.terms = bf16[8,64,256]{2,1,0:T(8,128)(2,1)S(1)} all-to-all(bf16[8,64,256]{2,1,0:T(8,128)(2,1)S(1)} %shard_map.107), channel_id=1, replica_groups=mesh['seq'=64,'mp'=8] {'mp'}, dimensions={0} | all-to-all | bytes 524288 | tf_op jit(solution)/shard_map/all_to_all | solution.py:302
  107.3 1.1 %shard_map.108 = bf16[4,64,64]{2,1,0:T(8,128)(2,1)} custom-call(bf16[8,64,256]{2,1,0:T(8,128)(2,1)S(1)} %all_to_all.41.terms, s32[1,64]{1,0:T(1,128)S(1)} %bitcast.8, s32[1,64]{1,0:T(1,128)S(1)} %copy-done.9, bf16[512]{0:T(512)(128)(2,1)S(1)} %copy-done.6, bf16[64,512]{1,0:T(8,128)(2,1)S(1)} %copy-done.2, bf16[64,512]{1,0:T(8,128)(2,1)S(1)} %get-tuple-element.8.slot_in), custom_call_target="tpu_custom_call" | custom-call | tf_op jit(solution)/shard_map/pallas_call | solution.py:286
  (2 shorter events, 0.1 us)
Async XLA Ops:
  0.0 0.7 copy-start.7
  0.7 0.9 copy-start.10
  1.6 15.3 %copy-start = (bf16[1280,640]{1,0:T(8,128)(2,1)S(1)}, bf16[1280,640]{1,0:T(8,128)(2,1)}, u32[]{:S(2)}) copy-start(bf16[1280,640]{1,0:T(8,128)(2,1)} %w_in.1) | copy-start | bytes 4915204
  1.6 15.3 %copy-start.1 = (bf16[640,1280]{1,0:T(8,128)(2,1)S(1)}, bf16[640,1280]{1,0:T(8,128)(2,1)}, u32[]{:S(2)}) copy-start(bf16[640,1280]{1,0:T(8,128)(2,1)} %w_out.1) | copy-start | bytes 4915204
  16.8 10.4 %copy-start.4 = (bf16[160,512]{1,0:T(8,128)(2,1)S(1)}, bf16[160,512]{1,0:T(8,128)(2,1)}, u32[]{:S(2)}) copy-start(bf16[160,512]{1,0:T(8,128)(2,1)} %w_embed.1) | copy-start | bytes 491524
  18.2 21.0 %copy-start.2 = (bf16[64,512]{1,0:T(8,128)(2,1)S(1)}, bf16[64,512]{1,0:T(8,128)(2,1)}, u32[]{:S(2)}) copy-start(bf16[64,512]{1,0:T(8,128)(2,1)} %positions.3) | copy-start | bytes 196612
  18.2 21.0 %copy-start.3 = (bf16[512,3,64]{0,2,1:T(8,128)(2,1)S(1)}, bf16[512,3,64]{0,2,1:T(8,128)(2,1)}, u32[]{:S(2)}) copy-start(bf16[512,3,64]{0,2,1:T(8,128)(2,1)} %param.18) | copy-start | bytes 589828
  18.2 21.0 %copy-start.6 = (bf16[512]{0:T(512)(128)(2,1)S(1)}, bf16[512]{0:T(512)(128)(2,1)}, u32[]{:S(2)}) copy-start(bf16[512]{0:T(512)(128)(2,1)} %mask_token.3) | copy-start | bytes 3076
  18.2 20.9 %copy-start.8 = (s32[1,64,1]{1,2,0:T(1,128)S(1)}, s32[1,64,1]{1,2,0:T(1,128)}, u32[]{:S(2)}) copy-start(s32[1,64,1]{1,2,0:T(1,128)} %param.11) | copy-start | bytes 772
  18.2 20.9 %copy-start.9 = (s32[1,64]{1,0:T(1,128)S(1)}, s32[1,64]{1,0:T(1,128)}, u32[]{:S(2)}) copy-start(s32[1,64]{1,0:T(1,128)} %counts.3) | copy-start | bytes 772
  39.2 55.9 %copy-start.5 = (bf16[64,512]{1,0:T(8,128)(2,1)S(1)}, bf16[64,512]{1,0:T(8,128)(2,1)}, u32[]{:S(2)}) copy-start(bf16[64,512]{1,0:T(8,128)(2,1)} %w_attn_out.1) | copy-start | bytes 196612

commit v7 on v6

--- a/solution.py
+++ b/solution.py
@@ -11,7 +11,9 @@
 HDIM = 32
 NY = 4
 NZ = 16
-GROUP = [[(2 * k + p) * NY + y for p in range(2) for y in range(NY)] for k in range(NZ // 2)]
+GROUP = [[(2 * k + p) * NY + y for y in range(NY) for p in range(2)] for k in range(NZ // 2)]
+PAIR = [[(2 * k + p) * NY + y for p in range(2)] for k in range(NZ // 2) for y in range(NY)]
+ALONG_Y = [[z * NY + y for y in range(NY)] for z in range(NZ)]
 COLUMN = [
     [z * NY + y for z in range(NZ) if (z + z // (NZ // 2)) % 2 == head]
     for head in range(2)
@@ -147,19 +149,17 @@
         cols = slice(256 + 64 * head, 256 + 64 * head + 64)
         block = jnp.concatenate([masked[:, cols], proj[:, cols]], axis=1)
         block = jnp.concatenate([query, block, extra], axis=0)
-        plane = jnp.where(turn == 0, head, 1 - head)
-        for k in range(NY):
-            out[NY * plane + k] = block
-
-
-def pair_kernel(group, out):
-    y = lax.axis_index("seq") % NY
-    first, second = group[y], group[NY + y]
+        out[jnp.where(turn == 0, head, 1 - head)] = block
+
+
+def pair_kernel(pair, q_out, kv_out):
+    first, second = pair[0], pair[1]
+    q_out[...] = jnp.concatenate([first[:64], second[:64]], axis=0)
     odd = iota((8, 128), 0) % 2 == 1
     ids = jnp.where(odd, second[128:].astype(F32), first[128:].astype(F32)).astype(BF)
     block = jnp.concatenate([first[64:128], second[64:128], ids], axis=0)
-    for k in range(out.shape[0]):
-        out[k] = block
+    for k in range(kv_out.shape[0]):
+        kv_out[k] = block
 
 
 def own_rows(start, lists, counts, mask_token, positions, slot_in, feats, rows):
@@ -186,7 +186,8 @@
 
 
 def attend_kernel(queries, column, out, kv_scr, msg_scr):
-    blocks, tubs = queries.shape[0], 64
+    tubs = 64
+    blocks = queries.shape[0] * queries.shape[1] // tubs
     nz = 2 * column.shape[0]
     vols = 4
     rows = vols * tubs
@@ -205,7 +206,7 @@
         mat = jnp.where(seen, placed, other).astype(BF)
         for v in range(vols):
             kv_scr[v, k * tubs : (k + 1) * tubs, :] = mat[v * tubs : (v + 1) * tubs]
-    packed = queries[:, :tubs, :].reshape(blocks * tubs, 128)
+    packed = queries[...].reshape(blocks * tubs, 128)
     scale = math.log2(math.e) / math.sqrt(HDIM)
 
     def score(v):
@@ -248,14 +249,14 @@
         sides = []
         for u in range(2):
             stats = [
-                message[NY * plane + k, 64:, :].astype(F32)[8 * u : 8 * u + 8] for k in range(NY)
+                message[2 * k + plane, 64:, :].astype(F32)[8 * u : 8 * u + 8] for k in range(NY)
             ]
             tops = [s[0:1] + s[1:2] + s[2:3] for s in stats]
             best = functools.reduce(jnp.maximum, tops)
             fades = [jnp.exp2(t - best) for t in tops]
             total = sum(f * (s[3:4] + s[4:5]) for f, s in zip(fades, stats))
             value = sum(
-                f * message[NY * plane + k, HDIM * u : HDIM * u + HDIM, :].astype(F32)
+                f * message[2 * k + plane, HDIM * u : HDIM * u + HDIM, :].astype(F32)
                 for k, f in enumerate(fades)
             )
             sides.append(value / total)
@@ -334,17 +335,22 @@
     parts = exchange(parts, "mp", ALONG_X)
     part_sum = call(join_kernel, shape(slots, dec, dtype=F32), parts)
     parts = lax.all_gather(part_sum, "mp", axis_index_groups=CORES)
-    slot_in, group = call(
+    slot_in, pair = call(
         project_kernel,
-        [shape(slots, dec), shape(ngroup, 136, 128)],
+        [shape(slots, dec), shape(2, 136, 128)],
         parts, lists, counts, mask_token, positions, w_rows,
     )
-    group = exchange(group, "seq", GROUP)
-    column = exchange(call(pair_kernel, shape(ncolumn, 136, 128), group), "seq", COLUMN)
+    queries, column = call(
+        pair_kernel,
+        [shape(2 * tubs, 128), shape(ncolumn, 136, 128)],
+        exchange(pair, "seq", PAIR),
+    )
+    column = exchange(column, "seq", COLUMN)
+    queries = lax.all_gather(queries, "seq", axis_index_groups=ALONG_Y)
     message = call(
         attend_kernel,
         shape(ngroup, 80, 128),
-        group,
+        queries,
         column,
         scratch=[pltpu.VMEM((vols, 2 * ncolumn * tubs, 64), BF), pltpu.VMEM((ngroup, 80, 128), F32)],
     )

time: 109 us -> 105 us (0.963)
  blocking collectives: 98.8 us -> 79.6 us
  starting transfers between devices: 0 us -> 10 us
  waiting for transfers between devices: 0 us -> 4.31 us
    all_to_all x7 -> x6, blocking collectives: 95.1 us -> 66 us  [exchange(): lax.all_to_all(values, axis, 0, 0, axis_index_groups=groups, tiled=True)]
    all_to_all x0 -> x1, starting transfers between devices: none -> 10 us  [exchange(): lax.all_to_all(values, axis, 0, 0, axis_index_groups=groups, tiled=True)]
    all_gather x0 -> x1, blocking collectives: none -> 9.88 us  [local(): queries = lax.all_gather(queries, 'seq', axis_index_groups=ALONG_Y)]
    all_to_all x0 -> x1, waiting for transfers between devices: none -> 4.31 us  [exchange(): lax.all_to_all(values, axis, 0, 0, axis_index_groups=groups, tiled=True)]
  transfers between devices with their start and end apart: 0 -> 1, of which waited for: 0 -> 1; matrix products, arithmetic and copies ran while one was open for 0% -> 0% of each run, Pallas kernels for 0% -> 0%
where the time goes in v7:
time: 105 us; the launch traced here: 104 us
  blocking collectives  79.6 us (76%)
  starting transfers between devices  10 us (10%)
  Pallas kernels  8.67 us (8%)
  waiting for transfers between devices  4.31 us (4%)
  local copies, waits for them, and re-layouts  1.6 us (2%)
    all_to_all x6, blocking collectives, exchange(): lax.all_to_all(values, axis, 0, 0, axis_index_groups=groups, tiled=True)  66 us
    all_to_all x1, starting transfers between devices, exchange(): lax.all_to_all(values, axis, 0, 0, axis_index_groups=groups, tiled=True)  10 us
    all_gather x1, blocking collectives, local(): queries = lax.all_gather(queries, 'seq', axis_index_groups=ALONG_Y)  9.88 us
    pallas_call x9, Pallas kernels, call(): pl.pallas_call(kernel, out_shape=out, in_specs=[one] * len(args), out_spe...  8.67 us
    all_to_all x1, waiting for transfers between devices, exchange(): lax.all_to_all(values, axis, 0, 0, axis_index_groups=groups, tiled=True)  4.31 us
    all_gather x1, blocking collectives, local(): parts = lax.all_gather(part_sum, 'mp', axis_index_groups=CORES)  3.69 us
  transfers between devices with their start and end apart: 1, of which 1 were waited for; matrix products, arithmetic and copies ran while one was open for 0% of the time, Pallas kernels for 0%

profile of v7, /device:TPU:1, one launch (start us, length us, event | category | flops | bytes accessed | tf_op | source)
XLA Modules:
  0.0 104.3 jit_solution(4599273148989439813)
XLA Ops:
  0.0 0.0 copy-start.7
  0.0 0.7 copy-done.7
  0.7 0.0 copy-start.10
  0.7 0.9 copy-done.10
  1.6 0.0 copy-start
  1.6 0.0 copy-start.1
  1.6 0.3 shard_map.100.own
  1.8 15.0 %all_to_all.35.gathered = bf16[8,80,128]{2,1,0:T(8,128)(2,1)S(1)} all-to-all(bf16[8,80,128]{2,1,0:T(8,128)(2,1)S(1)} %shard_map.100.own), channel_id=1, replica_groups=mesh['seq'=64,'mp'=8] {'mp'}, dimensions={0} | all-to-all | bytes 327680 | tf_op jit(solution)/shard_map/all_to_all | solution.py:303
  16.8 0.0 copy-done
  16.8 0.0 copy-done.1
  16.8 0.0 copy-start.4
  16.8 1.4 %shard_map.101 = bf16[8,80,128]{2,1,0:T(8,128)(2,1)S(1)} custom-call(bf16[8,80,128]{2,1,0:T(8,128)(2,1)S(1)} %all_to_all.35.gathered, bf16[1280,640]{1,0:T(8,128)(2,1)S(1)} %copy-done, bf16[640,1280]{1,0:T(8,128)(2,1)S(1)} %copy-done.1), custom_call_target="tpu_custom_call" | custom-call | tf_op jit(solution)/shard_map/pallas_call | solution.py:287
  18.2 0.0 copy-start.2
  18.2 0.0 copy-start.3
  18.2 0.0 copy-start.6
  18.2 0.0 copy-start.8
  18.2 0.0 copy-start.9
  18.3 9.0 %all_to_all.36.terms = bf16[8,80,128]{2,1,0:T(8,128)(2,1)S(1)} all-to-all(bf16[8,80,128]{2,1,0:T(8,128)(2,1)S(1)} %shard_map.101), channel_id=1, replica_groups=mesh['seq'=64,'mp'=8] {'mp'}, dimensions={0} | all-to-all | bytes 327680 | tf_op jit(solution)/shard_map/all_to_all | solution.py:303
  27.3 0.0 copy-done.4
  27.3 0.2 shard_map.102
  27.5 7.9 %all_to_all.37.parts = bf16[4,64,512]{2,1,0:T(8,128)(2,1)S(1)} all-to-all(bf16[4,64,512]{2,1,0:T(8,128)(2,1)S(1)} %shard_map.102), channel_id=1, replica_groups={{0,2,4,6},{1,3,5,7},{8,10,12,14},{9,11,13,15},{16,18,20,22},{17,19,21,2..., dimensions={0} | all-to-all | bytes 524288 | tf_op jit(solution)/shard_map/all_to_all | solution.py:303
  35.4 0.0 copy-start.5
  35.5 3.7 %all-gather = f32[128,512]{1,0:T(8,128)S(1)} all-gather(f32[64,512]{1,0:T(8,128)S(1)} %shard_map.103), channel_id=2, replica_groups={{0,1},{2,3},{4,5},{6,7},{8,9},{10,11},{12,13},{14,15},{16,17},{18,19},{..., dimensions={0}, use_global_device_ids=true | all-gather | bytes 393216 | tf_op jit(solution)/shard_map/all_gather | solution.py:337
  39.2 0.0 copy-done.2
  39.2 0.0 copy-done.3
  39.2 0.0 copy-done.6
  39.2 0.0 copy-done.8
  39.2 0.0 copy-done.9
  39.2 0.7 shard_map.104
  39.9 5.4 %all_to_all.38.pair = bf16[2,136,128]{2,1,0:T(8,128)(2,1)S(1)} all-to-all(bf16[2,136,128]{2,1,0:T(8,128)(2,1)S(1)} %get-tuple-element.9), channel_id=1, replica_groups={{0,32},{8,40},{16,48},{24,56},{64,96},{72,104},{80,112},{88,120},{128,1..., dimensions={0} | all-to-all | bytes 139264 | tf_op jit(solution)/shard_map/all_to_all | solution.py:303
  45.3 0.7 shard_map.105
  46.0 10.0 %all-to-all-start.4 = ((bf16[8,136,128]{2,1,0:T(8,128)(2,1)}), bf16[8,136,128]{2,1,0:T(8,128)(2,1)S(1)}, u32[]{:S(2)}, u32[]{:S(2)}) async-start(bf16[8,136,128]{2,1,0:T(8,128)(2,1)} %get-tuple-element.11), calls=%async_computation.4 | async-start | bytes 557056 | tf_op jit(solution)/shard_map/all_to_all | solution.py:303
  56.0 9.9 %all-gather.1 = bf16[512,128]{1,0:T(8,128)(2,1)S(1)} all-gather(bf16[128,128]{1,0:T(8,128)(2,1)S(1)} %get-tuple-element.10), channel_id=3, replica_groups={{0,8,16,24},{32,40,48,56},{64,72,80,88},{96,104,112,120},{128,136,144,1..., dimensions={0}, use_global_device_ids=true | all-gather | bytes 163840 | tf_op jit(solution)/shard_map/all_gather | solution.py:349
  65.9 4.3 %all-to-all-done.4.column = bf16[8,136,128]{2,1,0:T(8,128)(2,1)S(1)} async-done(((bf16[8,136,128]{2,1,0:T(8,128)(2,1)}), bf16[8,136,128]{2,1,0:T(8,128)(2,1)S(1)}, u32[]{:S(2)}, u32[]{:S(2)}) %all-to-all-start.4) | async-done | bytes 278560 | tf_op jit(solution)/shard_map/all_to_all | solution.py:303
  70.2 3.9 %shard_map.106 = bf16[8,80,128]{2,1,0:T(8,128)(2,1)S(1)} custom-call(bf16[4,128,128]{2,1,0:T(8,128)(2,1)S(1)} %bitcast.6, bf16[8,136,128]{2,1,0:T(8,128)(2,1)S(1)} %all-to-all-done.4.column), custom_call_target="tpu_custom_call" | custom-call | tf_op jit(solution)/shard_map/pallas_call | solution.py:287
  74.1 16.4 %all_to_all.39.message = bf16[8,80,128]{2,1,0:T(8,128)(2,1)S(1)} all-to-all(bf16[8,80,128]{2,1,0:T(8,128)(2,1)S(1)} %shard_map.106), channel_id=1, replica_groups={{0,32,8,40,16,48,24,56},{64,96,72,104,80,112,88,120},{128,160,136,168,1..., dimensions={0} | all-to-all | bytes 327680 | tf_op jit(solution)/shard_map/all_to_all | solution.py:303
  90.5 0.0 copy-done.5
  90.5 0.3 shard_map.107
  90.8 12.3 %all_to_all.40.terms = bf16[8,64,256]{2,1,0:T(8,128)(2,1)S(1)} all-to-all(bf16[8,64,256]{2,1,0:T(8,128)(2,1)S(1)} %shard_map.107), channel_id=1, replica_groups=mesh['seq'=64,'mp'=8] {'mp'}, dimensions={0} | all-to-all | bytes 524288 | tf_op jit(solution)/shard_map/all_to_all | solution.py:303
  103.2 1.1 %shard_map.108 = bf16[4,64,64]{2,1,0:T(8,128)(2,1)} custom-call(bf16[8,64,256]{2,1,0:T(8,128)(2,1)S(1)} %all_to_all.40.terms, s32[1,64]{1,0:T(1,128)S(1)} %bitcast.10, s32[1,64]{1,0:T(1,128)S(1)} %copy-done.9, bf16[512]{0:T(512)(128)(2,1)S(1)} %copy-done.6, bf16[64,512]{1,0:T(8,128)(2,1)S(1)} %copy-done.2, bf16[64,512]{1,0:T(8,128)(2,1)S(1)} %get-tuple-element.12.slot_in), custom_call_target="tpu_custom_call" | custom-call | tf_op jit(solution)/shard_map/pallas_call | solution.py:287
  (1 shorter events, 0.0 us)
Async XLA Ops:
  0.0 0.7 copy-start.7
  0.7 0.9 copy-start.10
  1.6 15.3 %copy-start = (bf16[1280,640]{1,0:T(8,128)(2,1)S(1)}, bf16[1280,640]{1,0:T(8,128)(2,1)}, u32[]{:S(2)}) copy-start(bf16[1280,640]{1,0:T(8,128)(2,1)} %w_in.1) | copy-start | bytes 4915204
  1.6 15.3 %copy-start.1 = (bf16[640,1280]{1,0:T(8,128)(2,1)S(1)}, bf16[640,1280]{1,0:T(8,128)(2,1)}, u32[]{:S(2)}) copy-start(bf16[640,1280]{1,0:T(8,128)(2,1)} %w_out.1) | copy-start | bytes 4915204
  16.8 10.4 %copy-start.4 = (bf16[160,512]{1,0:T(8,128)(2,1)S(1)}, bf16[160,512]{1,0:T(8,128)(2,1)}, u32[]{:S(2)}) copy-start(bf16[160,512]{1,0:T(8,128)(2,1)} %w_embed.1) | copy-start | bytes 491524
  18.2 21.0 %copy-start.2 = (bf16[64,512]{1,0:T(8,128)(2,1)S(1)}, bf16[64,512]{1,0:T(8,128)(2,1)}, u32[]{:S(2)}) copy-start(bf16[64,512]{1,0:T(8,128)(2,1)} %positions.3) | copy-start | bytes 196612
  18.2 21.0 %copy-start.3 = (bf16[512,3,64]{0,2,1:T(8,128)(2,1)S(1)}, bf16[512,3,64]{0,2,1:T(8,128)(2,1)}, u32[]{:S(2)}) copy-start(bf16[512,3,64]{0,2,1:T(8,128)(2,1)} %param.18) | copy-start | bytes 589828
  18.2 21.0 %copy-start.6 = (bf16[512]{0:T(512)(128)(2,1)S(1)}, bf16[512]{0:T(512)(128)(2,1)}, u32[]{:S(2)}) copy-start(bf16[512]{0:T(512)(128)(2,1)} %mask_token.3) | copy-start | bytes 3076
  18.2 20.9 %copy-start.8 = (s32[1,64,1]{1,2,0:T(1,128)S(1)}, s32[1,64,1]{1,2,0:T(1,128)}, u32[]{:S(2)}) copy-start(s32[1,64,1]{1,2,0:T(1,128)} %param.11) | copy-start | bytes 772
  18.2 20.9 %copy-start.9 = (s32[1,64]{1,0:T(1,128)S(1)}, s32[1,64]{1,0:T(1,128)}, u32[]{:S(2)}) copy-start(s32[1,64]{1,0:T(1,128)} %counts.3) | copy-start | bytes 772
  35.4 55.1 %copy-start.5 = (bf16[64,512]{1,0:T(8,128)(2,1)S(1)}, bf16[64,512]{1,0:T(8,128)(2,1)}, u32[]{:S(2)}) copy-start(bf16[64,512]{1,0:T(8,128)(2,1)} %w_attn_out.1) | copy-start | bytes 196612
  46.0 24.2 %all-to-all-start.4 = ((bf16[8,136,128]{2,1,0:T(8,128)(2,1)}), bf16[8,136,128]{2,1,0:T(8,128)(2,1)S(1)}, u32[]{:S(2)}, u32[]{:S(2)}) async-start(bf16[8,136,128]{2,1,0:T(8,128)(2,1)} %get-tuple-element.11), calls=%async_computation.4 | async-start | bytes 557056 | tf_op jit(solution)/shard_map/all_to_all | solution.py:303

commit v8 on v7

--- a/solution.py
+++ b/solution.py
@@ -141,7 +141,6 @@
     zero = jnp.zeros((slots, 128), BF)
     extra = jnp.concatenate([ids_row.astype(F32), jnp.zeros((1, 128 - slots), F32)], axis=1)
     extra = jnp.broadcast_to(extra, (8, 128)).astype(BF)
-    turn = plane_turn()
     for head in range(2):
         cols = slice(128 * head, 128 * head + 128)
         placed = dot(spot, jnp.where(of_volume, proj[:, cols], zero))
@@ -149,11 +148,12 @@
         cols = slice(256 + 64 * head, 256 + 64 * head + 64)
         block = jnp.concatenate([masked[:, cols], proj[:, cols]], axis=1)
         block = jnp.concatenate([query, block, extra], axis=0)
-        out[jnp.where(turn == 0, head, 1 - head)] = block
+        out[head] = block
 
 
 def pair_kernel(pair, q_out, kv_out):
-    first, second = pair[0], pair[1]
+    head = (lax.axis_index("seq") // NY + plane_turn()) % 2
+    first, second = pair[0, head], pair[1, head]
     q_out[...] = jnp.concatenate([first[:64], second[:64]], axis=0)
     odd = iota((8, 128), 0) % 2 == 1
     ids = jnp.where(odd, second[128:].astype(F32), first[128:].astype(F32)).astype(BF)
@@ -162,9 +162,11 @@
         kv_out[k] = block
 
 
-def own_rows(start, lists, counts, mask_token, positions, slot_in, feats, rows):
+def own_kernel(lists, counts, mask_token, positions, slot_in, out):
     tubs, dec = positions.shape
+    feats, rows = out.shape
     slots = lists.shape[1]
+    start = lax.axis_index("mp") * feats
     ids = column_of(live_row(lists[...], counts[...], rows))
     choose = (iota((dec, feats), 0) == iota((dec, feats), 1) + start).astype(F32).astype(BF)
     mask_in = (mask_token[...].astype(F32).reshape(1, -1) + positions[...].astype(F32)).astype(BF)
@@ -173,7 +175,8 @@
     picked = (ids == iota((slots, rows), 1)).astype(F32)
     seen = jnp.sum(picked, axis=0, keepdims=True) > 0
     tile = (iota((tubs, rows), 0) == iota((tubs, rows), 1) % tubs).astype(F32).astype(BF)
-    return jnp.where(seen, dot_tn(slot_own, picked.astype(BF)), dot_tn(mask_own, tile))
+    rows_own = jnp.where(seen, dot_tn(slot_own, picked.astype(BF)), dot_tn(mask_own, tile))
+    out[...] = rows_own.astype(BF)
 
 
 def split_pieces(values, count):
@@ -185,7 +188,7 @@
     return out
 
 
-def attend_kernel(queries, column, out, kv_scr, msg_scr):
+def attend_kernel(queries, column, out, kv_scr, ones_scr, msg_scr):
     tubs = 64
     blocks = queries.shape[0] * queries.shape[1] // tubs
     nz = 2 * column.shape[0]
@@ -204,8 +207,10 @@
         other = block[:, :64].astype(F32)
         other = jnp.concatenate([other] * vols, axis=0)
         mat = jnp.where(seen, placed, other).astype(BF)
+        ones = jnp.where(iota(mat.shape, 1) < HDIM, jnp.ones_like(mat), mat)
         for v in range(vols):
             kv_scr[v, k * tubs : (k + 1) * tubs, :] = mat[v * tubs : (v + 1) * tubs]
+            ones_scr[v, k * tubs : (k + 1) * tubs, :] = ones[v * tubs : (v + 1) * tubs]
     packed = queries[...].reshape(blocks * tubs, 128)
     scale = math.log2(math.e) / math.sqrt(HDIM)
 
@@ -217,10 +222,11 @@
     def weigh(scores):
         top = jnp.max(scores, axis=0, keepdims=True)
         weights = jnp.exp2((scores - top) * scale)
-        return top, jnp.sum(weights, axis=0, keepdims=True), weights.astype(BF)
-
-    def put(v, top, total, weights):
-        summed = dot_tn(kv_scr[v], weights)[HDIM:]
+        return top, weights.astype(BF)
+
+    def put(v, top, weights):
+        both = dot_tn(ones_scr[v], weights)
+        total, summed = both[:1], both[HDIM:]
         stats = split_pieces(top * scale, 3) + split_pieces(total, 2)
         stats = jnp.concatenate(stats + [jnp.zeros((3, blocks * tubs), F32)], axis=0)
         half, side = v // 2, slice(64 * (v % 2), 64 * (v % 2) + 64)
@@ -268,12 +274,9 @@
         out[k] = terms[k * feats : (k + 1) * feats]
 
 
-def finish_kernel(terms, lists, counts, mask_token, positions, slot_in, out):
-    vols, tubs, feats = out.shape
-    start = lax.axis_index("mp") * feats
-    total = own_rows(start, lists, counts, mask_token, positions, slot_in, feats, vols * tubs)
-    total = total + sum(terms[k].astype(F32) for k in range(terms.shape[0]))
-    out[...] = total.T.astype(BF).reshape(vols, tubs, feats)
+def finish_kernel(terms, dec_own, out):
+    total = dec_own[...].astype(F32) + sum(terms[k].astype(F32) for k in range(terms.shape[0]))
+    out[...] = total.T.astype(BF).reshape(out.shape)
 
 
 def call(kernel, out, *args, scratch=(), micros=0):
@@ -343,25 +346,29 @@
     queries, column = call(
         pair_kernel,
         [shape(2 * tubs, 128), shape(ncolumn, 136, 128)],
-        exchange(pair, "seq", PAIR),
+        lax.all_gather(pair, "seq", axis_index_groups=PAIR),
     )
     column = exchange(column, "seq", COLUMN)
     queries = lax.all_gather(queries, "seq", axis_index_groups=ALONG_Y)
+    dec_own = call(
+        own_kernel, shape(feats, rows), lists, counts, mask_token, positions, slot_in
+    )
+    queries, dec_own = lax.optimization_barrier((queries, dec_own))
     message = call(
         attend_kernel,
         shape(ngroup, 80, 128),
         queries,
         column,
-        scratch=[pltpu.VMEM((vols, 2 * ncolumn * tubs, 64), BF), pltpu.VMEM((ngroup, 80, 128), F32)],
+        scratch=[
+            pltpu.VMEM((vols, 2 * ncolumn * tubs, 64), BF),
+            pltpu.VMEM((vols, 2 * ncolumn * tubs, 64), BF),
+            pltpu.VMEM((ngroup, 80, 128), F32),
+        ],
     )
     message = exchange(message, "seq", GROUP)
     head_terms = call(combine_kernel, shape(nmp, feats, rows), message, w_attn_out)
     head_terms = exchange(head_terms, "mp")
-    return call(
-        finish_kernel,
-        shape(vols, tubs, feats),
-        head_terms, lists, counts, mask_token, positions, slot_in,
-    )
+    return call(finish_kernel, shape(vols, tubs, feats), head_terms, dec_own)
 
 
 def solution(mesh):

time: 105 us -> 103 us (0.981)
  blocking collectives: 79.6 us -> 75.6 us
  waiting for transfers between devices: 4.31 us -> 6.01 us
    all_to_all x6 -> x5, blocking collectives: 66 us -> 58 us  [exchange(): lax.all_to_all(values, axis, 0, 0, axis_index_groups=groups, tiled=True)]
    all_gather x0 -> x1, blocking collectives: none -> 3.84 us  [local(): lax.all_gather(pair, 'seq', axis_index_groups=PAIR)]
    all_to_all x1, waiting for transfers between devices: 4.31 us -> 6.01 us  [exchange(): lax.all_to_all(values, axis, 0, 0, axis_index_groups=groups, tiled=True)]
    pallas_call x9 -> x10, Pallas kernels: 8.67 us -> 8.43 us  [call(): pl.pallas_call(kernel, out_shape=out, in_specs=[one] * len(args), out_spe...]
where the time goes in v8:
time: 103 us; the launch traced here: 102 us
  blocking collectives  75.6 us (73%)
  starting transfers between devices  10.7 us (10%)
  Pallas kernels  8.43 us (8%)
  waiting for transfers between devices  6.01 us (6%)
  local copies, waits for them, and re-layouts  1.6 us (2%)
    all_to_all x5, blocking collectives, exchange(): lax.all_to_all(values, axis, 0, 0, axis_index_groups=groups, tiled=True)  58 us
    all_to_all x1, starting transfers between devices, exchange(): lax.all_to_all(values, axis, 0, 0, axis_index_groups=groups, tiled=True)  10.7 us
    all_gather x1, blocking collectives, local(): queries = lax.all_gather(queries, 'seq', axis_index_groups=ALONG_Y)  10.1 us
    pallas_call x10, Pallas kernels, call(): pl.pallas_call(kernel, out_shape=out, in_specs=[one] * len(args), out_spe...  8.43 us
    all_to_all x1, waiting for transfers between devices, exchange(): lax.all_to_all(values, axis, 0, 0, axis_index_groups=groups, tiled=True)  6.01 us
    all_gather x1, blocking collectives, local(): lax.all_gather(pair, 'seq', axis_index_groups=PAIR)  3.84 us
    all_gather x1, blocking collectives, local(): parts = lax.all_gather(part_sum, 'mp', axis_index_groups=CORES)  3.69 us
  transfers between devices with their start and end apart: 1, of which 1 were waited for; matrix products, arithmetic and copies ran while one was open for 0% of the time, Pallas kernels for 0%

profile of v8, /device:TPU:1, one launch (start us, length us, event | category | flops | bytes accessed | tf_op | source)
XLA Modules:
  0.0 102.4 jit_solution(13933483206064485888)
XLA Ops:
  0.0 0.0 copy-start.7
  0.0 0.7 copy-done.7
  0.7 0.0 copy-start.10
  0.7 0.9 copy-done.10
  1.6 0.0 copy-start
  1.6 0.0 copy-start.1
  1.6 0.3 shard_map.100.own
  1.8 15.0 %all_to_all.30.gathered = bf16[8,80,128]{2,1,0:T(8,128)(2,1)S(1)} all-to-all(bf16[8,80,128]{2,1,0:T(8,128)(2,1)S(1)} %shard_map.100.own), channel_id=1, replica_groups=mesh['seq'=64,'mp'=8] {'mp'}, dimensions={0} | all-to-all | bytes 327680 | tf_op jit(solution)/shard_map/all_to_all | solution.py:306
  16.8 0.0 copy-done
  16.8 0.0 copy-done.1
  16.8 0.0 copy-start.4
  16.8 1.4 %shard_map.101 = bf16[8,80,128]{2,1,0:T(8,128)(2,1)S(1)} custom-call(bf16[8,80,128]{2,1,0:T(8,128)(2,1)S(1)} %all_to_all.30.gathered, bf16[1280,640]{1,0:T(8,128)(2,1)S(1)} %copy-done, bf16[640,1280]{1,0:T(8,128)(2,1)S(1)} %copy-done.1), custom_call_target="tpu_custom_call" | custom-call | tf_op jit(solution)/shard_map/pallas_call | solution.py:290
  18.2 0.0 copy-start.2
  18.2 0.0 copy-start.3
  18.2 0.0 copy-start.6
  18.2 0.0 copy-start.8
  18.2 0.0 copy-start.9
  18.3 9.0 %all_to_all.31.terms = bf16[8,80,128]{2,1,0:T(8,128)(2,1)S(1)} all-to-all(bf16[8,80,128]{2,1,0:T(8,128)(2,1)S(1)} %shard_map.101), channel_id=1, replica_groups=mesh['seq'=64,'mp'=8] {'mp'}, dimensions={0} | all-to-all | bytes 327680 | tf_op jit(solution)/shard_map/all_to_all | solution.py:306
  27.3 0.0 copy-done.4
  27.3 0.2 shard_map.102
  27.5 7.9 %all_to_all.32.parts = bf16[4,64,512]{2,1,0:T(8,128)(2,1)S(1)} all-to-all(bf16[4,64,512]{2,1,0:T(8,128)(2,1)S(1)} %shard_map.102), channel_id=1, replica_groups={{0,2,4,6},{1,3,5,7},{8,10,12,14},{9,11,13,15},{16,18,20,22},{17,19,21,2..., dimensions={0} | all-to-all | bytes 524288 | tf_op jit(solution)/shard_map/all_to_all | solution.py:306
  35.4 0.0 copy-start.5
  35.5 3.7 %all-gather = f32[128,512]{1,0:T(8,128)S(1)} all-gather(f32[64,512]{1,0:T(8,128)S(1)} %shard_map.103), channel_id=2, replica_groups={{0,1},{2,3},{4,5},{6,7},{8,9},{10,11},{12,13},{14,15},{16,17},{18,19},{..., dimensions={0}, use_global_device_ids=true | all-gather | bytes 393216 | tf_op jit(solution)/shard_map/all_gather | solution.py:340
  39.2 0.0 copy-done.2
  39.2 0.0 copy-done.3
  39.2 0.0 copy-done.6
  39.2 0.0 copy-done.8
  39.2 0.0 copy-done.9
  39.2 0.7 shard_map.104
  39.9 3.8 %all-gather.1 = bf16[4,136,128]{2,1,0:T(8,128)(2,1)S(1)} all-gather(bf16[2,136,128]{2,1,0:T(8,128)(2,1)S(1)} %get-tuple-element.11), channel_id=3, replica_groups={{0,32},{8,40},{16,48},{24,56},{64,96},{72,104},{80,112},{88,120},{128,1..., dimensions={0}, use_global_device_ids=true | all-gather | bytes 208896 | tf_op jit(solution)/shard_map/all_gather | solution.py:349
  43.7 0.7 shard_map.105
  44.5 10.7 %all-to-all-start.3 = ((bf16[8,136,128]{2,1,0:T(8,128)(2,1)}), bf16[8,136,128]{2,1,0:T(8,128)(2,1)S(1)}, u32[]{:S(2)}, u32[]{:S(2)}) async-start(bf16[8,136,128]{2,1,0:T(8,128)(2,1)} %get-tuple-element.15), calls=%async_computation.3 | async-start | bytes 557056 | tf_op jit(solution)/shard_map/all_to_all | solution.py:306
  55.2 0.4 shard_map.106.dec_own
  55.6 10.1 %all-gather.2 = bf16[512,128]{1,0:T(8,128)(2,1)S(1)} all-gather(bf16[128,128]{1,0:T(8,128)(2,1)S(1)} %get-tuple-element.12), channel_id=4, replica_groups={{0,8,16,24},{32,40,48,56},{64,72,80,88},{96,104,112,120},{128,136,144,1..., dimensions={0}, use_global_device_ids=true | all-gather | bytes 163840 | tf_op jit(solution)/shard_map/all_gather | solution.py:352
  65.7 6.0 %all-to-all-done.3.column = bf16[8,136,128]{2,1,0:T(8,128)(2,1)S(1)} async-done(((bf16[8,136,128]{2,1,0:T(8,128)(2,1)}), bf16[8,136,128]{2,1,0:T(8,128)(2,1)S(1)}, u32[]{:S(2)}, u32[]{:S(2)}) %all-to-all-start.3) | async-done | bytes 278560 | tf_op jit(solution)/shard_map/all_to_all | solution.py:306
  71.7 3.6 %shard_map.107 = bf16[8,80,128]{2,1,0:T(8,128)(2,1)S(1)} custom-call(bf16[4,128,128]{2,1,0:T(8,128)(2,1)S(1)} %bitcast.8, bf16[8,136,128]{2,1,0:T(8,128)(2,1)S(1)} %all-to-all-done.3.column), custom_call_target="tpu_custom_call" | custom-call | tf_op jit(solution)/shard_map/pallas_call | solution.py:290
  75.3 10.5 %all_to_all.33.message = bf16[8,80,128]{2,1,0:T(8,128)(2,1)S(1)} all-to-all(bf16[8,80,128]{2,1,0:T(8,128)(2,1)S(1)} %shard_map.107), channel_id=1, replica_groups={{0,32,8,40,16,48,24,56},{64,96,72,104,80,112,88,120},{128,160,136,168,1..., dimensions={0} | all-to-all | bytes 327680 | tf_op jit(solution)/shard_map/all_to_all | solution.py:306
  85.8 0.0 copy-done.5
  85.8 0.3 shard_map.108
  86.1 15.6 %all_to_all.34.terms = bf16[8,64,256]{2,1,0:T(8,128)(2,1)S(1)} all-to-all(bf16[8,64,256]{2,1,0:T(8,128)(2,1)S(1)} %shard_map.108), channel_id=1, replica_groups=mesh['seq'=64,'mp'=8] {'mp'}, dimensions={0} | all-to-all | bytes 524288 | tf_op jit(solution)/shard_map/all_to_all | solution.py:306
  101.7 0.8 shard_map.109
  (1 shorter events, 0.0 us)
Async XLA Ops:
  0.0 0.7 copy-start.7
  0.7 0.9 copy-start.10
  1.6 15.3 %copy-start = (bf16[1280,640]{1,0:T(8,128)(2,1)S(1)}, bf16[1280,640]{1,0:T(8,128)(2,1)}, u32[]{:S(2)}) copy-start(bf16[1280,640]{1,0:T(8,128)(2,1)} %w_in.1) | copy-start | bytes 4915204
  1.6 15.3 %copy-start.1 = (bf16[640,1280]{1,0:T(8,128)(2,1)S(1)}, bf16[640,1280]{1,0:T(8,128)(2,1)}, u32[]{:S(2)}) copy-start(bf16[640,1280]{1,0:T(8,128)(2,1)} %w_out.1) | copy-start | bytes 4915204
  16.8 10.4 %copy-start.4 = (bf16[160,512]{1,0:T(8,128)(2,1)S(1)}, bf16[160,512]{1,0:T(8,128)(2,1)}, u32[]{:S(2)}) copy-start(bf16[160,512]{1,0:T(8,128)(2,1)} %w_embed.1) | copy-start | bytes 491524
  18.2 21.0 %copy-start.2 = (bf16[64,512]{1,0:T(8,128)(2,1)S(1)}, bf16[64,512]{1,0:T(8,128)(2,1)}, u32[]{:S(2)}) copy-start(bf16[64,512]{1,0:T(8,128)(2,1)} %positions.3) | copy-start | bytes 196612
  18.2 21.0 %copy-start.3 = (bf16[512,3,64]{0,2,1:T(8,128)(2,1)S(1)}, bf16[512,3,64]{0,2,1:T(8,128)(2,1)}, u32[]{:S(2)}) copy-start(bf16[512,3,64]{0,2,1:T(8,128)(2,1)} %param.18) | copy-start | bytes 589828
  18.2 21.0 %copy-start.6 = (bf16[512]{0:T(512)(128)(2,1)S(1)}, bf16[512]{0:T(512)(128)(2,1)}, u32[]{:S(2)}) copy-start(bf16[512]{0:T(512)(128)(2,1)} %mask_token.3) | copy-start | bytes 3076
  18.2 20.9 %copy-start.8 = (s32[1,64,1]{1,2,0:T(1,128)S(1)}, s32[1,64,1]{1,2,0:T(1,128)}, u32[]{:S(2)}) copy-start(s32[1,64,1]{1,2,0:T(1,128)} %param.11) | copy-start | bytes 772
  18.2 20.9 %copy-start.9 = (s32[1,64]{1,0:T(1,128)S(1)}, s32[1,64]{1,0:T(1,128)}, u32[]{:S(2)}) copy-start(s32[1,64]{1,0:T(1,128)} %counts.3) | copy-start | bytes 772
  35.4 50.4 %copy-start.5 = (bf16[64,512]{1,0:T(8,128)(2,1)S(1)}, bf16[64,512]{1,0:T(8,128)(2,1)}, u32[]{:S(2)}) copy-start(bf16[64,512]{1,0:T(8,128)(2,1)} %w_attn_out.1) | copy-start | bytes 196612
  44.5 27.2 %all-to-all-start.3 = ((bf16[8,136,128]{2,1,0:T(8,128)(2,1)}), bf16[8,136,128]{2,1,0:T(8,128)(2,1)S(1)}, u32[]{:S(2)}, u32[]{:S(2)}) async-start(bf16[8,136,128]{2,1,0:T(8,128)(2,1)} %get-tuple-element.15), calls=%async_computation.3 | async-start | bytes 557056 | tf_op jit(solution)/shard_map/all_to_all | solution.py:306

commit v9 on v8

--- a/solution.py
+++ b/solution.py
@@ -14,11 +14,9 @@
 GROUP = [[(2 * k + p) * NY + y for y in range(NY) for p in range(2)] for k in range(NZ // 2)]
 PAIR = [[(2 * k + p) * NY + y for p in range(2)] for k in range(NZ // 2) for y in range(NY)]
 ALONG_Y = [[z * NY + y for y in range(NY)] for z in range(NZ)]
-COLUMN = [
-    [z * NY + y for z in range(NZ) if (z + z // (NZ // 2)) % 2 == head]
-    for head in range(2)
-    for y in range(NY)
-]
+SIDES = [[z for z in range(NZ) if bin(z).count("1") % 2 == side] for side in range(2)]
+ORDER = (6, 1, 7, 0, 3, 4, 2, 5)
+COLUMN = [[planes[k] * NY + y for k in ORDER] for planes in SIDES for y in range(NY)]
 ALONG_X = [[0, 2, 4, 6], [1, 3, 5, 7]]
 CORES = [[0, 1], [2, 3], [4, 5], [6, 7]]
 BF = jnp.bfloat16
@@ -55,7 +53,8 @@
 
 
 def plane_turn():
-    return lax.axis_index("seq") // (NY * NZ // 2)
+    pair = lax.axis_index("seq") // (2 * NY)
+    return (pair + pair // 2 + pair // 4) % 2
 
 
 def live_row(lists, counts, rows):

time: 103 us -> 97.8 us (0.950)
  waiting for transfers between devices: 6.01 us -> 0.01 us
    all_to_all x1, waiting for transfers between devices: 6.01 us -> 0.01 us  [exchange(): lax.all_to_all(values, axis, 0, 0, axis_index_groups=groups, tiled=True)]
  transfers between devices with their start and end apart: 1 -> 1, of which waited for: 1 -> 0; matrix products, arithmetic and copies ran while one was open for 0% -> 0% of each run, Pallas kernels for 0% -> 0%
where the time goes in v9:
time: 97.8 us; the launch traced here: 97.4 us
  blocking collectives  76.2 us (78%)
  starting transfers between devices  11.1 us (11%)
  Pallas kernels  8.44 us (9%)
  local copies, waits for them, and re-layouts  1.6 us (2%)
    all_to_all x5, blocking collectives, exchange(): lax.all_to_all(values, axis, 0, 0, axis_index_groups=groups, tiled=True)  58.7 us
    all_to_all x1, starting transfers between devices, exchange(): lax.all_to_all(values, axis, 0, 0, axis_index_groups=groups, tiled=True)  11.1 us
    all_gather x1, blocking collectives, local(): queries = lax.all_gather(queries, 'seq', axis_index_groups=ALONG_Y)  9.94 us
    pallas_call x10, Pallas kernels, call(): pl.pallas_call(kernel, out_shape=out, in_specs=[one] * len(args), out_spe...  8.44 us
    all_gather x1, blocking collectives, local(): lax.all_gather(pair, 'seq', axis_index_groups=PAIR)  3.84 us
    all_gather x1, blocking collectives, local(): parts = lax.all_gather(part_sum, 'mp', axis_index_groups=CORES)  3.69 us
  transfers between devices with their start and end apart: 1, of which 0 were waited for; matrix products, arithmetic and copies ran while one was open for 0% of the time, Pallas kernels for 0%

profile of v9, /device:TPU:1, one launch (start us, length us, event | category | flops | bytes accessed | tf_op | source)
XLA Modules:
  0.0 97.4 jit_solution(11800614739456185900)
XLA Ops:
  0.0 0.0 copy-start.7
  0.0 0.7 copy-done.7
  0.7 0.0 copy-start.10
  0.7 0.9 copy-done.10
  1.6 0.0 copy-start
  1.6 0.0 copy-start.1
  1.6 0.3 shard_map.100.own
  1.8 15.0 %all_to_all.30.gathered = bf16[8,80,128]{2,1,0:T(8,128)(2,1)S(1)} all-to-all(bf16[8,80,128]{2,1,0:T(8,128)(2,1)S(1)} %shard_map.100.own), channel_id=1, replica_groups=mesh['seq'=64,'mp'=8] {'mp'}, dimensions={0} | all-to-all | bytes 327680 | tf_op jit(solution)/shard_map/all_to_all | solution.py:305
  16.8 0.0 copy-done
  16.8 0.0 copy-done.1
  16.8 0.0 copy-start.4
  16.8 1.4 %shard_map.101 = bf16[8,80,128]{2,1,0:T(8,128)(2,1)S(1)} custom-call(bf16[8,80,128]{2,1,0:T(8,128)(2,1)S(1)} %all_to_all.30.gathered, bf16[1280,640]{1,0:T(8,128)(2,1)S(1)} %copy-done, bf16[640,1280]{1,0:T(8,128)(2,1)S(1)} %copy-done.1), custom_call_target="tpu_custom_call" | custom-call | tf_op jit(solution)/shard_map/pallas_call | solution.py:289
  18.2 0.0 copy-start.2
  18.2 0.0 copy-start.3
  18.2 0.0 copy-start.6
  18.2 0.0 copy-start.8
  18.2 0.0 copy-start.9
  18.3 9.0 %all_to_all.31.terms = bf16[8,80,128]{2,1,0:T(8,128)(2,1)S(1)} all-to-all(bf16[8,80,128]{2,1,0:T(8,128)(2,1)S(1)} %shard_map.101), channel_id=1, replica_groups=mesh['seq'=64,'mp'=8] {'mp'}, dimensions={0} | all-to-all | bytes 327680 | tf_op jit(solution)/shard_map/all_to_all | solution.py:305
  27.3 0.0 copy-done.4
  27.3 0.2 shard_map.102
  27.5 7.9 %all_to_all.32.parts = bf16[4,64,512]{2,1,0:T(8,128)(2,1)S(1)} all-to-all(bf16[4,64,512]{2,1,0:T(8,128)(2,1)S(1)} %shard_map.102), channel_id=1, replica_groups={{0,2,4,6},{1,3,5,7},{8,10,12,14},{9,11,13,15},{16,18,20,22},{17,19,21,2..., dimensions={0} | all-to-all | bytes 524288 | tf_op jit(solution)/shard_map/all_to_all | solution.py:305
  35.4 0.0 copy-start.5
  35.5 3.7 %all-gather = f32[128,512]{1,0:T(8,128)S(1)} all-gather(f32[64,512]{1,0:T(8,128)S(1)} %shard_map.103), channel_id=2, replica_groups={{0,1},{2,3},{4,5},{6,7},{8,9},{10,11},{12,13},{14,15},{16,17},{18,19},{..., dimensions={0}, use_global_device_ids=true | all-gather | bytes 393216 | tf_op jit(solution)/shard_map/all_gather | solution.py:339
  39.2 0.0 copy-done.2
  39.2 0.0 copy-done.3
  39.2 0.0 copy-done.6
  39.2 0.0 copy-done.8
  39.2 0.0 copy-done.9
  39.2 0.7 shard_map.104
  39.9 3.8 %all-gather.1 = bf16[4,136,128]{2,1,0:T(8,128)(2,1)S(1)} all-gather(bf16[2,136,128]{2,1,0:T(8,128)(2,1)S(1)} %get-tuple-element.11), channel_id=3, replica_groups={{0,32},{8,40},{16,48},{24,56},{64,96},{72,104},{80,112},{88,120},{128,1..., dimensions={0}, use_global_device_ids=true | all-gather | bytes 208896 | tf_op jit(solution)/shard_map/all_gather | solution.py:348
  43.7 0.7 shard_map.105
  44.5 11.1 %all-to-all-start.3 = ((bf16[8,136,128]{2,1,0:T(8,128)(2,1)}), bf16[8,136,128]{2,1,0:T(8,128)(2,1)S(1)}, u32[]{:S(2)}, u32[]{:S(2)}) async-start(bf16[8,136,128]{2,1,0:T(8,128)(2,1)} %get-tuple-element.15), calls=%async_computation.3 | async-start | bytes 557056 | tf_op jit(solution)/shard_map/all_to_all | solution.py:305
  55.6 0.4 shard_map.106.dec_own
  56.0 9.9 %all-gather.2 = bf16[512,128]{1,0:T(8,128)(2,1)S(1)} all-gather(bf16[128,128]{1,0:T(8,128)(2,1)S(1)} %get-tuple-element.12), channel_id=4, replica_groups={{0,8,16,24},{32,40,48,56},{64,72,80,88},{96,104,112,120},{128,136,144,1..., dimensions={0}, use_global_device_ids=true | all-gather | bytes 163840 | tf_op jit(solution)/shard_map/all_gather | solution.py:351
  65.9 0.0 all-to-all-done.3.column
  65.9 3.6 %shard_map.107 = bf16[8,80,128]{2,1,0:T(8,128)(2,1)S(1)} custom-call(bf16[4,128,128]{2,1,0:T(8,128)(2,1)S(1)} %bitcast.8, bf16[8,136,128]{2,1,0:T(8,128)(2,1)S(1)} %all-to-all-done.3.column), custom_call_target="tpu_custom_call" | custom-call | tf_op jit(solution)/shard_map/pallas_call | solution.py:289
  69.5 14.4 %all_to_all.33.message = bf16[8,80,128]{2,1,0:T(8,128)(2,1)S(1)} all-to-all(bf16[8,80,128]{2,1,0:T(8,128)(2,1)S(1)} %shard_map.107), channel_id=1, replica_groups={{0,32,8,40,16,48,24,56},{64,96,72,104,80,112,88,120},{128,160,136,168,1..., dimensions={0} | all-to-all | bytes 327680 | tf_op jit(solution)/shard_map/all_to_all | solution.py:305
  84.0 0.0 copy-done.5
  84.0 0.3 shard_map.108
  84.3 12.4 %all_to_all.34.terms = bf16[8,64,256]{2,1,0:T(8,128)(2,1)S(1)} all-to-all(bf16[8,64,256]{2,1,0:T(8,128)(2,1)S(1)} %shard_map.108), channel_id=1, replica_groups=mesh['seq'=64,'mp'=8] {'mp'}, dimensions={0} | all-to-all | bytes 524288 | tf_op jit(solution)/shard_map/all_to_all | solution.py:305
  96.6 0.8 shard_map.109
  (1 shorter events, 0.0 us)
Async XLA Ops:
  0.0 0.7 copy-start.7
  0.7 0.9 copy-start.10
  1.6 15.3 %copy-start = (bf16[1280,640]{1,0:T(8,128)(2,1)S(1)}, bf16[1280,640]{1,0:T(8,128)(2,1)}, u32[]{:S(2)}) copy-start(bf16[1280,640]{1,0:T(8,128)(2,1)} %w_in.1) | copy-start | bytes 4915204
  1.6 15.3 %copy-start.1 = (bf16[640,1280]{1,0:T(8,128)(2,1)S(1)}, bf16[640,1280]{1,0:T(8,128)(2,1)}, u32[]{:S(2)}) copy-start(bf16[640,1280]{1,0:T(8,128)(2,1)} %w_out.1) | copy-start | bytes 4915204
  16.8 10.4 %copy-start.4 = (bf16[160,512]{1,0:T(8,128)(2,1)S(1)}, bf16[160,512]{1,0:T(8,128)(2,1)}, u32[]{:S(2)}) copy-start(bf16[160,512]{1,0:T(8,128)(2,1)} %w_embed.1) | copy-start | bytes 491524
  18.2 21.0 %copy-start.2 = (bf16[64,512]{1,0:T(8,128)(2,1)S(1)}, bf16[64,512]{1,0:T(8,128)(2,1)}, u32[]{:S(2)}) copy-start(bf16[64,512]{1,0:T(8,128)(2,1)} %positions.3) | copy-start | bytes 196612
  18.2 21.0 %copy-start.3 = (bf16[512,3,64]{0,2,1:T(8,128)(2,1)S(1)}, bf16[512,3,64]{0,2,1:T(8,128)(2,1)}, u32[]{:S(2)}) copy-start(bf16[512,3,64]{0,2,1:T(8,128)(2,1)} %param.18) | copy-start | bytes 589828
  18.2 21.0 %copy-start.6 = (bf16[512]{0:T(512)(128)(2,1)S(1)}, bf16[512]{0:T(512)(128)(2,1)}, u32[]{:S(2)}) copy-start(bf16[512]{0:T(512)(128)(2,1)} %mask_token.3) | copy-start | bytes 3076
  18.2 20.9 %copy-start.8 = (s32[1,64,1]{1,2,0:T(1,128)S(1)}, s32[1,64,1]{1,2,0:T(1,128)}, u32[]{:S(2)}) copy-start(s32[1,64,1]{1,2,0:T(1,128)} %param.11) | copy-start | bytes 772
  18.2 20.9 %copy-start.9 = (s32[1,64]{1,0:T(1,128)S(1)}, s32[1,64]{1,0:T(1,128)}, u32[]{:S(2)}) copy-start(s32[1,64]{1,0:T(1,128)} %counts.3) | copy-start | bytes 772
  35.4 48.5 %copy-start.5 = (bf16[64,512]{1,0:T(8,128)(2,1)S(1)}, bf16[64,512]{1,0:T(8,128)(2,1)}, u32[]{:S(2)}) copy-start(bf16[64,512]{1,0:T(8,128)(2,1)} %w_attn_out.1) | copy-start | bytes 196612
  44.5 21.4 %all-to-all-start.3 = ((bf16[8,136,128]{2,1,0:T(8,128)(2,1)}), bf16[8,136,128]{2,1,0:T(8,128)(2,1)S(1)}, u32[]{:S(2)}, u32[]{:S(2)}) async-start(bf16[8,136,128]{2,1,0:T(8,128)(2,1)} %get-tuple-element.15), calls=%async_computation.3 | async-start | bytes 557056 | tf_op jit(solution)/shard_map/all_to_all | solution.py:305

commit v10 on v9

--- a/solution.py
+++ b/solution.py
@@ -15,7 +15,7 @@
 PAIR = [[(2 * k + p) * NY + y for p in range(2)] for k in range(NZ // 2) for y in range(NY)]
 ALONG_Y = [[z * NY + y for y in range(NY)] for z in range(NZ)]
 SIDES = [[z for z in range(NZ) if bin(z).count("1") % 2 == side] for side in range(2)]
-ORDER = (6, 1, 7, 0, 3, 4, 2, 5)
+ORDER = (6, 2, 7, 0, 3, 4, 1, 5)
 COLUMN = [[planes[k] * NY + y for k in ORDER] for planes in SIDES for y in range(NY)]
 ALONG_X = [[0, 2, 4, 6], [1, 3, 5, 7]]
 CORES = [[0, 1], [2, 3], [4, 5], [6, 7]]

time: 97.8 us -> 96.7 us (0.989)
  blocking collectives: 76.2 us -> 75.1 us
    all_to_all x5, blocking collectives: 58.7 us -> 57.6 us  [exchange(): lax.all_to_all(values, axis, 0, 0, axis_index_groups=groups, tiled=True)]
where the time goes in v10:
time: 96.7 us; the launch traced here: 96.3 us
  blocking collectives  75.1 us (78%)
  starting transfers between devices  11.1 us (11%)
  Pallas kernels  8.44 us (9%)
  local copies, waits for them, and re-layouts  1.6 us (2%)
    all_to_all x5, blocking collectives, exchange(): lax.all_to_all(values, axis, 0, 0, axis_index_groups=groups, tiled=True)  57.6 us
    all_to_all x1, starting transfers between devices, exchange(): lax.all_to_all(values, axis, 0, 0, axis_index_groups=groups, tiled=True)  11.1 us
    all_gather x1, blocking collectives, local(): queries = lax.all_gather(queries, 'seq', axis_index_groups=ALONG_Y)  9.94 us
    pallas_call x10, Pallas kernels, call(): pl.pallas_call(kernel, out_shape=out, in_specs=[one] * len(args), out_spe...  8.44 us
    all_gather x1, blocking collectives, local(): lax.all_gather(pair, 'seq', axis_index_groups=PAIR)  3.84 us
    all_gather x1, blocking collectives, local(): parts = lax.all_gather(part_sum, 'mp', axis_index_groups=CORES)  3.69 us
  transfers between devices with their start and end apart: 1, of which 0 were waited for; matrix products, arithmetic and copies ran while one was open for 0% of the time, Pallas kernels for 0%

profile of v10, /device:TPU:1, one launch (start us, length us, event | category | flops | bytes accessed | tf_op | source)
XLA Modules:
  0.0 96.3 jit_solution(8902455474569873897)
XLA Ops:
  0.0 0.0 copy-start.7
  0.0 0.7 copy-done.7
  0.7 0.0 copy-start.10
  0.7 0.9 copy-done.10
  1.6 0.0 copy-start
  1.6 0.0 copy-start.1
  1.6 0.3 shard_map.100.own
  1.8 15.0 %all_to_all.30.gathered = bf16[8,80,128]{2,1,0:T(8,128)(2,1)S(1)} all-to-all(bf16[8,80,128]{2,1,0:T(8,128)(2,1)S(1)} %shard_map.100.own), channel_id=1, replica_groups=mesh['seq'=64,'mp'=8] {'mp'}, dimensions={0} | all-to-all | bytes 327680 | tf_op jit(solution)/shard_map/all_to_all | solution.py:305
  16.8 0.0 copy-done
  16.8 0.0 copy-done.1
  16.8 0.0 copy-start.4
  16.8 1.4 %shard_map.101 = bf16[8,80,128]{2,1,0:T(8,128)(2,1)S(1)} custom-call(bf16[8,80,128]{2,1,0:T(8,128)(2,1)S(1)} %all_to_all.30.gathered, bf16[1280,640]{1,0:T(8,128)(2,1)S(1)} %copy-done, bf16[640,1280]{1,0:T(8,128)(2,1)S(1)} %copy-done.1), custom_call_target="tpu_custom_call" | custom-call | tf_op jit(solution)/shard_map/pallas_call | solution.py:289
  18.2 0.0 copy-start.2
  18.2 0.0 copy-start.3
  18.2 0.0 copy-start.6
  18.2 0.0 copy-start.8
  18.2 0.0 copy-start.9
  18.3 9.0 %all_to_all.31.terms = bf16[8,80,128]{2,1,0:T(8,128)(2,1)S(1)} all-to-all(bf16[8,80,128]{2,1,0:T(8,128)(2,1)S(1)} %shard_map.101), channel_id=1, replica_groups=mesh['seq'=64,'mp'=8] {'mp'}, dimensions={0} | all-to-all | bytes 327680 | tf_op jit(solution)/shard_map/all_to_all | solution.py:305
  27.3 0.0 copy-done.4
  27.3 0.2 shard_map.102
  27.5 7.9 %all_to_all.32.parts = bf16[4,64,512]{2,1,0:T(8,128)(2,1)S(1)} all-to-all(bf16[4,64,512]{2,1,0:T(8,128)(2,1)S(1)} %shard_map.102), channel_id=1, replica_groups={{0,2,4,6},{1,3,5,7},{8,10,12,14},{9,11,13,15},{16,18,20,22},{17,19,21,2..., dimensions={0} | all-to-all | bytes 524288 | tf_op jit(solution)/shard_map/all_to_all | solution.py:305
  35.4 0.0 copy-start.5
  35.5 3.7 %all-gather = f32[128,512]{1,0:T(8,128)S(1)} all-gather(f32[64,512]{1,0:T(8,128)S(1)} %shard_map.103), channel_id=2, replica_groups={{0,1},{2,3},{4,5},{6,7},{8,9},{10,11},{12,13},{14,15},{16,17},{18,19},{..., dimensions={0}, use_global_device_ids=true | all-gather | bytes 393216 | tf_op jit(solution)/shard_map/all_gather | solution.py:339
  39.2 0.0 copy-done.2
  39.2 0.0 copy-done.3
  39.2 0.0 copy-done.6
  39.2 0.0 copy-done.8
  39.2 0.0 copy-done.9
  39.2 0.7 shard_map.104
  39.9 3.8 %all-gather.1 = bf16[4,136,128]{2,1,0:T(8,128)(2,1)S(1)} all-gather(bf16[2,136,128]{2,1,0:T(8,128)(2,1)S(1)} %get-tuple-element.11), channel_id=3, replica_groups={{0,32},{8,40},{16,48},{24,56},{64,96},{72,104},{80,112},{88,120},{128,1..., dimensions={0}, use_global_device_ids=true | all-gather | bytes 208896 | tf_op jit(solution)/shard_map/all_gather | solution.py:348
  43.7 0.7 shard_map.105
  44.5 11.1 %all-to-all-start.3 = ((bf16[8,136,128]{2,1,0:T(8,128)(2,1)}), bf16[8,136,128]{2,1,0:T(8,128)(2,1)S(1)}, u32[]{:S(2)}, u32[]{:S(2)}) async-start(bf16[8,136,128]{2,1,0:T(8,128)(2,1)} %get-tuple-element.15), calls=%async_computation.3 | async-start | bytes 557056 | tf_op jit(solution)/shard_map/all_to_all | solution.py:305
  55.6 0.4 shard_map.106.dec_own
  56.0 9.9 %all-gather.2 = bf16[512,128]{1,0:T(8,128)(2,1)S(1)} all-gather(bf16[128,128]{1,0:T(8,128)(2,1)S(1)} %get-tuple-element.12), channel_id=4, replica_groups={{0,8,16,24},{32,40,48,56},{64,72,80,88},{96,104,112,120},{128,136,144,1..., dimensions={0}, use_global_device_ids=true | all-gather | bytes 163840 | tf_op jit(solution)/shard_map/all_gather | solution.py:351
  65.9 0.0 all-to-all-done.3.column
  65.9 3.6 %shard_map.107 = bf16[8,80,128]{2,1,0:T(8,128)(2,1)S(1)} custom-call(bf16[4,128,128]{2,1,0:T(8,128)(2,1)S(1)} %bitcast.8, bf16[8,136,128]{2,1,0:T(8,128)(2,1)S(1)} %all-to-all-done.3.column), custom_call_target="tpu_custom_call" | custom-call | tf_op jit(solution)/shard_map/pallas_call | solution.py:289
  69.5 14.8 %all_to_all.33.message = bf16[8,80,128]{2,1,0:T(8,128)(2,1)S(1)} all-to-all(bf16[8,80,128]{2,1,0:T(8,128)(2,1)S(1)} %shard_map.107), channel_id=1, replica_groups={{0,32,8,40,16,48,24,56},{64,96,72,104,80,112,88,120},{128,160,136,168,1..., dimensions={0} | all-to-all | bytes 327680 | tf_op jit(solution)/shard_map/all_to_all | solution.py:305
  84.4 0.0 copy-done.5
  84.4 0.3 shard_map.108
  84.7 10.8 %all_to_all.34.terms = bf16[8,64,256]{2,1,0:T(8,128)(2,1)S(1)} all-to-all(bf16[8,64,256]{2,1,0:T(8,128)(2,1)S(1)} %shard_map.108), channel_id=1, replica_groups=mesh['seq'=64,'mp'=8] {'mp'}, dimensions={0} | all-to-all | bytes 524288 | tf_op jit(solution)/shard_map/all_to_all | solution.py:305
  95.5 0.8 shard_map.109
  (1 shorter events, 0.0 us)
Async XLA Ops:
  0.0 0.7 copy-start.7
  0.7 0.9 copy-start.10
  1.6 15.3 %copy-start = (bf16[1280,640]{1,0:T(8,128)(2,1)S(1)}, bf16[1280,640]{1,0:T(8,128)(2,1)}, u32[]{:S(2)}) copy-start(bf16[1280,640]{1,0:T(8,128)(2,1)} %w_in.1) | copy-start | bytes 4915204
  1.6 15.3 %copy-start.1 = (bf16[640,1280]{1,0:T(8,128)(2,1)S(1)}, bf16[640,1280]{1,0:T(8,128)(2,1)}, u32[]{:S(2)}) copy-start(bf16[640,1280]{1,0:T(8,128)(2,1)} %w_out.1) | copy-start | bytes 4915204
  16.8 10.4 %copy-start.4 = (bf16[160,512]{1,0:T(8,128)(2,1)S(1)}, bf16[160,512]{1,0:T(8,128)(2,1)}, u32[]{:S(2)}) copy-start(bf16[160,512]{1,0:T(8,128)(2,1)} %w_embed.1) | copy-start | bytes 491524
  18.2 21.0 %copy-start.2 = (bf16[64,512]{1,0:T(8,128)(2,1)S(1)}, bf16[64,512]{1,0:T(8,128)(2,1)}, u32[]{:S(2)}) copy-start(bf16[64,512]{1,0:T(8,128)(2,1)} %positions.3) | copy-start | bytes 196612
  18.2 21.0 %copy-start.3 = (bf16[512,3,64]{0,2,1:T(8,128)(2,1)S(1)}, bf16[512,3,64]{0,2,1:T(8,128)(2,1)}, u32[]{:S(2)}) copy-start(bf16[512,3,64]{0,2,1:T(8,128)(2,1)} %param.18) | copy-start | bytes 589828
  18.2 21.0 %copy-start.6 = (bf16[512]{0:T(512)(128)(2,1)S(1)}, bf16[512]{0:T(512)(128)(2,1)}, u32[]{:S(2)}) copy-start(bf16[512]{0:T(512)(128)(2,1)} %mask_token.3) | copy-start | bytes 3076
  18.2 20.9 %copy-start.8 = (s32[1,64,1]{1,2,0:T(1,128)S(1)}, s32[1,64,1]{1,2,0:T(1,128)}, u32[]{:S(2)}) copy-start(s32[1,64,1]{1,2,0:T(1,128)} %param.11) | copy-start | bytes 772
  18.2 20.9 %copy-start.9 = (s32[1,64]{1,0:T(1,128)S(1)}, s32[1,64]{1,0:T(1,128)}, u32[]{:S(2)}) copy-start(s32[1,64]{1,0:T(1,128)} %counts.3) | copy-start | bytes 772
  35.4 49.0 %copy-start.5 = (bf16[64,512]{1,0:T(8,128)(2,1)S(1)}, bf16[64,512]{1,0:T(8,128)(2,1)}, u32[]{:S(2)}) copy-start(bf16[64,512]{1,0:T(8,128)(2,1)} %w_attn_out.1) | copy-start | bytes 196612
  44.5 21.4 %all-to-all-start.3 = ((bf16[8,136,128]{2,1,0:T(8,128)(2,1)}), bf16[8,136,128]{2,1,0:T(8,128)(2,1)S(1)}, u32[]{:S(2)}, u32[]{:S(2)}) async-start(bf16[8,136,128]{2,1,0:T(8,128)(2,1)} %get-tuple-element.15), calls=%async_computation.3 | async-start | bytes 557056 | tf_op jit(solution)/shard_map/all_to_all | solution.py:305

commit v11 on v10

--- a/solution.py
+++ b/solution.py
@@ -11,7 +11,7 @@
 HDIM = 32
 NY = 4
 NZ = 16
-GROUP = [[(2 * k + p) * NY + y for y in range(NY) for p in range(2)] for k in range(NZ // 2)]
+GROUP = [[(2 * k + p) * NY + y for p in range(2) for y in range(NY)] for k in range(NZ // 2)]
 PAIR = [[(2 * k + p) * NY + y for p in range(2)] for k in range(NZ // 2) for y in range(NY)]
 ALONG_Y = [[z * NY + y for y in range(NY)] for z in range(NZ)]
 SIDES = [[z for z in range(NZ) if bin(z).count("1") % 2 == side] for side in range(2)]
@@ -231,8 +231,9 @@
         half, side = v // 2, slice(64 * (v % 2), 64 * (v % 2) + 64)
         for b in range(blocks):
             cols = slice(b * tubs, (b + 1) * tubs)
-            msg_scr[b, HDIM * half : HDIM * half + HDIM, side] = summed[:, cols]
-            msg_scr[b, 64 + 8 * half : 72 + 8 * half, side] = stats[:, cols]
+            dest = b % 2 * NY + b // 2
+            msg_scr[dest, HDIM * half : HDIM * half + HDIM, side] = summed[:, cols]
+            msg_scr[dest, 64 + 8 * half : 72 + 8 * half, side] = stats[:, cols]
 
     scores, waiting = score(0), None
     for v in range(vols):
@@ -254,14 +255,14 @@
         sides = []
         for u in range(2):
             stats = [
-                message[2 * k + plane, 64:, :].astype(F32)[8 * u : 8 * u + 8] for k in range(NY)
+                message[NY * plane + k, 64:, :].astype(F32)[8 * u : 8 * u + 8] for k in range(NY)
             ]
             tops = [s[0:1] + s[1:2] + s[2:3] for s in stats]
             best = functools.reduce(jnp.maximum, tops)
             fades = [jnp.exp2(t - best) for t in tops]
             total = sum(f * (s[3:4] + s[4:5]) for f, s in zip(fades, stats))
             value = sum(
-                f * message[2 * k + plane, HDIM * u : HDIM * u + HDIM, :].astype(F32)
+                f * message[NY * plane + k, HDIM * u : HDIM * u + HDIM, :].astype(F32)
                 for k, f in enumerate(fades)
             )
             sides.append(value / total)

time: 96.7 us -> 96.6 us (level)
  no operation moved by 1% of the time
where the time goes in v11:
time: 96.6 us; the launch traced here: 96.2 us
  blocking collectives  75 us (78%)
  starting transfers between devices  11.1 us (11%)
  Pallas kernels  8.44 us (9%)
  local copies, waits for them, and re-layouts  1.6 us (2%)
    all_to_all x5, blocking collectives, exchange(): lax.all_to_all(values, axis, 0, 0, axis_index_groups=groups, tiled=True)  57.5 us
    all_to_all x1, starting transfers between devices, exchange(): lax.all_to_all(values, axis, 0, 0, axis_index_groups=groups, tiled=True)  11.1 us
    all_gather x1, blocking collectives, local(): queries = lax.all_gather(queries, 'seq', axis_index_groups=ALONG_Y)  9.94 us
    pallas_call x10, Pallas kernels, call(): pl.pallas_call(kernel, out_shape=out, in_specs=[one] * len(args), out_spe...  8.44 us
    all_gather x1, blocking collectives, local(): lax.all_gather(pair, 'seq', axis_index_groups=PAIR)  3.84 us
    all_gather x1, blocking collectives, local(): parts = lax.all_gather(part_sum, 'mp', axis_index_groups=CORES)  3.69 us
  transfers between devices with their start and end apart: 1, of which 0 were waited for; matrix products, arithmetic and copies ran while one was open for 0% of the time, Pallas kernels for 0%

profile of v11, /device:TPU:1, one launch (start us, length us, event | category | flops | bytes accessed | tf_op | source)
XLA Modules:
  0.0 96.2 jit_solution(15625607765459633875)
XLA Ops:
  0.0 0.0 copy-start.7
  0.0 0.7 copy-done.7
  0.7 0.0 copy-start.10
  0.7 0.9 copy-done.10
  1.6 0.0 copy-start
  1.6 0.0 copy-start.1
  1.6 0.3 shard_map.100.own
  1.8 15.0 %all_to_all.30.gathered = bf16[8,80,128]{2,1,0:T(8,128)(2,1)S(1)} all-to-all(bf16[8,80,128]{2,1,0:T(8,128)(2,1)S(1)} %shard_map.100.own), channel_id=1, replica_groups=mesh['seq'=64,'mp'=8] {'mp'}, dimensions={0} | all-to-all | bytes 327680 | tf_op jit(solution)/shard_map/all_to_all | solution.py:306
  16.8 0.0 copy-done
  16.8 0.0 copy-done.1
  16.8 0.0 copy-start.4
  16.8 1.4 %shard_map.101 = bf16[8,80,128]{2,1,0:T(8,128)(2,1)S(1)} custom-call(bf16[8,80,128]{2,1,0:T(8,128)(2,1)S(1)} %all_to_all.30.gathered, bf16[1280,640]{1,0:T(8,128)(2,1)S(1)} %copy-done, bf16[640,1280]{1,0:T(8,128)(2,1)S(1)} %copy-done.1), custom_call_target="tpu_custom_call" | custom-call | tf_op jit(solution)/shard_map/pallas_call | solution.py:290
  18.2 0.0 copy-start.2
  18.2 0.0 copy-start.3
  18.2 0.0 copy-start.6
  18.2 0.0 copy-start.8
  18.2 0.0 copy-start.9
  18.3 9.0 %all_to_all.31.terms = bf16[8,80,128]{2,1,0:T(8,128)(2,1)S(1)} all-to-all(bf16[8,80,128]{2,1,0:T(8,128)(2,1)S(1)} %shard_map.101), channel_id=1, replica_groups=mesh['seq'=64,'mp'=8] {'mp'}, dimensions={0} | all-to-all | bytes 327680 | tf_op jit(solution)/shard_map/all_to_all | solution.py:306
  27.3 0.0 copy-done.4
  27.3 0.2 shard_map.102
  27.5 7.9 %all_to_all.32.parts = bf16[4,64,512]{2,1,0:T(8,128)(2,1)S(1)} all-to-all(bf16[4,64,512]{2,1,0:T(8,128)(2,1)S(1)} %shard_map.102), channel_id=1, replica_groups={{0,2,4,6},{1,3,5,7},{8,10,12,14},{9,11,13,15},{16,18,20,22},{17,19,21,2..., dimensions={0} | all-to-all | bytes 524288 | tf_op jit(solution)/shard_map/all_to_all | solution.py:306
  35.4 0.0 copy-start.5
  35.5 3.7 %all-gather = f32[128,512]{1,0:T(8,128)S(1)} all-gather(f32[64,512]{1,0:T(8,128)S(1)} %shard_map.103), channel_id=2, replica_groups={{0,1},{2,3},{4,5},{6,7},{8,9},{10,11},{12,13},{14,15},{16,17},{18,19},{..., dimensions={0}, use_global_device_ids=true | all-gather | bytes 393216 | tf_op jit(solution)/shard_map/all_gather | solution.py:340
  39.2 0.0 copy-done.2
  39.2 0.0 copy-done.3
  39.2 0.0 copy-done.6
  39.2 0.0 copy-done.8
  39.2 0.0 copy-done.9
  39.2 0.7 shard_map.104
  39.9 3.8 %all-gather.1 = bf16[4,136,128]{2,1,0:T(8,128)(2,1)S(1)} all-gather(bf16[2,136,128]{2,1,0:T(8,128)(2,1)S(1)} %get-tuple-element.11), channel_id=3, replica_groups={{0,32},{8,40},{16,48},{24,56},{64,96},{72,104},{80,112},{88,120},{128,1..., dimensions={0}, use_global_device_ids=true | all-gather | bytes 208896 | tf_op jit(solution)/shard_map/all_gather | solution.py:349
  43.7 0.7 shard_map.105
  44.5 11.1 %all-to-all-start.3 = ((bf16[8,136,128]{2,1,0:T(8,128)(2,1)}), bf16[8,136,128]{2,1,0:T(8,128)(2,1)S(1)}, u32[]{:S(2)}, u32[]{:S(2)}) async-start(bf16[8,136,128]{2,1,0:T(8,128)(2,1)} %get-tuple-element.15), calls=%async_computation.3 | async-start | bytes 557056 | tf_op jit(solution)/shard_map/all_to_all | solution.py:306
  55.6 0.4 shard_map.106.dec_own
  56.0 9.9 %all-gather.2 = bf16[512,128]{1,0:T(8,128)(2,1)S(1)} all-gather(bf16[128,128]{1,0:T(8,128)(2,1)S(1)} %get-tuple-element.12), channel_id=4, replica_groups={{0,8,16,24},{32,40,48,56},{64,72,80,88},{96,104,112,120},{128,136,144,1..., dimensions={0}, use_global_device_ids=true | all-gather | bytes 163840 | tf_op jit(solution)/shard_map/all_gather | solution.py:352
  65.9 0.0 all-to-all-done.3.column
  65.9 3.6 %shard_map.107 = bf16[8,80,128]{2,1,0:T(8,128)(2,1)S(1)} custom-call(bf16[4,128,128]{2,1,0:T(8,128)(2,1)S(1)} %bitcast.8, bf16[8,136,128]{2,1,0:T(8,128)(2,1)S(1)} %all-to-all-done.3.column), custom_call_target="tpu_custom_call" | custom-call | tf_op jit(solution)/shard_map/pallas_call | solution.py:290
  69.5 14.8 %all_to_all.33.message = bf16[8,80,128]{2,1,0:T(8,128)(2,1)S(1)} all-to-all(bf16[8,80,128]{2,1,0:T(8,128)(2,1)S(1)} %shard_map.107), channel_id=1, replica_groups={{0,8,16,24,32,40,48,56},{64,72,80,88,96,104,112,120},{128,136,144,152,1..., dimensions={0} | all-to-all | bytes 327680 | tf_op jit(solution)/shard_map/all_to_all | solution.py:306
  84.3 0.0 copy-done.5
  84.3 0.3 shard_map.108
  84.6 10.8 %all_to_all.34.terms = bf16[8,64,256]{2,1,0:T(8,128)(2,1)S(1)} all-to-all(bf16[8,64,256]{2,1,0:T(8,128)(2,1)S(1)} %shard_map.108), channel_id=1, replica_groups=mesh['seq'=64,'mp'=8] {'mp'}, dimensions={0} | all-to-all | bytes 524288 | tf_op jit(solution)/shard_map/all_to_all | solution.py:306
  95.4 0.8 shard_map.109
  (1 shorter events, 0.0 us)
Async XLA Ops:
  0.0 0.7 copy-start.7
  0.7 0.9 copy-start.10
  1.6 15.3 %copy-start = (bf16[1280,640]{1,0:T(8,128)(2,1)S(1)}, bf16[1280,640]{1,0:T(8,128)(2,1)}, u32[]{:S(2)}) copy-start(bf16[1280,640]{1,0:T(8,128)(2,1)} %w_in.1) | copy-start | bytes 4915204
  1.6 15.3 %copy-start.1 = (bf16[640,1280]{1,0:T(8,128)(2,1)S(1)}, bf16[640,1280]{1,0:T(8,128)(2,1)}, u32[]{:S(2)}) copy-start(bf16[640,1280]{1,0:T(8,128)(2,1)} %w_out.1) | copy-start | bytes 4915204
  16.8 10.4 %copy-start.4 = (bf16[160,512]{1,0:T(8,128)(2,1)S(1)}, bf16[160,512]{1,0:T(8,128)(2,1)}, u32[]{:S(2)}) copy-start(bf16[160,512]{1,0:T(8,128)(2,1)} %w_embed.1) | copy-start | bytes 491524
  18.2 21.0 %copy-start.2 = (bf16[64,512]{1,0:T(8,128)(2,1)S(1)}, bf16[64,512]{1,0:T(8,128)(2,1)}, u32[]{:S(2)}) copy-start(bf16[64,512]{1,0:T(8,128)(2,1)} %positions.3) | copy-start | bytes 196612
  18.2 21.0 %copy-start.3 = (bf16[512,3,64]{0,2,1:T(8,128)(2,1)S(1)}, bf16[512,3,64]{0,2,1:T(8,128)(2,1)}, u32[]{:S(2)}) copy-start(bf16[512,3,64]{0,2,1:T(8,128)(2,1)} %param.18) | copy-start | bytes 589828
  18.2 21.0 %copy-start.6 = (bf16[512]{0:T(512)(128)(2,1)S(1)}, bf16[512]{0:T(512)(128)(2,1)}, u32[]{:S(2)}) copy-start(bf16[512]{0:T(512)(128)(2,1)} %mask_token.3) | copy-start | bytes 3076
  18.2 20.9 %copy-start.8 = (s32[1,64,1]{1,2,0:T(1,128)S(1)}, s32[1,64,1]{1,2,0:T(1,128)}, u32[]{:S(2)}) copy-start(s32[1,64,1]{1,2,0:T(1,128)} %param.11) | copy-start | bytes 772
  18.2 20.9 %copy-start.9 = (s32[1,64]{1,0:T(1,128)S(1)}, s32[1,64]{1,0:T(1,128)}, u32[]{:S(2)}) copy-start(s32[1,64]{1,0:T(1,128)} %counts.3) | copy-start | bytes 772
  35.4 48.9 %copy-start.5 = (bf16[64,512]{1,0:T(8,128)(2,1)S(1)}, bf16[64,512]{1,0:T(8,128)(2,1)}, u32[]{:S(2)}) copy-start(bf16[64,512]{1,0:T(8,128)(2,1)} %w_attn_out.1) | copy-start | bytes 196612
  44.5 21.4 %all-to-all-start.3 = ((bf16[8,136,128]{2,1,0:T(8,128)(2,1)}), bf16[8,136,128]{2,1,0:T(8,128)(2,1)S(1)}, u32[]{:S(2)}, u32[]{:S(2)}) async-start(bf16[8,136,128]{2,1,0:T(8,128)(2,1)} %get-tuple-element.15), calls=%async_computation.3 | async-start | bytes 557056 | tf_op jit(solution)/shard_map/all_to_all | solution.py:306
